TPU v7x, 1024 devices: a whole 4x4x32 slice. The times are simulated.
1024 devices in a mesh: stream: 32 (over x, y, core), cross: 32 (over z).
Axes of the slice: x: 4, y: 4, z: 32, core: 2. Of those that a mesh axis runs over, the one named last changes fastest.
Arguments:
- sources: float32 [2, 32, 32, 8, 8, 128], P(None, 'stream', 'cross'), may hold values from -6 to 6
Outputs:
- correction: float32 [2, 32, 32, 8, 8, 128], P(None, 'stream', 'cross')
All inputs are finite; a program needn't handle non-finite values.
Results may differ from a plain program's by a relative error of at most 0.00011.
Values sent between devices are 32-bit elements; how exact they have to be, the bound alone decides.
A program may use at most 64 MiB of HBM per device.

v0:
```python
import math

import jax
import jax.numpy as jnp
import numpy as np
from jax import lax
from jax.sharding import PartitionSpec as P

ORDER = 7
MID_ORDER = 3


PRECISE = lax.Precision.HIGHEST


def padded_2(block, sides, width, periodic):
    for axis, dim in sides:
        count = lax.axis_size(axis)
        forward = [(i, i + 1) for i in range(count - 1)]
        if periodic:
            forward.append((count - 1, 0))
        backward = [(target, source) for source, target in forward]
        low = lax.ppermute(
            lax.slice_in_dim(block, block.shape[dim] - width, None, axis=dim), axis, forward
        )
        high = lax.ppermute(lax.slice_in_dim(block, 0, width, axis=dim), axis, backward)
        block = jnp.concatenate([low, block, high], axis=dim)
    return block


def legendre_pair(degree, points):
    below_poly = np.ones(points.shape)
    top_poly = points.copy()
    for order_step in range(2, degree + 1):
        below_poly, top_poly = (
            top_poly,
            ((2 * order_step - 1) * points * top_poly - (order_step - 1) * below_poly) / order_step,
        )
    return (below_poly, top_poly)


def gll_tables(degree):
    gll_nodes = -np.cos(np.pi * np.arange(degree + 1) / degree)
    for newton_step in range(100):
        below_poly, top_poly = legendre_pair(degree, gll_nodes)
        gll_nodes = gll_nodes - (gll_nodes * top_poly - below_poly) / ((degree + 1) * top_poly)
    at_nodes = legendre_pair(degree, gll_nodes)[1]
    weights = 2.0 / (degree * (degree + 1) * at_nodes**2)
    node_count = degree + 1
    derivative = np.zeros((node_count, node_count))
    for target in range(node_count):
        for source in range(node_count):
            if target != source:
                derivative[target, source] = at_nodes[target] / (
                    at_nodes[source] * (gll_nodes[target] - gll_nodes[source])
                )
    derivative[0, 0] = -degree * (degree + 1) / 4.0
    derivative[degree, degree] = degree * (degree + 1) / 4.0
    stiffness = derivative.T @ (weights[:, None] * derivative)
    return (gll_nodes, weights, stiffness)


def lagrange_matrix(fine_degree, coarse_degree):
    fine_nodes = gll_tables(fine_degree)[0]
    coarse_nodes = gll_tables(coarse_degree)[0]
    lagrange_table = np.ones((fine_degree + 1, coarse_degree + 1))
    for column in range(coarse_degree + 1):
        for other_node in range(coarse_degree + 1):
            if other_node != column:
                lagrange_table[:, column] *= (fine_nodes - coarse_nodes[other_node]) / (
                    coarse_nodes[column] - coarse_nodes[other_node]
                )
    return jnp.asarray(lagrange_table, jnp.float32)


def smoother_bounds(degree):
    stiffness = gll_tables(degree)[2]
    elements = 6
    size_total = elements * degree
    assembled = np.zeros((size_total, size_total))
    for element in range(elements):
        for local_row in range(degree + 1):
            for local_col in range(degree + 1):
                assembled[
                    (element * degree + local_row) % size_total,
                    (element * degree + local_col) % size_total,
                ] += stiffness[local_row, local_col]
    diagonal = np.sqrt(assembled[np.arange(size_total), np.arange(size_total)])
    scaled = assembled / diagonal[:, None] / diagonal[None, :]
    positions = np.arange(size_total)
    vector = np.where(positions % 2 == 0, 1.0, -1.0) * (1.0 + positions / size_total)
    for power_step in range(2000):
        vector = scaled @ vector
        vector = vector / np.sqrt(np.sum(vector * vector))
    upper_bound = float(np.sum(vector * (scaled @ vector)) / np.sum(vector * vector))
    return (0.1 * upper_bound, upper_bound)


def static_tables(degree, span_blocks):
    weights, stiffness = gll_tables(degree)[1:]
    stiff_sum = np.array([stiffness[index, index] for index in range(degree + 1)])
    stiff_sum[0] = stiffness[0, 0] + stiffness[degree, degree]
    stiff_sum[degree] = stiffness[0, 0] + stiffness[degree, degree]
    mass_sum = weights.copy()
    mass_sum[0] = weights[0] + weights[degree]
    mass_sum[degree] = weights[0] + weights[degree]
    shared = np.ones(degree + 1)
    shared[0] = 2.0
    shared[degree] = 2.0
    diagonal = (
        stiff_sum[:, None, None] * mass_sum[None, :, None] * mass_sum[None, None, :]
        + mass_sum[:, None, None] * stiff_sum[None, :, None] * mass_sum[None, None, :]
        + mass_sum[:, None, None] * mass_sum[None, :, None] * stiff_sum[None, None, :]
    )
    inverse_share = 1.0 / (shared[:, None, None] * shared[None, :, None] * shared[None, None, :])
    diag_tile = jnp.asarray(np.tile(1.0 / diagonal, (1, 1, span_blocks)), jnp.float32)
    share_tile = jnp.asarray(np.tile(inverse_share, (1, 1, span_blocks)), jnp.float32)
    return (
        jnp.asarray(stiffness, jnp.float32),
        jnp.asarray(weights, jnp.float32),
        diag_tile,
        share_tile,
    )


def wall_mask(wall_blocks, node_count):
    row_total = wall_blocks * lax.axis_size("cross")
    element_rows = lax.axis_index("cross") * wall_blocks + jnp.arange(wall_blocks, dtype=jnp.int32)
    node_rows = jnp.arange(node_count, dtype=jnp.int32)
    bottom = (element_rows[:, None] == 0) & (node_rows[None, :] == 0)
    top_wall = (element_rows[:, None] == row_total - 1) & (node_rows[None, :] == node_count - 1)
    wall_keep = jnp.where(bottom | top_wall, 0.0, 1.0).astype(jnp.float32)
    return wall_keep[None, None, :, None, :, None]


def build_level(degree, span_blocks, wall_blocks):
    stiffness, weights, diag_tile, share_tile = static_tables(degree, span_blocks)
    lower_bound, upper_bound = smoother_bounds(degree)
    return (
        degree + 1,
        stiffness,
        weights,
        diag_tile,
        share_tile,
        wall_mask(wall_blocks, degree + 1),
        lower_bound,
        upper_bound,
    )


def local_apply(nodal_field, stiffness, weights):
    node_count = stiffness.shape[0]
    blocks = nodal_field.reshape(
        nodal_field.shape[:5] + (nodal_field.shape[5] // node_count, node_count)
    )
    along_first = jnp.einsum("ai,rxyijzk->rxyajzk", stiffness, blocks, precision=PRECISE)
    along_second = jnp.einsum("bj,rxyijzk->rxyibzk", stiffness, blocks, precision=PRECISE)
    along_third = jnp.einsum("ck,rxyijzk->rxyijzc", stiffness, blocks, precision=PRECISE)
    weight_first = weights[:, None, None, None]
    weight_second = weights[None, :, None, None]
    weight_third = weights[None, None, None, :]
    total_sum = (
        along_first * weight_second * weight_third
        + along_second * weight_first * weight_third
        + along_third * weight_first * weight_second
    )
    return total_sum.reshape(nodal_field.shape)


def sum_spanwise(nodal_field, node_count):
    blocks = nodal_field.reshape(
        nodal_field.shape[:5] + (nodal_field.shape[5] // node_count, node_count)
    )
    joined = blocks[..., node_count - 1] + jnp.roll(blocks[..., 0], -1, axis=5)
    blocks = blocks.at[..., node_count - 1].set(joined)
    blocks = blocks.at[..., 0].set(jnp.roll(joined, 1, axis=5))
    return blocks.reshape(nodal_field.shape)


def sum_streamwise(nodal_field, node_count):
    final_node = node_count - 1
    first_face = nodal_field[:, :, :, 0]
    last_face = nodal_field[:, :, :, final_node]
    edge_faces = jnp.stack([first_face[:, 0], last_face[:, -1]], axis=1)
    padded = padded_2(edge_faces, (("stream", 1),), 1, True)
    before = jnp.concatenate([padded[:, 0:1], last_face[:, :-1]], axis=1)
    following = jnp.concatenate([first_face[:, 1:], padded[:, 3:4]], axis=1)
    nodal_field = nodal_field.at[:, :, :, 0].set(first_face + before)
    return nodal_field.at[:, :, :, final_node].set(last_face + following)


def sum_wallnormal(nodal_field, node_count):
    final_node = node_count - 1
    first_face = nodal_field[:, :, :, :, 0]
    last_face = nodal_field[:, :, :, :, final_node]
    edge_faces = jnp.stack([first_face[:, :, 0], last_face[:, :, -1]], axis=2)
    padded = padded_2(edge_faces, (("cross", 2),), 1, False)
    before = jnp.concatenate([padded[:, :, 0:1], last_face[:, :, :-1]], axis=2)
    following = jnp.concatenate([first_face[:, :, 1:], padded[:, :, 3:4]], axis=2)
    nodal_field = nodal_field.at[:, :, :, :, 0].set(first_face + before)
    return nodal_field.at[:, :, :, :, final_node].set(last_face + following)


def assemble(nodal_field, node_count):
    spanned = sum_spanwise(nodal_field, node_count)
    return sum_wallnormal(sum_streamwise(spanned, node_count), node_count)


def operate(nodal_field, level_data):
    return level_data[5] * assemble(
        local_apply(nodal_field, level_data[1], level_data[2]), level_data[0]
    )


def chebyshev(approx, residual, level_data, keep_residual):
    lower_bound = level_data[6]
    upper_bound = level_data[7]
    center = 0.5 * (upper_bound + lower_bound)
    spread = 0.5 * (upper_bound - lower_bound)
    sigma_ratio = center / spread
    rho_first = 1.0 / sigma_ratio
    rho_second = 1.0 / (2.0 * sigma_ratio - rho_first)
    scaling = level_data[5] * level_data[3]
    update = scaling * residual / center
    approx = approx + update
    residual = residual - operate(update, level_data)
    update = rho_second * rho_first * update + 2.0 * rho_second / spread * scaling * residual
    approx = approx + update
    if keep_residual:
        residual = residual - operate(update, level_data)
    return (approx, residual)


def restrict(nodal_field, lagrange_table):
    fine_count, coarse_count = lagrange_table.shape
    blocks = nodal_field.reshape(
        nodal_field.shape[:5] + (nodal_field.shape[5] // fine_count, fine_count)
    )
    reduced = jnp.einsum(
        "ia,jb,kc,rxyijzk->rxyabzc",
        lagrange_table,
        lagrange_table,
        lagrange_table,
        blocks,
        precision=PRECISE,
    )
    return reduced.reshape(
        nodal_field.shape[:3] + (coarse_count, coarse_count, reduced.shape[5] * coarse_count)
    )


def prolong(coarse_values, lagrange_table):
    fine_count, coarse_count = lagrange_table.shape
    blocks = coarse_values.reshape(
        coarse_values.shape[:5] + (coarse_values.shape[5] // coarse_count, coarse_count)
    )
    expanded = jnp.einsum(
        "ia,jb,kc,rxyabzc->rxyijzk",
        lagrange_table,
        lagrange_table,
        lagrange_table,
        blocks,
        precision=PRECISE,
    )
    return expanded.reshape(
        coarse_values.shape[:3] + (fine_count, fine_count, expanded.shape[5] * fine_count)
    )


def fourier_rows(row_index, point_index, total_count):
    half_size = total_count // 2
    frequency = jnp.where(row_index <= half_size, row_index, row_index - half_size)
    phase_angle = (
        2.0 * jnp.pi * (frequency * point_index % total_count).astype(jnp.float32) / total_count
    )
    row_scale = jnp.where(
        (row_index == 0) | (row_index == half_size),
        math.sqrt(1.0 / total_count),
        math.sqrt(2.0 / total_count),
    )
    return row_scale * jnp.where(row_index <= half_size, jnp.cos(phase_angle), jnp.sin(phase_angle))


def sine_rows(mode_index, point_index, total_count):
    product = mode_index * point_index % (2 * total_count)
    inside = (
        (mode_index > 0)
        & (mode_index < total_count)
        & (point_index > 0)
        & (point_index < total_count)
    )
    values = math.sqrt(2.0 / total_count) * jnp.sin(
        jnp.pi * product.astype(jnp.float32) / total_count
    )
    return jnp.where(inside, values, 0.0).astype(jnp.float32)


def gap_table(wall_index, span_index, wall_total, span_total):
    wall_angle = 0.5 * jnp.pi * wall_index.astype(jnp.float32) / wall_total
    wall_gap = 2.0 * jnp.sin(wall_angle) ** 2 + jnp.where(wall_index == 0, 1.0, 0.0)
    half_size = span_total // 2
    frequency = jnp.where(span_index <= half_size, span_index, span_index - half_size)
    span_gap = 2.0 * jnp.sin(jnp.pi * frequency.astype(jnp.float32) / span_total) ** 2
    return (wall_gap[:, None] + span_gap[None, :]).astype(jnp.float32)


def green_values(distance, half_gap, length):
    sinh_part = jnp.sqrt(half_gap * (2.0 + half_gap))
    decay_rate = jnp.log1p(half_gap + sinh_part)
    numerator = jnp.exp(-decay_rate * distance) + jnp.exp(-decay_rate * (length - distance))
    return numerator / (4.0 * sinh_part * -jnp.expm1(-decay_rate * length))


def expand_coarse(window, stream_blocks, wall_blocks):
    stream_parts = []
    for stream_shift in range(2):
        wall_parts = []
        for wall_shift in range(2):
            base_block = window[
                :,
                stream_shift : stream_shift + stream_blocks,
                wall_shift : wall_shift + wall_blocks,
            ]
            span_pair = jnp.stack([base_block, jnp.roll(base_block, -1, axis=3)], axis=4)
            wall_parts.append(span_pair.reshape(base_block.shape[:3] + (base_block.shape[3] * 2,)))
        stream_parts.append(jnp.stack(wall_parts, axis=3))
    return jnp.stack(stream_parts, axis=3)


def solve_coarse(coarse_field):
    values = coarse_field[:, :, :, 0, 0, 0::2]
    source_count, stream_blocks, wall_blocks, span_blocks = values.shape
    cross_count = lax.axis_size("cross")
    nx_total = stream_blocks * lax.axis_size("stream")
    ny_total = wall_blocks * cross_count
    stream_start = lax.axis_index("stream") * stream_blocks
    wall_start = lax.axis_index("cross") * wall_blocks
    span_index = jnp.arange(span_blocks, dtype=jnp.int32)
    fourier_table = fourier_rows(span_index[:, None], span_index[None, :], span_blocks)
    spectral = jnp.einsum("kz,rxyz->rxyk", fourier_table, values, precision=PRECISE)
    target_stream = stream_start + jnp.arange(stream_blocks + 1, dtype=jnp.int32)
    window_rows = wall_start + jnp.arange(wall_blocks + 1, dtype=jnp.int32)
    all_modes = jnp.arange(ny_total, dtype=jnp.int32)
    gap_all = gap_table(all_modes, span_index, ny_total, span_blocks)
    zero_whole = jnp.zeros((source_count, nx_total, ny_total, span_blocks), jnp.float32)
    shard_piece = lax.all_gather(spectral[None], ("stream", "cross"), axis=0, tiled=True)
    devices = jnp.arange(shard_piece.shape[0], dtype=jnp.int32)
    stream_rows = (devices // cross_count)[:, None, None] * stream_blocks + jnp.arange(
        stream_blocks, dtype=jnp.int32
    )[None, :, None]
    wall_rows = (devices % cross_count)[:, None, None] * wall_blocks + jnp.arange(
        wall_blocks, dtype=jnp.int32
    )[None, None, :]
    whole_field = zero_whole.at[:, stream_rows, wall_rows, :].add(jnp.moveaxis(shard_piece, 0, 1))
    sine_table = sine_rows(all_modes[:, None], all_modes[None, :], ny_total)
    modal_part = jnp.einsum("ay,rxyk->rxak", sine_table, whole_field, precision=PRECISE)
    stream_all = jnp.arange(nx_total, dtype=jnp.int32)
    distance = ((target_stream[:, None] - stream_all[None, :]) % nx_total).astype(jnp.float32)
    kernel = green_values(distance[:, :, None, None], gap_all[None, None], nx_total)
    solved = jnp.einsum("txak,rxak->rtak", kernel, modal_part, precision=PRECISE)
    sine_back = sine_rows(all_modes[:, None], window_rows[None, :], ny_total)
    window = jnp.einsum("aq,rtak->rtqk", sine_back, solved, precision=PRECISE)
    node_values = jnp.einsum("kz,rtqk->rtqz", fourier_table, window, precision=PRECISE)
    return expand_coarse(node_values, stream_blocks, wall_blocks)


def body(sources):
    wall_blocks = sources.shape[2]
    span_blocks = sources.shape[5] // (ORDER + 1)
    fine = build_level(ORDER, span_blocks, wall_blocks)
    middle = build_level(MID_ORDER, span_blocks, wall_blocks)
    coarse_keep = wall_mask(wall_blocks, 2)
    fine_to_mid = lagrange_matrix(ORDER, MID_ORDER)
    mid_to_coarse = lagrange_matrix(MID_ORDER, 1)
    forcing = fine[5] * assemble(sources, ORDER + 1)
    fine_approx, fine_resid = chebyshev(jnp.zeros_like(forcing), forcing, fine, True)
    mid_forcing = middle[5] * assemble(restrict(fine[4] * fine_resid, fine_to_mid), MID_ORDER + 1)
    mid_approx, mid_resid = chebyshev(jnp.zeros_like(mid_forcing), mid_forcing, middle, True)
    coarse_forcing = coarse_keep * assemble(restrict(middle[4] * mid_resid, mid_to_coarse), 2)
    coarse_values = solve_coarse(coarse_forcing)
    mid_approx = mid_approx + prolong(coarse_values, mid_to_coarse)
    mid_approx = chebyshev(mid_approx, mid_forcing - operate(mid_approx, middle), middle, False)[0]
    fine_approx = fine_approx + prolong(mid_approx, fine_to_mid)
    return chebyshev(fine_approx, forcing - operate(fine_approx, fine), fine, False)[0]


def solution(mesh):
    in_specs = (P(None, "stream", "cross", None, None, None),)
    out_specs = P(None, "stream", "cross", None, None, None)
    return jax.shard_map(body, mesh=mesh, in_specs=in_specs, out_specs=out_specs, check_vma=False)
```

profile of v0, /device:TPU:128, one launch (start us, length us, event | category | flops | bytes accessed | tf_op | source)
XLA Modules:
  0.0 589.0 jit_solution(631229854680324083)
XLA Ops:
  5.8 10.6 %scatter.220 = f32[2,1,1,8,8,16,8]{6,5,4,3,0,2,1:T(8,128)S(1)} dynamic-update-slice(f32[2,1,1,8,8,16,8]{6,5,4,3,0,2,1:T(8,128)S(1)} %reshape.4060, f32[2,1,1,8,8,16,1]{6,5,4,3,0,2,1:T(8,128)S(1)} %maximum_add_fusion, s32[]{:T(128)} %constant.1574.clone.1, s32[]{:T(128)} %constant.1574.clone.1, s32[]{:T(128)} %constant.1574.clone.1, s32[]{:T(128)} %constant.1574.clone.1, s32[]{:T(128)} %constant.1574.clone.1, ...) | dynamic-update-slice | bytes 16388 | tf_op jit(solution)/shard_map/scatter | solution.py:175
  16.4 2.0 scatter.221
  19.0 1.9 collective-permute-start
  20.9 7.0 %collective-permute-start.1 = (f32[2,1,1,8,128]{4,3,0,2,1:T(8,128)S(1)}, f32[2,1,1,8,128]{4,3,0,2,1:T(8,128)S(1)}, u32[]{:S(2)}, u32[]{:S(2)}) collective-permute-start(f32[2,1,1,8,128]{4,3,0,2,1:T(8,128)S(1)} %get-tuple-element.844), channel_id=1, source_target_pairs={{32,0},{64,32},{96,64},{128,96},{160,128},{192,160},{224,192},{256... | collective-permute-start | bytes 24584 | tf_op jit(solution)/shard_map/ppermute | solution.py:26
  29.2 3.8 collective-permute-start.2
  33.1 3.2 collective-permute-start.3
  40.4 7.4 %fusion.248 = f32[2,8,8,16,8]{3,4,2,1,0:T(8,128)S(1)} fusion(f32[2,8,8,16,8]{4,3,2,1,0:T(8,128)S(1)} %reshape.4067, f32[8,8,1,1,1]{1,0,4,3,2:T(8,128)S(1)} %copy-done.1), kind=kOutput, calls=%fused_computation.461 | convolution fusion | flops 1572864 | bytes 131328 | tf_op jit(solution)/shard_map/ck,rxyijzk->rxyijzc/dot_general | solution.py:158
  51.3 1.9 collective-permute-start.4
  53.2 7.0 %collective-permute-start.5 = (f32[2,1,1,8,128]{4,0,3,2,1:T(2,128)S(1)}, f32[2,1,1,8,128]{4,0,3,2,1:T(2,128)S(1)}, u32[]{:S(2)}, u32[]{:S(2)}) collective-permute-start(f32[2,1,1,8,128]{4,0,3,2,1:T(2,128)S(1)} %bitcast.1004), channel_id=1, source_target_pairs={{32,0},{64,32},{96,64},{128,96},{160,128},{192,160},{224,192},{256... | collective-permute-start | bytes 24584 | tf_op jit(solution)/shard_map/ppermute | solution.py:26
  61.6 4.6 collective-permute-start.7
  66.2 1.9 collective-permute-start.6
  68.2 4.8 collective-permute-done.6
  74.5 7.4 %fusion.250 = f32[2,8,8,16,8]{3,4,2,1,0:T(8,128)S(1)} fusion(f32[2,8,8,16,8]{4,3,2,1,0:T(8,128)S(1)} %reshape.4074, f32[8,8,1,1,1]{1,0,4,3,2:T(8,128)S(1)} %copy-done.1), kind=kOutput, calls=%fused_computation.463 | convolution fusion | flops 1572864 | bytes 131328 | tf_op jit(solution)/shard_map/ck,rxyijzk->rxyijzc/dot_general | solution.py:158
  85.3 1.9 collective-permute-start.8
  87.3 7.0 %collective-permute-start.9 = (f32[2,1,1,8,128]{4,0,3,2,1:T(2,128)S(1)}, f32[2,1,1,8,128]{4,0,3,2,1:T(2,128)S(1)}, u32[]{:S(2)}, u32[]{:S(2)}) collective-permute-start(f32[2,1,1,8,128]{4,0,3,2,1:T(2,128)S(1)} %bitcast.1005), channel_id=1, source_target_pairs={{32,0},{64,32},{96,64},{128,96},{160,128},{192,160},{224,192},{256... | collective-permute-start | bytes 24584 | tf_op jit(solution)/shard_map/ppermute | solution.py:26
  95.7 4.4 collective-permute-start.11
  102.1 4.8 collective-permute-done.10
  111.5 1.9 collective-permute-start.12
  113.4 7.0 %collective-permute-start.13 = (f32[2,1,1,4,64]{4,3,0,2,1:T(4,128)S(1)}, f32[2,1,1,4,64]{4,3,0,2,1:T(4,128)S(1)}, u32[]{:S(2)}, u32[]{:S(2)}) collective-permute-start(f32[2,1,1,4,64]{4,3,0,2,1:T(4,128)S(1)} %get-tuple-element.876), channel_id=1, source_target_pairs={{32,0},{64,32},{96,64},{128,96},{160,128},{192,160},{224,192},{256... | collective-permute-start | bytes 6152 | tf_op jit(solution)/shard_map/ppermute | solution.py:26
  121.7 3.0 collective-permute-start.15
  124.7 2.9 collective-permute-start.14
  127.6 3.8 collective-permute-done.14
  136.8 1.9 collective-permute-start.16
  138.7 7.0 %collective-permute-start.17 = (f32[2,1,1,4,64]{4,0,3,2,1:T(2,128)S(1)}, f32[2,1,1,4,64]{4,0,3,2,1:T(2,128)S(1)}, u32[]{:S(2)}, u32[]{:S(2)}) collective-permute-start(f32[2,1,1,4,64]{4,0,3,2,1:T(2,128)S(1)} %bitcast.1016), channel_id=1, source_target_pairs={{32,0},{64,32},{96,64},{128,96},{160,128},{192,160},{224,192},{256... | collective-permute-start | bytes 6152 | tf_op jit(solution)/shard_map/ppermute | solution.py:26
  147.1 2.9 collective-permute-start.19
  150.0 3.1 collective-permute-start.18
  153.1 3.5 collective-permute-done.18
  157.5 1.9 fusion.255
  161.1 1.9 collective-permute-start.20
  163.1 7.0 %collective-permute-start.21 = (f32[2,1,1,4,64]{4,0,3,2,1:T(2,128)S(1)}, f32[2,1,1,4,64]{4,0,3,2,1:T(2,128)S(1)}, u32[]{:S(2)}, u32[]{:S(2)}) collective-permute-start(f32[2,1,1,4,64]{4,0,3,2,1:T(2,128)S(1)} %bitcast.1017), channel_id=1, source_target_pairs={{32,0},{64,32},{96,64},{128,96},{160,128},{192,160},{224,192},{256... | collective-permute-start | bytes 6152 | tf_op jit(solution)/shard_map/ppermute | solution.py:26
  171.4 1.9 collective-permute-start.23
  173.4 3.9 collective-permute-start.22
  177.3 2.8 collective-permute-done.22
  183.1 1.9 collective-permute-start.24
  185.0 7.0 %collective-permute-start.25 = (f32[2,1,1,2,32]{4,3,0,2,1:T(2,128)S(1)}, f32[2,1,1,2,32]{4,3,0,2,1:T(2,128)S(1)}, u32[]{:S(2)}, u32[]{:S(2)}) collective-permute-start(f32[2,1,1,2,32]{4,3,0,2,1:T(2,128)S(1)} %get-tuple-element.900), channel_id=1, source_target_pairs={{32,0},{64,32},{96,64},{128,96},{160,128},{192,160},{224,192},{256... | collective-permute-start | bytes 1544 | tf_op jit(solution)/shard_map/ppermute | solution.py:26
  195.2 3.9 collective-permute-start.26
  199.3 2.6 collective-permute-done.26
  202.6 227.6 %all-gather.1 = f32[1024,2,16]{2,1,0:T(2,128)S(1)} all-gather(f32[1,2,16]{2,1,0:T(2,128)S(1)} %convolution_bitcast_fusion.13), channel_id=2, replica_groups=mesh['stream'=32,'cross'=32] {'stream','cross'}, dimensions={0}, use_global_device_ids=true | all-gather | bytes 131200 | tf_op jit(solution)/shard_map/all_gather | solution.py:346
  430.5 32.8 %scatter_fusion = f32[1024,2,16]{2,1,0:T(2,128)S(1)} fusion(f32[1024,2,16]{2,1,0:T(2,128)S(1)} %broadcast.1482, s32[1024]{0:T(1024)S(1)} %broadcast_select_fusion, f32[1024,2,16]{2,1,0:T(2,128)S(1)} %all-gather.1), kind=kCustom, calls=%fused_computation | custom fusion | flops 32768 | bytes 397312
  465.1 4.3 convolution_bitcast_fusion.5
  472.9 1.9 fusion.258
  476.5 1.9 collective-permute-start.28
  478.4 7.4 %collective-permute-start.29 = (f32[2,1,1,4,64]{4,0,3,2,1:T(2,128)S(1)}, f32[2,1,1,4,64]{4,0,3,2,1:T(2,128)S(1)}, u32[]{:S(2)}, u32[]{:S(2)}) collective-permute-start(f32[2,1,1,4,64]{4,0,3,2,1:T(2,128)S(1)} %bitcast.1018), channel_id=1, source_target_pairs={{32,0},{64,32},{96,64},{128,96},{160,128},{192,160},{224,192},{256... | collective-permute-start | bytes 6152 | tf_op jit(solution)/shard_map/ppermute | solution.py:26
  486.8 3.5 collective-permute-start.31
  490.3 2.3 collective-permute-start.30
  492.7 4.4 collective-permute-done.30
  497.9 1.9 fusion.261
  501.7 1.9 collective-permute-start.32
  503.7 7.0 %collective-permute-start.33 = (f32[2,1,1,4,64]{4,0,3,2,1:T(2,128)S(1)}, f32[2,1,1,4,64]{4,0,3,2,1:T(2,128)S(1)}, u32[]{:S(2)}, u32[]{:S(2)}) collective-permute-start(f32[2,1,1,4,64]{4,0,3,2,1:T(2,128)S(1)} %bitcast.1019), channel_id=1, source_target_pairs={{32,0},{64,32},{96,64},{128,96},{160,128},{192,160},{224,192},{256... | collective-permute-start | bytes 6152 | tf_op jit(solution)/shard_map/ppermute | solution.py:26
  512.0 2.2 collective-permute-start.35
  514.2 3.6 collective-permute-start.34
  517.9 3.0 collective-permute-done.34
  525.3 7.4 %fusion.264 = f32[2,8,8,16,8]{3,4,2,1,0:T(8,128)S(1)} fusion(f32[2,8,8,16,8]{4,3,2,1,0:T(8,128)S(1)} %reshape.4128, f32[8,8,1,1,1]{1,0,4,3,2:T(8,128)S(1)} %copy-done.1), kind=kOutput, calls=%fused_computation.477 | convolution fusion | flops 1572864 | bytes 131328 | tf_op jit(solution)/shard_map/ck,rxyijzk->rxyijzc/dot_general | solution.py:158
  536.1 1.9 collective-permute-start.36
  538.0 7.0 %collective-permute-start.37 = (f32[2,1,1,8,128]{4,0,3,2,1:T(2,128)S(1)}, f32[2,1,1,8,128]{4,0,3,2,1:T(2,128)S(1)}, u32[]{:S(2)}, u32[]{:S(2)}) collective-permute-start(f32[2,1,1,8,128]{4,0,3,2,1:T(2,128)S(1)} %bitcast.1006), channel_id=1, source_target_pairs={{32,0},{64,32},{96,64},{128,96},{160,128},{192,160},{224,192},{256... | collective-permute-start | bytes 24584 | tf_op jit(solution)/shard_map/ppermute | solution.py:26
  546.4 2.4 collective-permute-start.39
  548.8 3.4 collective-permute-start.38
  552.3 3.3 collective-permute-done.38
  557.3 7.4 %fusion.267 = f32[2,8,8,16,8]{3,4,2,1,0:T(8,128)S(1)} fusion(f32[2,8,8,16,8]{4,3,2,1,0:T(8,128)S(1)} %reshape.4135, f32[8,8,1,1,1]{1,0,4,3,2:T(8,128)S(1)} %copy-done.1), kind=kOutput, calls=%fused_computation.480 | convolution fusion | flops 1572864 | bytes 131328 | tf_op jit(solution)/shard_map/ck,rxyijzk->rxyijzc/dot_general | solution.py:158
  568.7 1.9 collective-permute-start.40
  570.7 7.0 %collective-permute-start.41 = (f32[2,1,1,8,128]{4,0,3,2,1:T(2,128)S(1)}, f32[2,1,1,8,128]{4,0,3,2,1:T(2,128)S(1)}, u32[]{:S(2)}, u32[]{:S(2)}) collective-permute-start(f32[2,1,1,8,128]{4,0,3,2,1:T(2,128)S(1)} %bitcast.1007), channel_id=1, source_target_pairs={{32,0},{64,32},{96,64},{128,96},{160,128},{192,160},{224,192},{256... | collective-permute-start | bytes 24584 | tf_op jit(solution)/shard_map/ppermute | solution.py:26
  579.1 2.2 collective-permute-start.43
  581.3 3.6 collective-permute-start.42
  585.0 3.1 collective-permute-done.42
  (430 shorter events, 76.7 us)
Async XLA Ops:
  5.8 10.6 %copy-start = (f32[2,1,1,8,8,16,1]{6,5,4,3,0,2,1:T(8,128)S(1)}, f32[2,1,1,8,8,16,1]{6,5,4,3,0,2,1:T(8,128)}, u32[]{:S(2)}) copy-start(f32[2,1,1,8,8,16,1]{6,5,4,3,0,2,1:T(8,128)} %copy.1515) | copy-start | bytes 24580
  19.0 9.1 %copy-start.6 = (f32[8,8,128]{2,1,0:T(8,128)S(1)}, f32[8,8,128]{2,1,0:T(8,128)}, u32[]{:S(2)}) copy-start(f32[8,8,128]{2,1,0:T(8,128)} %constant.1606.clone) | copy-start | bytes 98308
  19.0 10.0 %collective-permute-start = (f32[2,1,1,8,128]{4,3,0,2,1:T(8,128)S(1)}, f32[2,1,1,8,128]{4,3,0,2,1:T(8,128)S(1)}, u32[]{:S(2)}, u32[]{:S(2)}) collective-permute-start(f32[2,1,1,8,128]{4,3,0,2,1:T(8,128)S(1)} %get-tuple-element.843), channel_id=1, source_target_pairs={{0,32},{32,64},{64,96},{96,128},{128,160},{160,192},{192,224},{224... | collective-permute-start | bytes 24584 | tf_op jit(solution)/shard_map/ppermute | solution.py:23
  20.9 8.3 %collective-permute-start.1 = (f32[2,1,1,8,128]{4,3,0,2,1:T(8,128)S(1)}, f32[2,1,1,8,128]{4,3,0,2,1:T(8,128)S(1)}, u32[]{:S(2)}, u32[]{:S(2)}) collective-permute-start(f32[2,1,1,8,128]{4,3,0,2,1:T(8,128)S(1)} %get-tuple-element.844), channel_id=1, source_target_pairs={{32,0},{64,32},{96,64},{128,96},{160,128},{192,160},{224,192},{256... | collective-permute-start | bytes 24584 | tf_op jit(solution)/shard_map/ppermute | solution.py:26
  28.0 0.7 copy-start.10
  29.2 7.8 %collective-permute-start.2 = (f32[2,1,1,8,128]{4,3,0,2,1:T(8,128)S(1)}, f32[2,1,1,8,128]{4,3,0,2,1:T(8,128)S(1)}, u32[]{:S(2)}, u32[]{:S(2)}) collective-permute-start(f32[2,1,1,8,128]{4,3,0,2,1:T(8,128)S(1)} %bitcast.973), channel_id=1, source_target_pairs={{0,1},{1,2},{2,3},{3,4},{4,5},{5,6},{6,7},{7,8},{8,9},{9,10},{10,1... | collective-permute-start | bytes 24584 | tf_op jit(solution)/shard_map/ppermute | solution.py:23
  33.1 5.5 collective-permute-start.3
  36.3 0.7 copy-start.11
  39.7 0.7 copy-start.1
  47.8 0.7 copy-start.2
  51.3 9.0 %collective-permute-start.4 = (f32[2,1,1,8,128]{4,0,3,2,1:T(2,128)S(1)}, f32[2,1,1,8,128]{4,0,3,2,1:T(2,128)S(1)}, u32[]{:S(2)}, u32[]{:S(2)}) collective-permute-start(f32[2,1,1,8,128]{4,0,3,2,1:T(2,128)S(1)} %bitcast.1003), channel_id=1, source_target_pairs={{0,32},{32,64},{64,96},{96,128},{128,160},{160,192},{192,224},{224... | collective-permute-start | bytes 24584 | tf_op jit(solution)/shard_map/ppermute | solution.py:23
  53.2 8.3 %collective-permute-start.5 = (f32[2,1,1,8,128]{4,0,3,2,1:T(2,128)S(1)}, f32[2,1,1,8,128]{4,0,3,2,1:T(2,128)S(1)}, u32[]{:S(2)}, u32[]{:S(2)}) collective-permute-start(f32[2,1,1,8,128]{4,0,3,2,1:T(2,128)S(1)} %bitcast.1004), channel_id=1, source_target_pairs={{32,0},{64,32},{96,64},{128,96},{160,128},{192,160},{224,192},{256... | collective-permute-start | bytes 24584 | tf_op jit(solution)/shard_map/ppermute | solution.py:26
  61.6 6.6 %collective-permute-start.7 = (f32[2,1,1,8,128]{4,3,0,2,1:T(8,128)S(1)}, f32[2,1,1,8,128]{4,3,0,2,1:T(8,128)S(1)}, u32[]{:S(2)}, u32[]{:S(2)}) collective-permute-start(f32[2,1,1,8,128]{4,3,0,2,1:T(8,128)S(1)} %get-tuple-element.836), channel_id=1, source_target_pairs={{1,0},{2,1},{3,2},{4,3},{5,4},{6,5},{7,6},{8,7},{9,8},{10,9},{11,1... | collective-permute-start | bytes 24584 | tf_op jit(solution)/shard_map/ppermute | solution.py:26
  66.2 6.8 %collective-permute-start.6 = (f32[2,1,1,8,128]{4,3,0,2,1:T(8,128)S(1)}, f32[2,1,1,8,128]{4,3,0,2,1:T(8,128)S(1)}, u32[]{:S(2)}, u32[]{:S(2)}) collective-permute-start(f32[2,1,1,8,128]{4,3,0,2,1:T(8,128)S(1)} %get-tuple-element.835), channel_id=1, source_target_pairs={{0,1},{1,2},{2,3},{3,4},{4,5},{5,6},{6,7},{7,8},{8,9},{9,10},{10,1... | collective-permute-start | bytes 24584 | tf_op jit(solution)/shard_map/ppermute | solution.py:23
  85.3 9.0 %collective-permute-start.8 = (f32[2,1,1,8,128]{4,0,3,2,1:T(2,128)S(1)}, f32[2,1,1,8,128]{4,0,3,2,1:T(2,128)S(1)}, u32[]{:S(2)}, u32[]{:S(2)}) collective-permute-start(f32[2,1,1,8,128]{4,0,3,2,1:T(2,128)S(1)} %bitcast.1008), channel_id=1, source_target_pairs={{0,32},{32,64},{64,96},{96,128},{128,160},{160,192},{192,224},{224... | collective-permute-start | bytes 24584 | tf_op jit(solution)/shard_map/ppermute | solution.py:23
  87.3 8.3 %collective-permute-start.9 = (f32[2,1,1,8,128]{4,0,3,2,1:T(2,128)S(1)}, f32[2,1,1,8,128]{4,0,3,2,1:T(2,128)S(1)}, u32[]{:S(2)}, u32[]{:S(2)}) collective-permute-start(f32[2,1,1,8,128]{4,0,3,2,1:T(2,128)S(1)} %bitcast.1005), channel_id=1, source_target_pairs={{32,0},{64,32},{96,64},{128,96},{160,128},{192,160},{224,192},{256... | collective-permute-start | bytes 24584 | tf_op jit(solution)/shard_map/ppermute | solution.py:26
  95.7 6.4 %collective-permute-start.11 = (f32[2,1,1,8,128]{4,3,0,2,1:T(8,128)S(1)}, f32[2,1,1,8,128]{4,3,0,2,1:T(8,128)S(1)}, u32[]{:S(2)}, u32[]{:S(2)}) collective-permute-start(f32[2,1,1,8,128]{4,3,0,2,1:T(8,128)S(1)} %get-tuple-element.830), channel_id=1, source_target_pairs={{1,0},{2,1},{3,2},{4,3},{5,4},{6,5},{7,6},{8,7},{9,8},{10,9},{11,1... | collective-permute-start | bytes 24584 | tf_op jit(solution)/shard_map/ppermute | solution.py:26
  100.2 6.7 %collective-permute-start.10 = (f32[2,1,1,8,128]{4,3,0,2,1:T(8,128)S(1)}, f32[2,1,1,8,128]{4,3,0,2,1:T(8,128)S(1)}, u32[]{:S(2)}, u32[]{:S(2)}) collective-permute-start(f32[2,1,1,8,128]{4,3,0,2,1:T(8,128)S(1)} %get-tuple-element.829), channel_id=1, source_target_pairs={{0,1},{1,2},{2,3},{3,4},{4,5},{5,6},{6,7},{7,8},{8,9},{9,10},{10,1... | collective-permute-start | bytes 24584 | tf_op jit(solution)/shard_map/ppermute | solution.py:23
  107.0 0.8 copy-start.5
  108.4 0.7 copy-start.4
  111.5 8.9 %collective-permute-start.12 = (f32[2,1,1,4,64]{4,3,0,2,1:T(4,128)S(1)}, f32[2,1,1,4,64]{4,3,0,2,1:T(4,128)S(1)}, u32[]{:S(2)}, u32[]{:S(2)}) collective-permute-start(f32[2,1,1,4,64]{4,3,0,2,1:T(4,128)S(1)} %get-tuple-element.875), channel_id=1, source_target_pairs={{0,32},{32,64},{64,96},{96,128},{128,160},{160,192},{192,224},{224... | collective-permute-start | bytes 6152 | tf_op jit(solution)/shard_map/ppermute | solution.py:23
  113.4 8.3 %collective-permute-start.13 = (f32[2,1,1,4,64]{4,3,0,2,1:T(4,128)S(1)}, f32[2,1,1,4,64]{4,3,0,2,1:T(4,128)S(1)}, u32[]{:S(2)}, u32[]{:S(2)}) collective-permute-start(f32[2,1,1,4,64]{4,3,0,2,1:T(4,128)S(1)} %get-tuple-element.876), channel_id=1, source_target_pairs={{32,0},{64,32},{96,64},{128,96},{160,128},{192,160},{224,192},{256... | collective-permute-start | bytes 6152 | tf_op jit(solution)/shard_map/ppermute | solution.py:26
  121.7 9.7 %collective-permute-start.15 = (f32[2,1,1,4,64]{4,3,0,2,1:T(4,128)S(1)}, f32[2,1,1,4,64]{4,3,0,2,1:T(4,128)S(1)}, u32[]{:S(2)}, u32[]{:S(2)}) collective-permute-start(f32[2,1,1,4,64]{4,3,0,2,1:T(4,128)S(1)} %bitcast.984), channel_id=1, source_target_pairs={{1,0},{2,1},{3,2},{4,3},{5,4},{6,5},{7,6},{8,7},{9,8},{10,9},{11,1... | collective-permute-start | bytes 6152 | tf_op jit(solution)/shard_map/ppermute | solution.py:26
  124.7 6.7 %collective-permute-start.14 = (f32[2,1,1,4,64]{4,3,0,2,1:T(4,128)S(1)}, f32[2,1,1,4,64]{4,3,0,2,1:T(4,128)S(1)}, u32[]{:S(2)}, u32[]{:S(2)}) collective-permute-start(f32[2,1,1,4,64]{4,3,0,2,1:T(4,128)S(1)} %bitcast.982), channel_id=1, source_target_pairs={{0,1},{1,2},{2,3},{3,4},{4,5},{5,6},{6,7},{7,8},{8,9},{9,10},{10,1... | collective-permute-start | bytes 6152 | tf_op jit(solution)/shard_map/ppermute | solution.py:23
  132.0 0.7 copy-start.3
  134.7 0.7 copy-start.7
  136.8 8.9 %collective-permute-start.16 = (f32[2,1,1,4,64]{4,0,3,2,1:T(2,128)S(1)}, f32[2,1,1,4,64]{4,0,3,2,1:T(2,128)S(1)}, u32[]{:S(2)}, u32[]{:S(2)}) collective-permute-start(f32[2,1,1,4,64]{4,0,3,2,1:T(2,128)S(1)} %bitcast.1015), channel_id=1, source_target_pairs={{0,32},{32,64},{64,96},{96,128},{128,160},{160,192},{192,224},{224... | collective-permute-start | bytes 6152 | tf_op jit(solution)/shard_map/ppermute | solution.py:23
  138.7 8.3 %collective-permute-start.17 = (f32[2,1,1,4,64]{4,0,3,2,1:T(2,128)S(1)}, f32[2,1,1,4,64]{4,0,3,2,1:T(2,128)S(1)}, u32[]{:S(2)}, u32[]{:S(2)}) collective-permute-start(f32[2,1,1,4,64]{4,0,3,2,1:T(2,128)S(1)} %bitcast.1016), channel_id=1, source_target_pairs={{32,0},{64,32},{96,64},{128,96},{160,128},{192,160},{224,192},{256... | collective-permute-start | bytes 6152 | tf_op jit(solution)/shard_map/ppermute | solution.py:26
  147.1 6.1 %collective-permute-start.19 = (f32[2,1,1,4,64]{4,3,0,2,1:T(4,128)S(1)}, f32[2,1,1,4,64]{4,3,0,2,1:T(4,128)S(1)}, u32[]{:S(2)}, u32[]{:S(2)}) collective-permute-start(f32[2,1,1,4,64]{4,3,0,2,1:T(4,128)S(1)} %get-tuple-element.868), channel_id=1, source_target_pairs={{1,0},{2,1},{3,2},{4,3},{5,4},{6,5},{7,6},{8,7},{9,8},{10,9},{11,1... | collective-permute-start | bytes 6152 | tf_op jit(solution)/shard_map/ppermute | solution.py:26
  150.0 6.7 %collective-permute-start.18 = (f32[2,1,1,4,64]{4,3,0,2,1:T(4,128)S(1)}, f32[2,1,1,4,64]{4,3,0,2,1:T(4,128)S(1)}, u32[]{:S(2)}, u32[]{:S(2)}) collective-permute-start(f32[2,1,1,4,64]{4,3,0,2,1:T(4,128)S(1)} %get-tuple-element.867), channel_id=1, source_target_pairs={{0,1},{1,2},{2,3},{3,4},{4,5},{5,6},{6,7},{7,8},{8,9},{9,10},{10,1... | collective-permute-start | bytes 6152 | tf_op jit(solution)/shard_map/ppermute | solution.py:23
  161.1 8.9 %collective-permute-start.20 = (f32[2,1,1,4,64]{4,0,3,2,1:T(2,128)S(1)}, f32[2,1,1,4,64]{4,0,3,2,1:T(2,128)S(1)}, u32[]{:S(2)}, u32[]{:S(2)}) collective-permute-start(f32[2,1,1,4,64]{4,0,3,2,1:T(2,128)S(1)} %bitcast.1020), channel_id=1, source_target_pairs={{0,32},{32,64},{64,96},{96,128},{128,160},{160,192},{192,224},{224... | collective-permute-start | bytes 6152 | tf_op jit(solution)/shard_map/ppermute | solution.py:23
  163.1 8.3 %collective-permute-start.21 = (f32[2,1,1,4,64]{4,0,3,2,1:T(2,128)S(1)}, f32[2,1,1,4,64]{4,0,3,2,1:T(2,128)S(1)}, u32[]{:S(2)}, u32[]{:S(2)}) collective-permute-start(f32[2,1,1,4,64]{4,0,3,2,1:T(2,128)S(1)} %bitcast.1017), channel_id=1, source_target_pairs={{32,0},{64,32},{96,64},{128,96},{160,128},{192,160},{224,192},{256... | collective-permute-start | bytes 6152 | tf_op jit(solution)/shard_map/ppermute | solution.py:26
  171.4 5.9 collective-permute-start.23
  173.4 6.7 %collective-permute-start.22 = (f32[2,1,1,4,64]{4,3,0,2,1:T(4,128)S(1)}, f32[2,1,1,4,64]{4,3,0,2,1:T(4,128)S(1)}, u32[]{:S(2)}, u32[]{:S(2)}) collective-permute-start(f32[2,1,1,4,64]{4,3,0,2,1:T(4,128)S(1)} %get-tuple-element.861), channel_id=1, source_target_pairs={{0,1},{1,2},{2,3},{3,4},{4,5},{5,6},{6,7},{7,8},{8,9},{9,10},{10,1... | collective-permute-start | bytes 6152 | tf_op jit(solution)/shard_map/ppermute | solution.py:23
  180.1 0.7 copy-start.9
  181.1 0.7 copy-start.8
  183.1 8.9 %collective-permute-start.24 = (f32[2,1,1,2,32]{4,3,0,2,1:T(2,128)S(1)}, f32[2,1,1,2,32]{4,3,0,2,1:T(2,128)S(1)}, u32[]{:S(2)}, u32[]{:S(2)}) collective-permute-start(f32[2,1,1,2,32]{4,3,0,2,1:T(2,128)S(1)} %get-tuple-element.899), channel_id=1, source_target_pairs={{0,32},{32,64},{64,96},{96,128},{128,160},{160,192},{192,224},{224... | collective-permute-start | bytes 1544 | tf_op jit(solution)/shard_map/ppermute | solution.py:23
  185.0 8.3 %collective-permute-start.25 = (f32[2,1,1,2,32]{4,3,0,2,1:T(2,128)S(1)}, f32[2,1,1,2,32]{4,3,0,2,1:T(2,128)S(1)}, u32[]{:S(2)}, u32[]{:S(2)}) collective-permute-start(f32[2,1,1,2,32]{4,3,0,2,1:T(2,128)S(1)} %get-tuple-element.900), channel_id=1, source_target_pairs={{32,0},{64,32},{96,64},{128,96},{160,128},{192,160},{224,192},{256... | collective-permute-start | bytes 1544 | tf_op jit(solution)/shard_map/ppermute | solution.py:26
  193.3 8.7 %collective-permute-start.27 = (f32[2,1,1,2,32]{4,3,0,2,1:T(2,128)S(1)}, f32[2,1,1,2,32]{4,3,0,2,1:T(2,128)S(1)}, u32[]{:S(2)}, u32[]{:S(2)}) collective-permute-start(f32[2,1,1,2,32]{4,3,0,2,1:T(2,128)S(1)} %bitcast.1013), channel_id=1, source_target_pairs={{1,0},{2,1},{3,2},{4,3},{5,4},{6,5},{7,6},{8,7},{9,8},{10,9},{11,1... | collective-permute-start | bytes 1544 | tf_op jit(solution)/shard_map/ppermute | solution.py:26
  195.2 6.7 %collective-permute-start.26 = (f32[2,1,1,2,32]{4,3,0,2,1:T(2,128)S(1)}, f32[2,1,1,2,32]{4,3,0,2,1:T(2,128)S(1)}, u32[]{:S(2)}, u32[]{:S(2)}) collective-permute-start(f32[2,1,1,2,32]{4,3,0,2,1:T(2,128)S(1)} %bitcast.1011), channel_id=1, source_target_pairs={{0,1},{1,2},{2,3},{3,4},{4,5},{5,6},{6,7},{7,8},{8,9},{9,10},{10,1... | collective-permute-start | bytes 1544 | tf_op jit(solution)/shard_map/ppermute | solution.py:23
  476.5 9.3 %collective-permute-start.28 = (f32[2,1,1,4,64]{4,0,3,2,1:T(2,128)S(1)}, f32[2,1,1,4,64]{4,0,3,2,1:T(2,128)S(1)}, u32[]{:S(2)}, u32[]{:S(2)}) collective-permute-start(f32[2,1,1,4,64]{4,0,3,2,1:T(2,128)S(1)} %bitcast.1021), channel_id=1, source_target_pairs={{0,32},{32,64},{64,96},{96,128},{128,160},{160,192},{192,224},{224... | collective-permute-start | bytes 6152 | tf_op jit(solution)/shard_map/ppermute | solution.py:23
  478.4 8.3 %collective-permute-start.29 = (f32[2,1,1,4,64]{4,0,3,2,1:T(2,128)S(1)}, f32[2,1,1,4,64]{4,0,3,2,1:T(2,128)S(1)}, u32[]{:S(2)}, u32[]{:S(2)}) collective-permute-start(f32[2,1,1,4,64]{4,0,3,2,1:T(2,128)S(1)} %bitcast.1018), channel_id=1, source_target_pairs={{32,0},{64,32},{96,64},{128,96},{160,128},{192,160},{224,192},{256... | collective-permute-start | bytes 6152 | tf_op jit(solution)/shard_map/ppermute | solution.py:26
  486.8 5.9 collective-permute-start.31
  490.3 6.7 %collective-permute-start.30 = (f32[2,1,1,4,64]{4,3,0,2,1:T(4,128)S(1)}, f32[2,1,1,4,64]{4,3,0,2,1:T(4,128)S(1)}, u32[]{:S(2)}, u32[]{:S(2)}) collective-permute-start(f32[2,1,1,4,64]{4,3,0,2,1:T(4,128)S(1)} %get-tuple-element.855), channel_id=1, source_target_pairs={{0,1},{1,2},{2,3},{3,4},{4,5},{5,6},{6,7},{7,8},{8,9},{9,10},{10,1... | collective-permute-start | bytes 6152 | tf_op jit(solution)/shard_map/ppermute | solution.py:23
  501.7 8.9 %collective-permute-start.32 = (f32[2,1,1,4,64]{4,0,3,2,1:T(2,128)S(1)}, f32[2,1,1,4,64]{4,0,3,2,1:T(2,128)S(1)}, u32[]{:S(2)}, u32[]{:S(2)}) collective-permute-start(f32[2,1,1,4,64]{4,0,3,2,1:T(2,128)S(1)} %bitcast.1022), channel_id=1, source_target_pairs={{0,32},{32,64},{64,96},{96,128},{128,160},{160,192},{192,224},{224... | collective-permute-start | bytes 6152 | tf_op jit(solution)/shard_map/ppermute | solution.py:23
  503.7 8.3 %collective-permute-start.33 = (f32[2,1,1,4,64]{4,0,3,2,1:T(2,128)S(1)}, f32[2,1,1,4,64]{4,0,3,2,1:T(2,128)S(1)}, u32[]{:S(2)}, u32[]{:S(2)}) collective-permute-start(f32[2,1,1,4,64]{4,0,3,2,1:T(2,128)S(1)} %bitcast.1019), channel_id=1, source_target_pairs={{32,0},{64,32},{96,64},{128,96},{160,128},{192,160},{224,192},{256... | collective-permute-start | bytes 6152 | tf_op jit(solution)/shard_map/ppermute | solution.py:26
  512.0 5.9 collective-permute-start.35
  514.2 6.7 %collective-permute-start.34 = (f32[2,1,1,4,64]{4,3,0,2,1:T(4,128)S(1)}, f32[2,1,1,4,64]{4,3,0,2,1:T(4,128)S(1)}, u32[]{:S(2)}, u32[]{:S(2)}) collective-permute-start(f32[2,1,1,4,64]{4,3,0,2,1:T(4,128)S(1)} %get-tuple-element.849), channel_id=1, source_target_pairs={{0,1},{1,2},{2,3},{3,4},{4,5},{5,6},{6,7},{7,8},{8,9},{9,10},{10,1... | collective-permute-start | bytes 6152 | tf_op jit(solution)/shard_map/ppermute | solution.py:23
  536.1 8.9 %collective-permute-start.36 = (f32[2,1,1,8,128]{4,0,3,2,1:T(2,128)S(1)}, f32[2,1,1,8,128]{4,0,3,2,1:T(2,128)S(1)}, u32[]{:S(2)}, u32[]{:S(2)}) collective-permute-start(f32[2,1,1,8,128]{4,0,3,2,1:T(2,128)S(1)} %bitcast.1009), channel_id=1, source_target_pairs={{0,32},{32,64},{64,96},{96,128},{128,160},{160,192},{192,224},{224... | collective-permute-start | bytes 24584 | tf_op jit(solution)/shard_map/ppermute | solution.py:23
  538.0 8.3 %collective-permute-start.37 = (f32[2,1,1,8,128]{4,0,3,2,1:T(2,128)S(1)}, f32[2,1,1,8,128]{4,0,3,2,1:T(2,128)S(1)}, u32[]{:S(2)}, u32[]{:S(2)}) collective-permute-start(f32[2,1,1,8,128]{4,0,3,2,1:T(2,128)S(1)} %bitcast.1006), channel_id=1, source_target_pairs={{32,0},{64,32},{96,64},{128,96},{160,128},{192,160},{224,192},{256... | collective-permute-start | bytes 24584 | tf_op jit(solution)/shard_map/ppermute | solution.py:26
  546.4 5.9 collective-permute-start.39
  548.8 6.8 %collective-permute-start.38 = (f32[2,1,1,8,128]{4,3,0,2,1:T(8,128)S(1)}, f32[2,1,1,8,128]{4,3,0,2,1:T(8,128)S(1)}, u32[]{:S(2)}, u32[]{:S(2)}) collective-permute-start(f32[2,1,1,8,128]{4,3,0,2,1:T(8,128)S(1)} %get-tuple-element.813), channel_id=1, source_target_pairs={{0,1},{1,2},{2,3},{3,4},{4,5},{5,6},{6,7},{7,8},{8,9},{9,10},{10,1... | collective-permute-start | bytes 24584 | tf_op jit(solution)/shard_map/ppermute | solution.py:23
  568.7 8.9 %collective-permute-start.40 = (f32[2,1,1,8,128]{4,0,3,2,1:T(2,128)S(1)}, f32[2,1,1,8,128]{4,0,3,2,1:T(2,128)S(1)}, u32[]{:S(2)}, u32[]{:S(2)}) collective-permute-start(f32[2,1,1,8,128]{4,0,3,2,1:T(2,128)S(1)} %bitcast.1010), channel_id=1, source_target_pairs={{0,32},{32,64},{64,96},{96,128},{128,160},{160,192},{192,224},{224... | collective-permute-start | bytes 24584 | tf_op jit(solution)/shard_map/ppermute | solution.py:23
  570.7 8.3 %collective-permute-start.41 = (f32[2,1,1,8,128]{4,0,3,2,1:T(2,128)S(1)}, f32[2,1,1,8,128]{4,0,3,2,1:T(2,128)S(1)}, u32[]{:S(2)}, u32[]{:S(2)}) collective-permute-start(f32[2,1,1,8,128]{4,0,3,2,1:T(2,128)S(1)} %bitcast.1007), channel_id=1, source_target_pairs={{32,0},{64,32},{96,64},{128,96},{160,128},{192,160},{224,192},{256... | collective-permute-start | bytes 24584 | tf_op jit(solution)/shard_map/ppermute | solution.py:26
  579.1 5.9 collective-permute-start.43
  581.3 6.8 %collective-permute-start.42 = (f32[2,1,1,8,128]{4,3,0,2,1:T(8,128)S(1)}, f32[2,1,1,8,128]{4,3,0,2,1:T(8,128)S(1)}, u32[]{:S(2)}, u32[]{:S(2)}) collective-permute-start(f32[2,1,1,8,128]{4,3,0,2,1:T(8,128)S(1)} %get-tuple-element.807), channel_id=1, source_target_pairs={{0,1},{1,2},{2,3},{3,4},{4,5},{5,6},{6,7},{7,8},{8,9},{9,10},{10,1... | collective-permute-start | bytes 24584 | tf_op jit(solution)/shard_map/ppermute | solution.py:23
where the time goes:
time: 599 us; the launch traced here: 589 us
  blocking collectives  228 us (38%)
  starting transfers between devices  165 us (28%)
  matrix products  55.6 us (9%)
  waiting for transfers between devices  50.1 us (8%)
  local copies, waits for them, and re-layouts  48.1 us (8%)
  other arithmetic  40.4 us (7%)
    all_gather x1, blocking collectives, solve_coarse(): lax.all_gather(spectral[None], ('stream', 'cross'), axis=0, tiled=True)  228 us
    ppermute x22, starting transfers between devices, padded_2(): lax.ppermute(lax.slice_in_dim(block, 0, width, axis=dim), axis, backward)  109 us
    ppermute x22, starting transfers between devices, padded_2(): lax.ppermute(lax.slice_in_dim(block, block.shape[dim] - width, None, axis...  55.6 us
    dot_general x8, matrix products, local_apply(): jnp.einsum('ck,rxyijzk->rxyijzc', stiffness, blocks, precision=PRECISE)  37.3 us
    ppermute x22, waiting for transfers between devices, padded_2(): lax.ppermute(lax.slice_in_dim(block, block.shape[dim] - width, None, axis...  36.2 us
    unnamed x4, other arithmetic  32.9 us
    ppermute x22, waiting for transfers between devices, padded_2(): lax.ppermute(lax.slice_in_dim(block, 0, width, axis=dim), axis, backward)  13.9 us
  transfers between devices with their start and end apart: 44, of which 22 were waited for; matrix products, arithmetic and copies ran while one was open for 0% of the time, Pallas kernels for 0%

commit v1 on v0

v1 whole, which is shorter than its diff:
```python
import functools
import math

import jax
import jax.numpy as jnp
import numpy as np
from jax import lax
from jax.experimental import pallas as pl
from jax.experimental.pallas import tpu as pltpu
from jax.sharding import PartitionSpec as P

ORDER = 7
MID_ORDER = 3
EZ = 16
LANES = 128
MODES = 32
EXACT = lax.Precision.HIGHEST
MESH_ID = pl.DeviceIdType.MESH


def legendre_pair(degree, points):
    below_poly = np.ones(points.shape)
    top_poly = points.copy()
    for step in range(2, degree + 1):
        below_poly, top_poly = (
            top_poly,
            ((2 * step - 1) * points * top_poly - (step - 1) * below_poly) / step,
        )
    return (below_poly, top_poly)


@functools.lru_cache(None)
def gll_tables(degree):
    nodes = -np.cos(np.pi * np.arange(degree + 1) / degree)
    for _ in range(100):
        below_poly, top_poly = legendre_pair(degree, nodes)
        nodes = nodes - (nodes * top_poly - below_poly) / ((degree + 1) * top_poly)
    at_nodes = legendre_pair(degree, nodes)[1]
    weights = 2.0 / (degree * (degree + 1) * at_nodes**2)
    count = degree + 1
    derivative = np.zeros((count, count))
    for target in range(count):
        for source in range(count):
            if target != source:
                derivative[target, source] = at_nodes[target] / (
                    at_nodes[source] * (nodes[target] - nodes[source])
                )
    derivative[0, 0] = -degree * (degree + 1) / 4.0
    derivative[degree, degree] = degree * (degree + 1) / 4.0
    stiffness = derivative.T @ (weights[:, None] * derivative)
    return (nodes, weights, stiffness)


def lagrange_matrix(fine_degree, coarse_degree):
    fine_nodes = gll_tables(fine_degree)[0]
    coarse_nodes = gll_tables(coarse_degree)[0]
    table = np.ones((fine_degree + 1, coarse_degree + 1))
    for column in range(coarse_degree + 1):
        for other in range(coarse_degree + 1):
            if other != column:
                table[:, column] *= (fine_nodes - coarse_nodes[other]) / (
                    coarse_nodes[column] - coarse_nodes[other]
                )
    return table


@functools.lru_cache(None)
def smoother(degree):
    stiffness = gll_tables(degree)[2]
    elements = 6
    size = elements * degree
    assembled = np.zeros((size, size))
    for element in range(elements):
        for row in range(degree + 1):
            for col in range(degree + 1):
                assembled[(element * degree + row) % size, (element * degree + col) % size] += (
                    stiffness[row, col]
                )
    diagonal = np.sqrt(np.diagonal(assembled))
    scaled = assembled / diagonal[:, None] / diagonal[None, :]
    positions = np.arange(size)
    vector = np.where(positions % 2 == 0, 1.0, -1.0) * (1.0 + positions / size)
    for _ in range(2000):
        vector = scaled @ vector
        vector = vector / np.sqrt(np.sum(vector * vector))
    high = float(np.sum(vector * (scaled @ vector)) / np.sum(vector * vector))
    low = 0.1 * high
    theta, delta = 0.5 * (high + low), 0.5 * (high - low)
    sigma = theta / delta
    rho1 = 1.0 / sigma
    rho2 = 1.0 / (2.0 * sigma - rho1)
    return theta, rho2 * rho1, 2.0 * rho2 / delta * theta


def level(degree):
    _, w, k = gll_tables(degree)
    t = w.copy()
    t[0] = t[-1] = w[0] + w[-1]
    s = np.diagonal(k).copy()
    s[0] = s[-1] = k[0, 0] + k[-1, -1]
    c = np.ones(degree + 1)
    c[0] = c[-1] = 0.5
    diag = (
        s[:, None, None] * t[None, :, None] * t[None, None, :]
        + t[:, None, None] * s[None, :, None] * t[None, None, :]
        + t[:, None, None] * t[None, :, None] * s[None, None, :]
    )
    return w, k, t, c, 1.0 / (diag * smoother(degree)[0])


def join_z(count):
    size = EZ * count
    m = np.eye(size)
    for e in range(EZ):
        a, b = e * count + count - 1, ((e + 1) % EZ) * count
        m[a, b] += 1.0
        m[b, a] += 1.0
    return m


def two(m):
    return np.kron(np.eye(2), m)


def lanes(values):
    return np.broadcast_to(values[None, :], (8, LANES))


def rows(values):
    return np.broadcast_to(np.asarray(values)[..., None], np.shape(values) + (LANES,))


def fourier_rows(total):
    k, n = np.meshgrid(np.arange(total), np.arange(total), indexing="ij")
    half = total // 2
    freq = np.where(k <= half, k, k - half)
    angle = 2.0 * np.pi * (freq * n % total) / total
    scale = np.where((k == 0) | (k == half), math.sqrt(1.0 / total), math.sqrt(2.0 / total))
    return scale * np.where(k <= half, np.cos(angle), np.sin(angle))


def sine_rows(mode, point, total):
    product = mode * point % (2 * total)
    inside = (mode > 0) & (mode < total) & (point > 0) & (point < total)
    return np.where(inside, math.sqrt(2.0 / total) * np.sin(np.pi * product / total), 0.0)


def green_table(nx, ny):
    mode = np.arange(MODES)
    wall_gap = 2.0 * np.sin(0.5 * np.pi * mode / ny) ** 2 + np.where(mode % ny == 0, 1.0, 0.0)
    freq = np.arange(EZ)
    freq = np.where(freq <= EZ // 2, freq, freq - EZ // 2)
    span_gap = 2.0 * np.sin(np.pi * freq / EZ) ** 2
    half_gap = wall_gap[:, None] + span_gap[None, :]
    root = np.sqrt(half_gap * (2.0 + half_gap))
    rate = np.log1p(half_gap + root)
    d = np.arange(nx)[:, None, None]
    top = np.exp(-rate * d) + np.exp(-rate * (nx - d))
    return top / (4.0 * root * -np.expm1(-rate * nx))


def modal(values):
    v = values.reshape(values.shape[:-2] + (MODES // 8, 8, EZ))
    v = np.stack([v, v], axis=-2)
    v = np.moveaxis(v, -4, -3)
    return v.reshape(v.shape[:-3] + (LANES,))


def assembled_1d(local_cols, window):
    count = local_cols.shape[0]
    out = np.zeros((count, window))
    out[:, 1:3] += local_cols
    out[0, 0:2] += local_cols[-1]
    out[-1, 2:4] += local_cols[0]
    return out


@functools.lru_cache(None)
def build_tables(nx, ny):
    f, q = ORDER + 1, MID_ORDER + 1
    w7, k7, t7, c7, e7 = level(ORDER)
    w3, k3, t3, c3, e3 = level(MID_ORDER)
    j73 = lagrange_matrix(ORDER, MID_ORDER)
    j31 = lagrange_matrix(MID_ORDER, 1)
    tile = {}
    tk = np.tile(t7, EZ)
    ones = np.ones((8, LANES))
    tile["kx"] = np.stack(
        [np.stack([k7[i, a] * t7[:, None] * tk[None, :] for i in range(f)]) for a in range(f)]
    ).reshape(f * f, 8, LANES)
    roll = np.stack([[k7[j, (j - s) % f] for j in range(f)] for s in range(f)])
    tile["ky"] = roll[:, :, None] * tk[None, None, :]
    tile["e7"] = np.tile(e7, (1, 1, EZ))
    tile["ti"] = np.stack([t * ones for t in t7])
    tile["tij"] = np.stack([t * rows(t7) for t in t7])
    tile["cj"] = rows(c7)[None]
    tile["ci"] = np.stack([c * ones for c in c7])
    tile["jx"] = np.stack([j73[i, a] * ones for i in range(f) for a in range(q)])
    tile["jb"] = np.stack([rows(j73[:, b]) for b in range(q)])
    tile["ji"] = np.stack([j73[i, a] * ones for a in range(q) for i in range(f)])
    green = modal(green_table(nx, ny))
    tile["green"] = green[(np.arange(nx + 3) - 1) % nx]
    point = np.arange(-2, ny + 4)
    tile["sine"] = modal(
        np.broadcast_to(
            sine_rows(np.arange(MODES)[None, :], point[:, None], ny)[:, :, None],
            (len(point), MODES, EZ),
        )
    )
    row = {}
    mid = [(a, b) for a in range(q) for b in range(q)]
    tc = np.tile(np.tile(t3, EZ), 2)

    def left(matrix, scale=None):
        scale = np.ones(LANES) if scale is None else scale
        return matrix.T[:, :, None] * scale[None, None, :]

    row["jy"] = left(
        np.array([[(a == a2) * j73[j, b] for a2 in range(q) for j in range(f)] for a, b in mid])
    )
    row["lx"] = left(np.kron(k3, np.diag(t3)), tc)
    row["ly"] = left(np.kron(np.diag(t3), k3), tc)
    row["e3"] = np.stack([np.tile(np.tile(e3[a, b], EZ), 2) for a, b in mid])[None]
    row["tab"] = rows([t3[a] * t3[b] for a, b in mid])[None]
    row["ca"] = rows([c3[a] for a, b in mid])[None]
    row["cb"] = rows([c3[b] for a, b in mid])[None]
    groups = [np.array([j31[a, x] * j31[b, y] for a, b in mid]) for x in (0, 1) for y in (0, 1)]
    row["jj"] = np.repeat(np.stack(groups, axis=1), MODES, axis=1)[None]
    own = np.zeros((q, 4))
    own[:, 1:3] = j31
    stiff = assembled_1d(k3 @ j31, 4)
    mass = t3[:, None] * own
    row["pj"] = left(np.kron(own, own))
    row["kt"] = left(np.kron(stiff, mass) + np.kron(mass, stiff), tc)
    row["tt"] = left(np.kron(mass, mass))

    mat = {}
    az7 = (join_z(f) @ np.kron(np.eye(EZ), k7)).T
    az3 = two((join_z(q) @ np.kron(np.eye(EZ), k3)).T)
    down = (join_z(q) @ np.kron(np.eye(EZ), j73.T) @ np.diag(np.tile(c7, EZ))).T
    zero = np.zeros_like(down)
    mat["az7"] = az7
    mat["down"] = np.concatenate(
        [np.concatenate([down, zero], axis=1), np.concatenate([zero, down], axis=1)], axis=0
    )
    mat["az3"] = az3
    up = np.kron(np.eye(EZ), j73).T
    mat["up"] = two(up)
    gather = np.zeros((EZ, EZ * q))
    for e in range(EZ):
        for node in (0, 1):
            gather[(e + node) % EZ, e * q : (e + 1) * q] += j31[:, node] * c3
    b1 = two((fourier_rows(EZ) @ gather).T)
    b1 = np.tile(b1, (1, 4))
    mat["b12"] = np.concatenate([b1, az3 @ b1], axis=0)
    spread = np.zeros((EZ * q, EZ))
    for e in range(EZ):
        for node in (0, 1):
            spread[e * q : (e + 1) * q, (e + node) % EZ] += j31[:, node]
    back = two((spread @ fourier_rows(EZ).T).T)
    back = np.tile(back, (4, 1))
    mat["back"] = np.concatenate([back, back @ az3], axis=1)
    mode, here = np.arange(MODES)[:, None], np.arange(32)[None, :]
    s0 = np.where(here < ny, sine_rows(mode, here, ny), 0.0)
    s1 = np.where(here < ny, sine_rows(mode, here + 1, ny), 0.0)
    mat["sin"] = np.concatenate([s0, s1], axis=0)
    packed, where = [], {}
    at = 0
    for name, value in tile.items():
        where[name] = (at, value.shape[0])
        packed.append(value)
        at += value.shape[0]
    tiles = np.concatenate(packed).astype(np.float32)
    packed, at = [], 0
    for name, value in row.items():
        where[name] = (at, value.shape[0])
        packed.append(value)
        at += value.shape[0]
    row16 = np.concatenate(packed).astype(np.float32)
    mats = {name: value.astype(np.float32) for name, value in mat.items()}
    return tiles, row16, mats, where


MATS = ("az7", "down", "az3", "up", "b12", "back", "sin")
N_LINKS = 8 + 4 + 4 + 4 + 4 + 8 + 4 + 4 + 4


def kernel(nx, ny, where, x_ref, tile_ref, row_ref, *rest):
    mat = dict(zip(MATS, rest[: len(MATS)]))
    (out_ref, fine_send, fine_recv, mid_send, mid_recv, line_send, line_recv, mode_send, mode_recv,
     send_sem, recv_sem, line_ss, line_rs, mode_ss, mode_rs) = rest[len(MATS) :]
    sx, cx = lax.axis_index("stream"), lax.axis_index("cross")

    def at(dx, dy):
        return {"stream": lax.rem(sx + (nx + dx), nx), "cross": lax.rem(cx + (ny + dy), ny)}

    def tab(name):
        start, size = where[name]
        return tile_ref[start : start + size]

    def rtab(name):
        start, size = where[name]
        return row_ref[start : start + size]

    bar = pltpu.get_barrier_semaphore()
    corners = ((1, 1), (1, -1), (-1, 1), (-1, -1))
    faces = ((1, 0), (-1, 0), (0, 1), (0, -1))
    for d in corners:
        pl.semaphore_signal(bar, inc=1, device_id=at(*d), device_id_type=MESH_ID)

    def greet_stream(d, carry):
        pl.semaphore_signal(bar, inc=1, device_id={"stream": lax.rem(sx + d, nx)},
                            device_id_type=MESH_ID)
        return carry

    def greet_cross(d, carry):
        pl.semaphore_signal(bar, inc=1, device_id={"cross": lax.rem(cx + d, ny)},
                            device_id_type=MESH_ID)
        return carry

    lax.fori_loop(1, nx, greet_stream, 0)
    lax.fori_loop(1, ny, greet_cross, 0)

    links = [0]
    sent = []

    def start(src, dst, to):
        n = links[0]
        links[0] += 1
        copy = pltpu.make_async_remote_copy(
            src, dst, send_sem.at[n], recv_sem.at[n], device_id=at(*to), device_id_type=MESH_ID)
        copy.start()
        sent.append(copy)
        return copy

    jrow = lax.broadcasted_iota(jnp.int32, (8, LANES), 0)
    lane = lax.broadcasted_iota(jnp.int32, (8, LANES), 1)
    low_wall = jnp.where(cx == 0, 0, -1)
    high_wall = jnp.where(cx == ny - 1, ORDER, -1)
    keep7 = jnp.where((jrow == low_wall) | (jrow == high_wall), 0.0, 1.0)
    mrow = lax.broadcasted_iota(jnp.int32, (16, LANES), 0)
    brow = lax.rem(mrow, 4)
    high_wall3 = jnp.where(cx == ny - 1, MID_ORDER, -1)
    keep3 = jnp.where((brow == low_wall) | (brow == high_wall3), 0.0, 1.0)
    e7 = tab("e7") * keep7[None]
    e3 = rtab("e3")[0] * keep3
    _, keep_f, gain_f = smoother(ORDER)
    _, keep_m, gain_m = smoother(MID_ORDER)

    def dot(a, b):
        return jnp.dot(a, b, preferred_element_type=jnp.float32, precision=EXACT)

    def fine_xy(u):
        kx = tab("kx").reshape(8, 8, 8, LANES)
        ax = kx[0][None] * u[:, 0:1]
        for a in range(1, 8):
            ax = ax + kx[a][None] * u[:, a : a + 1]
        ky = tab("ky")
        flat = u.reshape(16, 8, LANES)
        ay = ky[0][None] * flat
        for s in range(1, 8):
            ay = ay + ky[s][None] * pltpu.roll(flat, s, 1)
        return ax, ay.reshape(2, 8, 8, LANES) * tab("ti")[None]

    def fine_z(u):
        az = dot(u.reshape(128, LANES), mat["az7"][...])
        return az.reshape(2, 8, 8, LANES) * tab("tij")[None]

    def fine_send_faces(n, ax, ay):
        fine_send[n, 0] = ax[:, 7].reshape(16, LANES)
        fine_send[n, 1] = ax[:, 0].reshape(16, LANES)
        flat = ay.reshape(16, 8, LANES)
        fine_send[n, 2] = flat[:, 7, :]
        fine_send[n, 3] = flat[:, 0, :]
        return [start(fine_send.at[n, d], fine_recv.at[n, d], faces[d]) for d in range(4)]

    def add_x(field, low, high):
        return jnp.concatenate(
            [field[:, 0:1] + low.reshape(2, 1, 8, LANES), field[:, 1:7],
             field[:, 7:8] + high.reshape(2, 1, 8, LANES)], axis=1)

    def add_y(field, low, high):
        flat = field.reshape(16, 8, LANES)
        flat = flat + jnp.where(jrow[None] == 0, low[:, None, :], 0.0)
        flat = flat + jnp.where(jrow[None] == 7, high[:, None, :], 0.0)
        return flat.reshape(2, 8, 8, LANES)

    def fine_join(n, copies, field):
        for copy in copies:
            copy.wait_recv()
        field = add_x(field, fine_recv[n, 0], fine_recv[n, 1])
        return add_y(field, fine_recv[n, 2], fine_recv[n, 3])

    def left(name, v):
        start_row, size = where[name]
        acc = row_ref[start_row] * v[0:1]
        for c in range(1, size):
            acc = acc + row_ref[start_row + c] * v[c : c + 1]
        return acc

    def mid_start(n, ax, ay):
        mid_send[n, 0] = ax
        mid_send[n, 1] = ay
        return [start(mid_send.at[n, d // 2], mid_recv.at[n, d], faces[d]) for d in range(4)]

    def shifted(v, shift, mask):
        return jnp.where(mask, pltpu.roll(v, shift, 0), 0.0)

    def mid_join(n, copies, field):
        for copy in copies:
            copy.wait_recv()
        field = field + shifted(mid_recv[n, 0], 4, mrow < 4)
        field = field + shifted(mid_recv[n, 1], 12, mrow >= 12)
        field = field + shifted(mid_recv[n, 2], 13, brow == 0)
        return field + shifted(mid_recv[n, 3], 3, brow == 3)

    src = x_ref[...].reshape(16, 8, LANES)
    knode = lax.rem(lane, 8)
    src = (src + jnp.where(knode[None] == 7, pltpu.roll(src, LANES - 1, 2), 0.0)
           + jnp.where(knode[None] == 0, pltpu.roll(src, 1, 2), 0.0))
    fine_send[0, 2] = src[:, 7, :]
    fine_send[0, 3] = src[:, 0, :]
    src = src.reshape(2, 8, 8, LANES)
    fine_send[0, 0] = src[:, 7].reshape(16, LANES)
    fine_send[0, 1] = src[:, 0].reshape(16, LANES)
    pl.semaphore_wait(bar, 4 + nx - 1 + ny - 1)
    copies = [start(fine_send.at[0, 2 if d[1] > 0 else 3], fine_recv.at[5, n], d)
              for n, d in enumerate(corners)]
    copies += [start(fine_send.at[0, d], fine_recv.at[0, d], faces[d]) for d in range(4)]
    for copy in copies:
        copy.wait_recv()
    irow = jrow[None]

    def end(n, shift, row):
        line = fine_recv[5, n].reshape(2, 8, LANES)
        return jnp.where(irow == row, pltpu.roll(line, shift, 1), 0.0).reshape(16, LANES)

    low = fine_recv[0, 2] + end(0, 1, 0) + end(2, 7, 7)
    high = fine_recv[0, 3] + end(1, 1, 0) + end(3, 7, 7)
    b7 = add_y(add_x(src, fine_recv[0, 0], fine_recv[0, 1]), low, high)

    u1 = e7[None] * b7
    ax, ay = fine_xy(u1)
    copies = fine_send_faces(1, ax, ay)
    az = fine_z(u1)
    r1 = b7 - fine_join(1, copies, ax + ay + az)
    x7 = (1.0 + keep_f) * u1 + gain_f * (e7[None] * r1)
    ax, ay = fine_xy(x7)
    side7 = fine_send_faces(2, ax, ay)
    az = fine_z(x7)
    local7 = ax + ay + az
    ci = tab("ci")[None]
    rest7 = (src - tab("cj")[None] * (ax + ci * az) - ci * ay) * keep7[None, None]
    jx = tab("jx").reshape(8, 4, 8, LANES)
    g = jx[0][None] * rest7[:, 0:1]
    for i in range(1, 8):
        g = g + jx[i][None] * rest7[:, i : i + 1]
    g = jnp.concatenate([g[0].reshape(32, LANES), g[1].reshape(32, LANES)], axis=1)
    g3 = left("jy", dot(g, mat["down"][...]))
    mid_send[3, 0] = g3
    around = faces + corners
    copies = [start(mid_send.at[3, 0], mid_recv.at[3 + n // 4, n % 4], d)
              for n, d in enumerate(around)]
    rest7 = b7 - fine_join(2, side7, local7)
    for copy in copies:
        copy.wait_recv()
    shifts = ((4, mrow < 4), (12, mrow >= 12), (13, brow == 0), (3, brow == 3),
              (1, mrow == 0), (7, mrow == 3), (9, mrow == 12), (15, mrow == 15))
    b3 = g3
    for n, (shift, mask) in enumerate(shifts):
        b3 = b3 + shifted(mid_recv[3 + n // 4, n % 4], shift, mask)

    tab3 = rtab("tab")[0]

    def mid_z(v):
        return tab3 * dot(v, mat["az3"][...])

    v1 = e3 * b3
    ax, ay = left("lx", v1), left("ly", v1)
    copies = mid_start(0, ax, ay)
    az = mid_z(v1)
    r1 = b3 - mid_join(0, copies, ax + ay + az)
    x3 = (1.0 + keep_m) * v1 + gain_m * (e3 * r1)
    ax, ay = left("lx", x3), left("ly", x3)
    ca, cb = rtab("ca")[0], rtab("cb")[0]
    part = keep3 * (g3 - cb * ax - ca * ay)
    other = keep3 * (ca * cb * tab3) * x3
    line = dot(jnp.concatenate([part, -other], axis=1), mat["b12"][...])
    line = jnp.sum(rtab("jj")[0] * line, axis=0, keepdims=True)
    line_send[0] = line

    def line_copy(d, slot, to):
        return pltpu.make_async_remote_copy(
            line_send.at[0], line_recv.at[slot], line_ss.at[d], line_rs.at[d],
            device_id={"cross": to}, device_id_type=MESH_ID)

    def line_out(d, carry):
        line_copy(d, cx, lax.rem(cx + d, ny)).start()
        return carry

    lax.fori_loop(1, ny, line_out, 0)
    line_recv[cx] = line
    side3 = mid_start(1, ax, ay)
    if ny < 32:
        line_recv[ny:] = jnp.zeros((32 - ny, 1, LANES), jnp.float32)
    rest3 = b3 - mid_join(1, side3, ax + ay + mid_z(x3))

    def line_in(d, carry):
        line_copy(d, lax.rem(cx + ny - d, ny), cx).wait()
        return carry

    lax.fori_loop(1, ny, line_in, 0)
    spectrum = dot(mat["sin"][...], line_recv[:, 0, :])
    group = lax.div(lane, 32)
    for alpha in range(2):
        total = jnp.zeros((8, LANES), jnp.float32)
        for hi in range(4):
            for beta in range(2):
                piece = spectrum[(beta * 4 + hi) * 8 : (beta * 4 + hi + 1) * 8]
                shift = 32 * (hi - 2 * alpha - beta) % LANES
                if shift:
                    piece = pltpu.roll(piece, shift, 1)
                total = total + jnp.where(group == hi, piece, 0.0)
        mode_send[alpha] = total

    def mode_copy(d, to):
        return pltpu.make_async_remote_copy(
            mode_send, mode_recv.at[d], mode_ss.at[d], mode_rs.at[d],
            device_id={"stream": to}, device_id_type=MESH_ID)

    def mode_out(d, carry):
        mode_copy(d, lax.rem(sx + d, nx)).start()
        return carry

    def mode_in(d, carry):
        mode_copy(d, sx).wait()
        return carry

    lax.fori_loop(1, nx, mode_out, 0)
    mode_recv[0] = mode_send[...]
    lax.fori_loop(1, nx, mode_in, 0)
    first = mode_recv[:, 0]
    second = mode_recv[:, 1]
    nodes = first + jnp.concatenate([second[1:], second[:1]], axis=0)
    start_g = where["green"][0]
    solved = [jnp.sum(tile_ref[start_g + n : start_g + n + nx] * nodes, axis=0) for n in range(4)]
    sine = tile_ref[pl.ds(where["sine"][0] + cx + 1, 4)]
    window = [jnp.sum(sine * s[None], axis=1) for s in solved]
    window = jnp.concatenate(window, axis=0)
    window = dot(window, mat["back"][...])
    zval, zstiff = window[:, :LANES], window[:, LANES:]

    x3 = x3 + left("pj", zval)
    r0 = rest3 - left("kt", zval) - left("tt", zstiff)
    w1 = e3 * r0
    ax, ay = left("lx", w1), left("ly", w1)
    copies = mid_start(2, ax, ay)
    r1 = r0 - mid_join(2, copies, ax + ay + mid_z(w1))
    x3 = x3 + (1.0 + keep_m) * w1 + gain_m * (e3 * r1)

    jb, ji = tab("jb"), tab("ji").reshape(4, 8, 8, LANES)
    halves = dot(x3, mat["up"][...])
    parts = []
    for r in range(2):
        half = halves[:, r * LANES : (r + 1) * LANES]
        cols = []
        for a in range(4):
            acc = jb[0] * half[4 * a : 4 * a + 1]
            for b in range(1, 4):
                acc = acc + jb[b] * half[4 * a + b : 4 * a + b + 1]
            cols.append(acc)
        acc = ji[0] * cols[0][None]
        for a in range(1, 4):
            acc = acc + ji[a] * cols[a][None]
        parts.append(acc)
    px = jnp.stack(parts, axis=0)
    ax, ay = fine_xy(px)
    copies = fine_send_faces(3, ax, ay)
    r0 = rest7 - fine_join(3, copies, ax + ay + fine_z(px))
    u1 = e7[None] * r0
    ax, ay = fine_xy(u1)
    copies = fine_send_faces(4, ax, ay)
    r1 = r0 - fine_join(4, copies, ax + ay + fine_z(u1))
    out = x7 + px + (1.0 + keep_f) * u1 + gain_f * (e7[None] * r1)
    out_ref[...] = out.reshape(128, LANES)
    for copy in sent:
        copy.wait_send()


def solution(mesh):
    nx, ny = mesh.shape["stream"], mesh.shape["cross"]
    tiles, row16, mats, where = build_tables(nx, ny)
    vmem = pl.BlockSpec(memory_space=pltpu.VMEM)

    def body(sources):
        flat = sources.reshape(128, LANES)
        operands = [flat, jnp.asarray(tiles), jnp.asarray(row16)]
        operands += [jnp.asarray(mats[name]) for name in MATS]
        out = pl.pallas_call(
            functools.partial(kernel, nx, ny, where),
            out_shape=jax.ShapeDtypeStruct((128, LANES), jnp.float32),
            in_specs=[vmem] * len(operands),
            out_specs=vmem,
            scratch_shapes=[
                pltpu.VMEM((5, 4, 16, LANES), jnp.float32),
                pltpu.VMEM((6, 4, 16, LANES), jnp.float32),
                pltpu.VMEM((4, 2, 16, LANES), jnp.float32),
                pltpu.VMEM((5, 4, 16, LANES), jnp.float32),
                pltpu.VMEM((1, 1, LANES), jnp.float32),
                pltpu.VMEM((32, 1, LANES), jnp.float32),
                pltpu.VMEM((2, 8, LANES), jnp.float32),
                pltpu.VMEM((nx, 2, 8, LANES), jnp.float32),
                pltpu.SemaphoreType.DMA((N_LINKS,)),
                pltpu.SemaphoreType.DMA((N_LINKS,)),
                pltpu.SemaphoreType.DMA((ny,)),
                pltpu.SemaphoreType.DMA((ny,)),
                pltpu.SemaphoreType.DMA((nx,)),
                pltpu.SemaphoreType.DMA((nx,)),
            ],
            compiler_params=pltpu.CompilerParams(
                collective_id=0, has_side_effects=True, vmem_limit_bytes=32 * 1024 * 1024),
            name="vcycle",
        )(*operands)
        return out.reshape(sources.shape)

    spec = P(None, "stream", "cross", None, None, None)
    return jax.shard_map(body, mesh=mesh, in_specs=(spec,), out_specs=spec, check_vma=False)
```

time: 599 us -> 87.7 us (0.15)
  the two profiles are of different devices: /device:TPU:128 before, /device:TPU:1 now
where the time goes in v1:
time: 87.7 us; the launch traced here: 86.3 us
  Pallas kernels  76.3 us (87%)
  local copies, waits for them, and re-layouts  9.92 us (11%)
    pallas_call x1, Pallas kernels, body(): pl.pallas_call(functools.partial(kernel, nx, ny, where), out_shape=jax.Sh...  76.3 us
    unnamed x21, local copies, waits for them, and re-layouts  9.92 us

profile of v1, /device:TPU:1, one launch (start us, length us, event | category | flops | bytes accessed | tf_op | source)
XLA Modules:
  0.0 86.3 jit_solution(2625426195661012358)
XLA Ops:
  0.0 0.0 copy-start
  0.0 1.2 %copy-done = f32[246,8,128]{2,1,0:T(8,128)S(1)} copy-done((f32[246,8,128]{2,1,0:T(8,128)S(1)}, f32[246,8,128]{2,1,0:T(8,128)}, u32[]{:S(2)}) %copy-start) | copy-done | bytes 1007640
  1.2 0.0 copy-start.1
  1.2 1.2 %copy-done.1 = f32[117,16,128]{2,1,0:T(8,128)S(1)} copy-done((f32[117,16,128]{2,1,0:T(8,128)S(1)}, f32[117,16,128]{2,1,0:T(8,128)}, u32[]{:S(2)}) %copy-start.1) | copy-done | bytes 958488
  2.4 0.0 copy-start.2
  2.4 0.9 %copy-done.2 = f32[128,256]{1,0:T(8,128)S(1)} copy-done((f32[128,256]{1,0:T(8,128)S(1)}, f32[128,256]{1,0:T(8,128)}, u32[]{:S(2)}) %copy-start.2) | copy-done | bytes 131096
  3.3 0.0 copy-start.3
  3.3 0.9 %copy-done.3 = f32[256,128]{1,0:T(8,128)S(1)} copy-done((f32[256,128]{1,0:T(8,128)S(1)}, f32[256,128]{1,0:T(8,128)}, u32[]{:S(2)}) %copy-start.3) | copy-done | bytes 131096
  4.2 0.0 copy-start.4
  4.2 0.9 %copy-done.4 = f32[128,256]{1,0:T(8,128)S(1)} copy-done((f32[128,256]{1,0:T(8,128)S(1)}, f32[128,256]{1,0:T(8,128)}, u32[]{:S(2)}) %copy-start.4) | copy-done | bytes 131096
  5.1 0.0 copy-start.5
  5.1 0.9 %copy-done.5 = f32[256,128]{1,0:T(8,128)S(1)} copy-done((f32[256,128]{1,0:T(8,128)S(1)}, f32[256,128]{1,0:T(8,128)}, u32[]{:S(2)}) %copy-start.5) | copy-done | bytes 131096
  6.0 0.0 copy-start.6
  6.0 0.8 copy-done.6
  6.9 0.0 copy-start.7
  6.9 0.8 copy-done.7
  7.7 0.0 copy-start.8
  7.7 0.8 copy-done.8
  8.5 0.0 copy-start.9
  8.5 0.8 copy-done.9
  9.3 76.3 %vcycle.1 = f32[128,128]{1,0:T(8,128)S(1)} custom-call(f32[128,128]{1,0:T(8,128)S(1)} %bitcast.5, f32[246,8,128]{2,1,0:T(8,128)S(1)} %copy-done, f32[117,16,128]{2,1,0:T(8,128)S(1)} %copy-done.1, f32[128,128]{1,0:T(8,128)S(1)} %copy-done.8, f32[256,128]{1,0:T(8,128)S(1)} %copy-done.5, f32[128,128]{1,0:T(8,128)S(1)} %copy-done.7, f32[128,256]{1,0:T(8,128)S(1)} %copy-done.4, ...), custom_call_target="tpu_custom_call" | custom-call | tf_op jit(solution)/shard_map/vcycle/pallas_call | solution.py:599
  85.6 0.6 copy.13
Async XLA Ops:
  0.0 1.2 %copy-start = (f32[246,8,128]{2,1,0:T(8,128)S(1)}, f32[246,8,128]{2,1,0:T(8,128)}, u32[]{:S(2)}) copy-start(f32[246,8,128]{2,1,0:T(8,128)} %constant.18.clone.tile_ref) | copy-start | bytes 3022852
  1.2 1.2 %copy-start.1 = (f32[117,16,128]{2,1,0:T(8,128)S(1)}, f32[117,16,128]{2,1,0:T(8,128)}, u32[]{:S(2)}) copy-start(f32[117,16,128]{2,1,0:T(8,128)} %constant.19.clone.row_ref) | copy-start | bytes 2875396
  2.4 0.9 %copy-start.2 = (f32[128,256]{1,0:T(8,128)S(1)}, f32[128,256]{1,0:T(8,128)}, u32[]{:S(2)}) copy-start(f32[128,256]{1,0:T(8,128)} %constant.25.clone.rest_5_) | copy-start | bytes 393220
  3.3 0.9 %copy-start.3 = (f32[256,128]{1,0:T(8,128)S(1)}, f32[256,128]{1,0:T(8,128)}, u32[]{:S(2)}) copy-start(f32[256,128]{1,0:T(8,128)} %constant.24.clone.rest_4_) | copy-start | bytes 393220
  4.2 0.9 %copy-start.4 = (f32[128,256]{1,0:T(8,128)S(1)}, f32[128,256]{1,0:T(8,128)}, u32[]{:S(2)}) copy-start(f32[128,256]{1,0:T(8,128)} %constant.23.clone.rest_3_) | copy-start | bytes 393220
  5.1 0.9 %copy-start.5 = (f32[256,128]{1,0:T(8,128)S(1)}, f32[256,128]{1,0:T(8,128)}, u32[]{:S(2)}) copy-start(f32[256,128]{1,0:T(8,128)} %constant.21.clone.rest_1_) | copy-start | bytes 393220
  6.0 0.8 copy-start.6
  6.9 0.8 copy-start.7
  7.7 0.8 copy-start.8
  8.5 0.8 copy-start.9

commit v2 on v1

--- a/solution.py
+++ b/solution.py
@@ -285,11 +285,24 @@
 N_LINKS = 8 + 4 + 4 + 4 + 4 + 8 + 4 + 4 + 4
 
 
-def kernel(nx, ny, where, x_ref, tile_ref, row_ref, *rest):
-    mat = dict(zip(MATS, rest[: len(MATS)]))
-    (out_ref, fine_send, fine_recv, mid_send, mid_recv, line_send, line_recv, mode_send, mode_recv,
-     send_sem, recv_sem, line_ss, line_rs, mode_ss, mode_rs) = rest[len(MATS) :]
+def reach(n):
+    base = max(n // 8, 1)
+    known, hops = base, []
+    while known < n // 2:
+        hops.append(known)
+        known *= 2
+    return range(1, base + 1), hops
+
+
+def kernel(nx, ny, where, *refs):
+    names = ("x", "tiles", "rows") + MATS
+    count = len(names)
+    hbm, out_ref, vmem = refs[:count], refs[count], refs[count + 1 : 2 * count + 1]
+    (fine_send, fine_recv, mid_send, mid_recv, line_send, line_recv, mode_send, mode_recv,
+     load_sem, send_sem, recv_sem, line_ss, line_rs, mode_ss, mode_rs, known) = refs[2 * count + 1 :]
     sx, cx = lax.axis_index("stream"), lax.axis_index("cross")
+    tile_ref, row_ref = vmem[1], vmem[2]
+    mat = dict(zip(MATS, vmem[3:]))
 
     def at(dx, dy):
         return {"stream": lax.rem(sx + (nx + dx), nx), "cross": lax.rem(cx + (ny + dy), ny)}
@@ -305,21 +318,35 @@
     bar = pltpu.get_barrier_semaphore()
     corners = ((1, 1), (1, -1), (-1, 1), (-1, -1))
     faces = ((1, 0), (-1, 0), (0, 1), (0, -1))
-    for d in corners:
+    near_x, hops_x = reach(nx)
+    near_y, hops_y = reach(ny)
+    near = [(s * d, 0) for d in near_x for s in (1, -1)]
+    near += [(0, s * d) for d in near_y for s in (1, -1)]
+    near += corners
+    for d in near:
         pl.semaphore_signal(bar, inc=1, device_id=at(*d), device_id_type=MESH_ID)
-
-    def greet_stream(d, carry):
-        pl.semaphore_signal(bar, inc=1, device_id={"stream": lax.rem(sx + d, nx)},
-                            device_id_type=MESH_ID)
-        return carry
-
-    def greet_cross(d, carry):
-        pl.semaphore_signal(bar, inc=1, device_id={"cross": lax.rem(cx + d, ny)},
-                            device_id_type=MESH_ID)
-        return carry
-
-    lax.fori_loop(1, nx, greet_stream, 0)
-    lax.fori_loop(1, ny, greet_cross, 0)
+    loads = {}
+    for n, name in enumerate(names):
+        loads[name] = pltpu.make_async_copy(hbm[n], vmem[n], load_sem.at[n])
+        loads[name].start()
+
+    def need(*wanted):
+        for name in wanted:
+            if name in loads:
+                loads.pop(name).wait()
+
+    def tell(step):
+        for n, hops in enumerate((hops_x, hops_y)):
+            if step < len(hops):
+                for s in (1, -1):
+                    d = (s * hops[step], 0) if n == 0 else (0, s * hops[step])
+                    pl.semaphore_signal(
+                        known.at[step, n], inc=1, device_id=at(*d), device_id_type=MESH_ID)
+
+    def told(step):
+        for n, hops in enumerate((hops_x, hops_y)):
+            if step < len(hops):
+                pl.semaphore_wait(known.at[step, n], 2)
 
     links = [0]
     sent = []
@@ -342,8 +369,6 @@
     brow = lax.rem(mrow, 4)
     high_wall3 = jnp.where(cx == ny - 1, MID_ORDER, -1)
     keep3 = jnp.where((brow == low_wall) | (brow == high_wall3), 0.0, 1.0)
-    e7 = tab("e7") * keep7[None]
-    e3 = rtab("e3")[0] * keep3
     _, keep_f, gain_f = smoother(ORDER)
     _, keep_m, gain_m = smoother(MID_ORDER)
 
@@ -414,7 +439,8 @@
         field = field + shifted(mid_recv[n, 2], 13, brow == 0)
         return field + shifted(mid_recv[n, 3], 3, brow == 3)
 
-    src = x_ref[...].reshape(16, 8, LANES)
+    need("x")
+    src = vmem[0][...].reshape(16, 8, LANES)
     knode = lax.rem(lane, 8)
     src = (src + jnp.where(knode[None] == 7, pltpu.roll(src, LANES - 1, 2), 0.0)
            + jnp.where(knode[None] == 0, pltpu.roll(src, 1, 2), 0.0))
@@ -423,12 +449,17 @@
     src = src.reshape(2, 8, 8, LANES)
     fine_send[0, 0] = src[:, 7].reshape(16, LANES)
     fine_send[0, 1] = src[:, 0].reshape(16, LANES)
-    pl.semaphore_wait(bar, 4 + nx - 1 + ny - 1)
+    pl.semaphore_wait(bar, len(near))
+    tell(0)
     copies = [start(fine_send.at[0, 2 if d[1] > 0 else 3], fine_recv.at[5, n], d)
               for n, d in enumerate(corners)]
     copies += [start(fine_send.at[0, d], fine_recv.at[0, d], faces[d]) for d in range(4)]
+    need("tiles", "az7")
+    e7 = tab("e7") * keep7[None]
     for copy in copies:
         copy.wait_recv()
+    told(0)
+    tell(1)
     irow = jrow[None]
 
     def end(n, shift, row):
@@ -451,6 +482,7 @@
     local7 = ax + ay + az
     ci = tab("ci")[None]
     rest7 = (src - tab("cj")[None] * (ax + ci * az) - ci * ay) * keep7[None, None]
+    need("rows", "down")
     jx = tab("jx").reshape(8, 4, 8, LANES)
     g = jx[0][None] * rest7[:, 0:1]
     for i in range(1, 8):
@@ -470,6 +502,9 @@
     for n, (shift, mask) in enumerate(shifts):
         b3 = b3 + shifted(mid_recv[3 + n // 4, n % 4], shift, mask)
 
+    need("az3", "b12", "sin", "back", "up")
+    told(1)
+    e3 = rtab("e3")[0] * keep3
     tab3 = rtab("tab")[0]
 
     def mid_z(v):
@@ -590,35 +625,37 @@
 def solution(mesh):
     nx, ny = mesh.shape["stream"], mesh.shape["cross"]
     tiles, row16, mats, where = build_tables(nx, ny)
-    vmem = pl.BlockSpec(memory_space=pltpu.VMEM)
 
     def body(sources):
         flat = sources.reshape(128, LANES)
         operands = [flat, jnp.asarray(tiles), jnp.asarray(row16)]
         operands += [jnp.asarray(mats[name]) for name in MATS]
+        links, f32 = pltpu.SemaphoreType.DMA, jnp.float32
         out = pl.pallas_call(
             functools.partial(kernel, nx, ny, where),
             out_shape=jax.ShapeDtypeStruct((128, LANES), jnp.float32),
-            in_specs=[vmem] * len(operands),
-            out_specs=vmem,
-            scratch_shapes=[
-                pltpu.VMEM((5, 4, 16, LANES), jnp.float32),
-                pltpu.VMEM((6, 4, 16, LANES), jnp.float32),
-                pltpu.VMEM((4, 2, 16, LANES), jnp.float32),
-                pltpu.VMEM((5, 4, 16, LANES), jnp.float32),
-                pltpu.VMEM((1, 1, LANES), jnp.float32),
-                pltpu.VMEM((32, 1, LANES), jnp.float32),
-                pltpu.VMEM((2, 8, LANES), jnp.float32),
-                pltpu.VMEM((nx, 2, 8, LANES), jnp.float32),
-                pltpu.SemaphoreType.DMA((N_LINKS,)),
-                pltpu.SemaphoreType.DMA((N_LINKS,)),
-                pltpu.SemaphoreType.DMA((ny,)),
-                pltpu.SemaphoreType.DMA((ny,)),
-                pltpu.SemaphoreType.DMA((nx,)),
-                pltpu.SemaphoreType.DMA((nx,)),
+            in_specs=[pl.BlockSpec(memory_space=pl.ANY)] * len(operands),
+            out_specs=pl.BlockSpec(memory_space=pltpu.VMEM),
+            scratch_shapes=[pltpu.VMEM(o.shape, f32) for o in operands]
+            + [
+                pltpu.VMEM((5, 4, 16, LANES), f32),
+                pltpu.VMEM((6, 4, 16, LANES), f32),
+                pltpu.VMEM((4, 2, 16, LANES), f32),
+                pltpu.VMEM((5, 4, 16, LANES), f32),
+                pltpu.VMEM((1, 1, LANES), f32),
+                pltpu.VMEM((32, 1, LANES), f32),
+                pltpu.VMEM((2, 8, LANES), f32),
+                pltpu.VMEM((nx, 2, 8, LANES), f32),
+                links((len(operands),)),
+                links((N_LINKS,)),
+                links((N_LINKS,)),
+                links((ny,)),
+                links((ny,)),
+                links((nx,)),
+                links((nx,)),
+                pltpu.SemaphoreType.REGULAR((2, 2)),
             ],
-            compiler_params=pltpu.CompilerParams(
-                collective_id=0, has_side_effects=True, vmem_limit_bytes=32 * 1024 * 1024),
+            compiler_params=pltpu.CompilerParams(collective_id=0, has_side_effects=True),
             name="vcycle",
         )(*operands)
         return out.reshape(sources.shape)

time: 87.7 us -> 75 us (0.86)
  local copies, waits for them, and re-layouts: 9.92 us -> 1.47 us
  Pallas kernels: 76.3 us -> 72.5 us
    unnamed x21 -> x1, local copies, waits for them, and re-layouts: 9.92 us -> 1.47 us
    pallas_call x1, Pallas kernels: 76.3 us -> 72.5 us  [body(): pl.pallas_call(functools.partial(kernel, nx, ny, where), out_shape=jax.Sh...]
where the time goes in v2:
time: 75 us; the launch traced here: 74 us
  Pallas kernels  72.5 us (97%)
  local copies, waits for them, and re-layouts  1.47 us (2%)
    pallas_call x1, Pallas kernels, body(): pl.pallas_call(functools.partial(kernel, nx, ny, where), out_shape=jax.Sh...  72.5 us

profile of v2, /device:TPU:1, one launch (start us, length us, event | category | flops | bytes accessed | tf_op | source)
XLA Modules:
  0.0 74.0 jit_solution(12935870293280926794)
XLA Ops:
  0.0 72.5 %vcycle.1 = f32[128,128]{1,0:T(8,128)} custom-call(f32[128,128]{1,0:T(8,128)} %bitcast.5, f32[246,8,128]{2,1,0:T(8,128)} %constant.18.clone.refs_1_, f32[117,16,128]{2,1,0:T(8,128)} %constant.19.clone.refs_2_, f32[128,128]{1,0:T(8,128)} %constant.20.clone.refs_3_, f32[256,128]{1,0:T(8,128)} %constant.21.clone.refs_4_, f32[128,128]{1,0:T(8,128)} %constant.22.clone.refs_5_, ...), custom_call_target="tpu_custom_call" | custom-call | tf_op jit(solution)/shard_map/vcycle/pallas_call | solution.py:634
  72.5 1.5 %copy.13 = f32[2,1,1,8,8,128]{5,4,3,2,1,0:T(8,128)} copy(f32[2,1,1,8,8,128]{5,4,3,2,1,0:T(8,128)} %bitcast.4) | data formatting | bytes 131072

commit v3 on v2

--- a/solution.py
+++ b/solution.py
@@ -16,6 +16,8 @@
 MODES = 32
 EXACT = lax.Precision.HIGHEST
 MESH_ID = pl.DeviceIdType.MESH
+FACES = ((1, 0), (-1, 0), (0, 1), (0, -1))
+WIDE, SPAN, PAD = 4, 10, 16
 
 
 def legendre_pair(degree, points):
@@ -166,6 +168,18 @@
     return v.reshape(v.shape[:-3] + (LANES,))
 
 
+def offsets(radius):
+    found = [(0, 0), *FACES]
+    for ring in range(2, radius + 1):
+        found += [
+            (dx, dy)
+            for dx in range(-ring, ring + 1)
+            for dy in range(-ring, ring + 1)
+            if abs(dx) + abs(dy) == ring
+        ]
+    return found
+
+
 def assembled_1d(local_cols, window):
     count = local_cols.shape[0]
     out = np.zeros((count, window))
@@ -190,17 +204,17 @@
     ).reshape(f * f, 8, LANES)
     roll = np.stack([[k7[j, (j - s) % f] for j in range(f)] for s in range(f)])
     tile["ky"] = roll[:, :, None] * tk[None, None, :]
+    tile["kyl"] = (k7[f - 1][:, None] * tk[None, :])[None]
+    tile["kyf"] = (k7[0][:, None] * tk[None, :])[None]
     tile["e7"] = np.tile(e7, (1, 1, EZ))
     tile["ti"] = np.stack([t * ones for t in t7])
     tile["tij"] = np.stack([t * rows(t7) for t in t7])
     tile["cj"] = rows(c7)[None]
     tile["ci"] = np.stack([c * ones for c in c7])
     tile["jx"] = np.stack([j73[i, a] * ones for i in range(f) for a in range(q)])
-    tile["jb"] = np.stack([rows(j73[:, b]) for b in range(q)])
-    tile["ji"] = np.stack([j73[i, a] * ones for a in range(q) for i in range(f)])
     green = modal(green_table(nx, ny))
-    tile["green"] = green[(np.arange(nx + 3) - 1) % nx]
-    point = np.arange(-2, ny + 4)
+    tile["green"] = green[(np.arange(nx + SPAN - 1) - WIDE) % nx]
+    point = np.arange(-WIDE, ny - WIDE + PAD)
     tile["sine"] = modal(
         np.broadcast_to(
             sine_rows(np.arange(MODES)[None, :], point[:, None], ny)[:, :, None],
@@ -230,11 +244,60 @@
     own[:, 1:3] = j31
     stiff = assembled_1d(k3 @ j31, 4)
     mass = t3[:, None] * own
-    row["pj"] = left(np.kron(own, own))
-    row["kt"] = left(np.kron(stiff, mass) + np.kron(mass, stiff), tc)
-    row["tt"] = left(np.kron(mass, mass))
+
+    ring1, ring2, ring3 = offsets(1), offsets(2), offsets(3)
+
+    def placed(first, second, elements):
+        out = np.zeros((len(elements), q, q, SPAN, PAD))
+        for n, (dx, dy) in enumerate(elements):
+            x0, y0 = dx - 1 + WIDE, dy - 1 + WIDE
+            out[n, :, :, x0 : x0 + 4, y0 : y0 + 4] = np.einsum("at,bq->abtq", first, second)
+        return out.reshape(len(elements) * q * q, SPAN * PAD)
 
     mat = {}
+    mat["kt"] = np.concatenate(
+        [placed(stiff, mass, ring3) + placed(mass, stiff, ring3), placed(own, own, ring2)])
+    mat["tt"] = placed(mass, mass, ring3)
+    cross = np.zeros((len(ring2), q, q, len(ring3), q, q))
+    ends = {(1, 0): (3, 0), (-1, 0): (0, 3), (0, 1): (3, 0), (0, -1): (0, 3)}
+    diag3 = np.diag(t3)
+    for n, (dx, dy) in enumerate(ring2):
+        cross[n, :, :, n] += np.einsum("ac,bd->abcd", k3, diag3)
+        cross[n, :, :, n] += np.einsum("ac,bd->abcd", diag3, k3)
+        for (fx, fy), (mine, theirs) in ends.items():
+            m = ring3.index((dx + fx, dy + fy))
+            line = np.zeros((q, q))
+            line[mine] = k3[theirs]
+            if fx:
+                cross[n, :, :, m] += np.einsum("ac,bd->abcd", line, diag3)
+            else:
+                cross[n, :, :, m] += np.einsum("ac,bd->abcd", diag3, line)
+    mat["lxy"] = cross.reshape(len(ring2) * 16, len(ring3) * 16)
+    k7j = k7 @ j73
+    lines = np.zeros((len(ring1), 4, 4, len(ring2), q, q))
+    fine = np.zeros((f, f, 48))
+    t7j = t7[:, None] * j73
+    fine[:, :, :16] = (
+        np.einsum("ia,jb->ijab", k7j, t7j) + np.einsum("ia,jb->ijab", t7j, k7j)
+    ).reshape(f, f, 16)
+    fine[:, :, 32:] = np.einsum("ia,jb->ijab", t7j, t7j).reshape(f, f, 16)
+    for face, ((fx, fy), (mine, theirs)) in enumerate(ends.items()):
+        mine, theirs = (f - 1 if mine else 0), (f - 1 if theirs else 0)
+        for n, (dx, dy) in enumerate(ring1):
+            m = ring2.index((dx + fx, dy + fy))
+            for c in range(q):
+                if fx:
+                    lines[n, face, c, m, :, c] = k7j[theirs]
+                else:
+                    lines[n, face, c, m, c, :] = k7j[theirs]
+        if fx:
+            fine[mine, :, 16 + 4 * face : 20 + 4 * face] = t7j
+        else:
+            fine[:, mine, 16 + 4 * face : 20 + 4 * face] = t7j
+    mat["lines"] = lines.reshape(len(ring1) * 16, len(ring2) * 16)
+    mat["fine"] = fine.reshape(f * f, 48)
+    mat["pfine"] = np.einsum("ia,jb->ijab", j73, j73).reshape(f * f, 16)
+    row["tc"] = np.broadcast_to(tc, (1, 16, LANES))
     az7 = (join_z(f) @ np.kron(np.eye(EZ), k7)).T
     az3 = two((join_z(q) @ np.kron(np.eye(EZ), k3)).T)
     down = (join_z(q) @ np.kron(np.eye(EZ), j73.T) @ np.diag(np.tile(c7, EZ))).T
@@ -246,6 +309,8 @@
     mat["az3"] = az3
     up = np.kron(np.eye(EZ), j73).T
     mat["up"] = two(up)
+    up_tk = up * np.tile(t7, EZ)[None]
+    mat["upt"] = np.concatenate([two(up_tk), two(up @ az7)], axis=1)
     gather = np.zeros((EZ, EZ * q))
     for e in range(EZ):
         for node in (0, 1):
@@ -281,8 +346,9 @@
     return tiles, row16, mats, where
 
 
-MATS = ("az7", "down", "az3", "up", "b12", "back", "sin")
-N_LINKS = 8 + 4 + 4 + 4 + 4 + 8 + 4 + 4 + 4
+MATS = ("az7", "down", "az3", "b12", "sin", "back", "kt", "tt", "lxy", "lines", "up", "upt",
+        "fine", "pfine")
+N_LINKS = 8 + 4 + 4 + 8 + 4 + 4 + 12 + 24 + 4
 
 
 def reach(n):
@@ -299,7 +365,7 @@
     count = len(names)
     hbm, out_ref, vmem = refs[:count], refs[count], refs[count + 1 : 2 * count + 1]
     (fine_send, fine_recv, mid_send, mid_recv, line_send, line_recv, mode_send, mode_recv,
-     load_sem, send_sem, recv_sem, line_ss, line_rs, mode_ss, mode_rs, known) = refs[2 * count + 1 :]
+     rest3_all, x3_all, rest7_all, load_sem, send_sem, recv_sem, line_ss, line_rs, mode_ss, mode_rs, known) = refs[2 * count + 1 :]
     sx, cx = lax.axis_index("stream"), lax.axis_index("cross")
     tile_ref, row_ref = vmem[1], vmem[2]
     mat = dict(zip(MATS, vmem[3:]))
@@ -317,7 +383,7 @@
 
     bar = pltpu.get_barrier_semaphore()
     corners = ((1, 1), (1, -1), (-1, 1), (-1, -1))
-    faces = ((1, 0), (-1, 0), (0, 1), (0, -1))
+    faces = FACES
     near_x, hops_x = reach(nx)
     near_y, hops_y = reach(ny)
     near = [(s * d, 0) for d in near_x for s in (1, -1)]
@@ -493,7 +559,7 @@
     around = faces + corners
     copies = [start(mid_send.at[3, 0], mid_recv.at[3 + n // 4, n % 4], d)
               for n, d in enumerate(around)]
-    rest7 = b7 - fine_join(2, side7, local7)
+    rest7_all[0] = (b7 - fine_join(2, side7, local7)).reshape(128, LANES)
     for copy in copies:
         copy.wait_recv()
     shifts = ((4, mrow < 4), (12, mrow >= 12), (13, brow == 0), (3, brow == 3),
@@ -502,7 +568,7 @@
     for n, (shift, mask) in enumerate(shifts):
         b3 = b3 + shifted(mid_recv[3 + n // 4, n % 4], shift, mask)
 
-    need("az3", "b12", "sin", "back", "up")
+    need("az3", "b12")
     told(1)
     e3 = rtab("e3")[0] * keep3
     tab3 = rtab("tab")[0]
@@ -535,10 +601,19 @@
 
     lax.fori_loop(1, ny, line_out, 0)
     line_recv[cx] = line
+    ring1, ring2, ring3 = offsets(1), offsets(2), offsets(3)
     side3 = mid_start(1, ax, ay)
+    x3_all[0] = x3
+    side = [start(x3_all.at[0], x3_all.at[n], (-dx, -dy))
+            for n, (dx, dy) in enumerate(ring2) if n]
+    side += [start(rest7_all.at[0], rest7_all.at[n], (-dx, -dy))
+             for n, (dx, dy) in enumerate(ring1) if n]
     if ny < 32:
         line_recv[ny:] = jnp.zeros((32 - ny, 1, LANES), jnp.float32)
-    rest3 = b3 - mid_join(1, side3, ax + ay + mid_z(x3))
+    rest3_all[0] = b3 - mid_join(1, side3, ax + ay + mid_z(x3))
+    side += [start(rest3_all.at[0], rest3_all.at[n], (-dx, -dy))
+             for n, (dx, dy) in enumerate(ring3) if n]
+    need("sin")
 
     def line_in(d, carry):
         line_copy(d, lax.rem(cx + ny - d, ny), cx).wait()
@@ -578,45 +653,78 @@
     second = mode_recv[:, 1]
     nodes = first + jnp.concatenate([second[1:], second[:1]], axis=0)
     start_g = where["green"][0]
-    solved = [jnp.sum(tile_ref[start_g + n : start_g + n + nx] * nodes, axis=0) for n in range(4)]
-    sine = tile_ref[pl.ds(where["sine"][0] + cx + 1, 4)]
+    solved = [jnp.sum(tile_ref[start_g + n : start_g + n + nx] * nodes, axis=0)
+              for n in range(SPAN)]
+    sine = tile_ref[pl.ds(where["sine"][0] + cx, PAD)]
     window = [jnp.sum(sine * s[None], axis=1) for s in solved]
     window = jnp.concatenate(window, axis=0)
+    need(*MATS)
     window = dot(window, mat["back"][...])
     zval, zstiff = window[:, :LANES], window[:, LANES:]
 
-    x3 = x3 + left("pj", zval)
-    r0 = rest3 - left("kt", zval) - left("tt", zstiff)
-    w1 = e3 * r0
-    ax, ay = left("lx", w1), left("ly", w1)
-    copies = mid_start(2, ax, ay)
-    r1 = r0 - mid_join(2, copies, ax + ay + mid_z(w1))
-    x3 = x3 + (1.0 + keep_m) * w1 + gain_m * (e3 * r1)
-
-    jb, ji = tab("jb"), tab("ji").reshape(4, 8, 8, LANES)
-    halves = dot(x3, mat["up"][...])
-    parts = []
-    for r in range(2):
-        half = halves[:, r * LANES : (r + 1) * LANES]
-        cols = []
-        for a in range(4):
-            acc = jb[0] * half[4 * a : 4 * a + 1]
-            for b in range(1, 4):
-                acc = acc + jb[b] * half[4 * a + b : 4 * a + b + 1]
-            cols.append(acc)
-        acc = ji[0] * cols[0][None]
-        for a in range(1, 4):
-            acc = acc + ji[a] * cols[a][None]
-        parts.append(acc)
-    px = jnp.stack(parts, axis=0)
-    ax, ay = fine_xy(px)
-    copies = fine_send_faces(3, ax, ay)
-    r0 = rest7 - fine_join(3, copies, ax + ay + fine_z(px))
-    u1 = e7[None] * r0
-    ax, ay = fine_xy(u1)
-    copies = fine_send_faces(4, ax, ay)
-    r1 = r0 - fine_join(4, copies, ax + ay + fine_z(u1))
-    out = x7 + px + (1.0 + keep_f) * u1 + gain_f * (e7[None] * r1)
+    def masked(dy, table, top, index):
+        low = jnp.where(cx + dy == 0, 0, -1)
+        high = jnp.where(cx + dy == ny - 1, top, -1)
+        return table * jnp.where((index == low) | (index == high), 0.0, 1.0)
+
+    e3 = {dy: masked(dy, rtab("e3")[0], MID_ORDER, brow) for dy in range(-3, 4)}
+    tc = rtab("tc")[0]
+    n2, n3 = 16 * len(ring2), 16 * len(ring3)
+    for copy in side:
+        copy.wait_recv()
+
+    def per(table, count):
+        return jnp.concatenate([table] * count, axis=0)
+
+    from_low = dot(mat["kt"][...], zval)
+    r0 = rest3_all[...].reshape(n3, LANES) - per(tc, len(ring3)) * from_low[:n3]
+    r0 = r0 - dot(mat["tt"][...], zstiff)
+    e3_all = jnp.concatenate([e3[dy] for _, dy in ring3], axis=0)
+    w1 = e3_all * r0
+    aw = per(tc, len(ring2)) * dot(mat["lxy"][...], w1)
+    aw = aw + per(tab3, len(ring2)) * dot(w1[:n2], mat["az3"][...])
+    x3 = x3_all[...].reshape(n2, LANES) + from_low[n3:]
+    x3 = x3 + (1.0 + keep_m) * w1[:n2] + gain_m * (e3_all[:n2] * (r0[:n2] - aw))
+
+    n1 = 16 * len(ring1)
+    lines = dot(dot(mat["lines"][...], x3), mat["upt"][:, : 2 * LANES])
+    mine = dot(x3[:n1], mat["upt"][...])
+    px = dot(x3[:16], mat["up"][...])
+    px = jnp.stack([dot(mat["pfine"][...], px[:, r * LANES : (r + 1) * LANES]) for r in range(2)])
+    px = px.reshape(2, 8, 8, LANES)
+    columns = []
+    for n in range(len(ring1)):
+        for r in range(2):
+            at_n, at_r = slice(16 * n, 16 * n + 16), slice(r * LANES, (r + 1) * LANES)
+            also = slice((2 + r) * LANES, (3 + r) * LANES)
+            columns.append(jnp.concatenate(
+                [mine[at_n, at_r], lines[at_n, at_r], mine[at_n, also]], axis=0))
+    apx = dot(mat["fine"][...], jnp.concatenate(columns, axis=1))
+    kx = tab("kx").reshape(8, 8, 8, LANES)
+    ky_last, ky_first = tab("kyl"), tab("kyf")
+    r0, u1 = [], []
+    for n, (dx, dy) in enumerate(ring1):
+        moved = jnp.stack([apx[:, (2 * n + r) * LANES : (2 * n + r + 1) * LANES] for r in range(2)])
+        r0.append(rest7_all[n].reshape(2, 8, 8, LANES) - moved.reshape(2, 8, 8, LANES))
+        scale = masked(dy, tab("e7"), ORDER, jrow[None]) if dy else e7
+        u1.append(scale[None] * r0[n])
+
+    def along_x(u, row):
+        acc = kx[0][row][None] * u[:, 0]
+        for a in range(1, 8):
+            acc = acc + kx[a][row][None] * u[:, a]
+        return acc.reshape(16, LANES)
+
+    def along_y(u, table):
+        weighted = jnp.sum(table[None] * u, axis=2)
+        return (tab("ti")[:, 0][None] * weighted).reshape(16, LANES)
+
+    ax, ay = fine_xy(u1[0])
+    au = ax + ay + fine_z(u1[0])
+    au = add_x(au, along_x(u1[2], 7), along_x(u1[1], 0))
+    au = add_y(au, along_y(u1[4], ky_last), along_y(u1[3], ky_first))
+    x7 = x7 + px
+    out = x7 + (1.0 + keep_f) * u1[0] + gain_f * (e7[None] * (r0[0] - au))
     out_ref[...] = out.reshape(128, LANES)
     for copy in sent:
         copy.wait_send()
@@ -646,6 +754,9 @@
                 pltpu.VMEM((32, 1, LANES), f32),
                 pltpu.VMEM((2, 8, LANES), f32),
                 pltpu.VMEM((nx, 2, 8, LANES), f32),
+                pltpu.VMEM((len(offsets(3)), 16, LANES), f32),
+                pltpu.VMEM((len(offsets(2)), 16, LANES), f32),
+                pltpu.VMEM((len(offsets(1)), 128, LANES), f32),
                 links((len(operands),)),
                 links((N_LINKS,)),
                 links((N_LINKS,)),

time: 75 us -> 67.5 us (0.900); the launches traced: 74 us -> 67.3 us
  Pallas kernels: 72.5 us -> 65.8 us
    pallas_call x1, Pallas kernels: 72.5 us -> 65.8 us  [body(): pl.pallas_call(functools.partial(kernel, nx, ny, where), out_shape=jax.Sh...]
where the time goes in v3:
time: 67.5 us; the launch traced here: 67.3 us
  Pallas kernels  65.8 us (97%)
  local copies, waits for them, and re-layouts  1.47 us (2%)
    pallas_call x1, Pallas kernels, body(): pl.pallas_call(functools.partial(kernel, nx, ny, where), out_shape=jax.Sh...  65.8 us
    unnamed x1, local copies, waits for them, and re-layouts  1.47 us

profile of v3, /device:TPU:1, one launch (start us, length us, event | category | flops | bytes accessed | tf_op | source)
XLA Modules:
  0.0 67.3 jit_solution(4059661815289557797)
XLA Ops:
  0.0 65.8 %vcycle.1 = f32[128,128]{1,0:T(8,128)} custom-call(f32[128,128]{1,0:T(8,128)} %bitcast.5, f32[228,8,128]{2,1,0:T(8,128)} %constant.32.clone.refs_1_, f32[70,16,128]{2,1,0:T(8,128)} %constant.33.clone.refs_2_, f32[128,128]{1,0:T(8,128)} %constant.34.clone.refs_3_, f32[256,128]{1,0:T(8,128)} %constant.35.clone.refs_4_, f32[128,128]{1,0:T(8,128)} %constant.36.clone.refs_5_, ...), custom_call_target="tpu_custom_call" | custom-call | tf_op jit(solution)/shard_map/vcycle/pallas_call | solution.py:742
  65.8 1.5 %copy.20 = f32[2,1,1,8,8,128]{5,4,3,2,1,0:T(8,128)} copy(f32[2,1,1,8,8,128]{5,4,3,2,1,0:T(8,128)} %bitcast.4) | data formatting | bytes 131072

commit v4 on v3

--- a/solution.py
+++ b/solution.py
@@ -14,9 +14,12 @@
 EZ = 16
 LANES = 128
 MODES = 32
-EXACT = lax.Precision.HIGHEST
 MESH_ID = pl.DeviceIdType.MESH
 FACES = ((1, 0), (-1, 0), (0, 1), (0, -1))
+CORNERS = ((1, 1), (1, -1), (-1, 1), (-1, -1))
+TWICE = ((2, 0), (-2, 0), (0, 2), (0, -2))
+KNIGHTS = tuple((s * a, t * b) for a, b in ((2, 1), (1, 2)) for s in (1, -1) for t in (1, -1))
+AROUND = ((0, 0),) + FACES + CORNERS + TWICE + KNIGHTS
 WIDE, SPAN, PAD = 4, 10, 16
 
 
@@ -272,6 +275,18 @@
                 cross[n, :, :, m] += np.einsum("ac,bd->abcd", line, diag3)
             else:
                 cross[n, :, :, m] += np.einsum("ac,bd->abcd", diag3, line)
+    pick = np.zeros((len(ring1), q, q, len(AROUND), q, q))
+    for n, (dx, dy) in enumerate(ring1):
+        for m, (gx, gy) in enumerate(AROUND):
+            sx, sy = gx - dx, gy - dy
+            if max(abs(sx), abs(sy)) > 1:
+                continue
+            span_x = [(a, a) for a in range(q)] if sx == 0 else [(q - 1, 0) if sx > 0 else (0, q - 1)]
+            span_y = [(b, b) for b in range(q)] if sy == 0 else [(q - 1, 0) if sy > 0 else (0, q - 1)]
+            for a, a2 in span_x:
+                for b, b2 in span_y:
+                    pick[n, a, b, m, a2, b2] = 1.0
+    mat["pick"] = pick.reshape(len(ring1) * 16, len(AROUND) * 16)
     mat["lxy"] = cross.reshape(len(ring2) * 16, len(ring3) * 16)
     k7j = k7 @ j73
     lines = np.zeros((len(ring1), 4, 4, len(ring2), q, q))
@@ -294,6 +309,7 @@
             fine[mine, :, 16 + 4 * face : 20 + 4 * face] = t7j
         else:
             fine[:, mine, 16 + 4 * face : 20 + 4 * face] = t7j
+    mat["lown"] = mat["lxy"][:16, : 16 * len(ring1)]
     mat["lines"] = lines.reshape(len(ring1) * 16, len(ring2) * 16)
     mat["fine"] = fine.reshape(f * f, 48)
     mat["pfine"] = np.einsum("ia,jb->ijab", j73, j73).reshape(f * f, 16)
@@ -346,9 +362,9 @@
     return tiles, row16, mats, where
 
 
-MATS = ("az7", "down", "az3", "b12", "sin", "back", "kt", "tt", "lxy", "lines", "up", "upt",
+MATS = ("az7", "down", "pick", "lown", "az3", "b12", "sin", "back", "kt", "tt", "lxy", "lines", "up", "upt",
         "fine", "pfine")
-N_LINKS = 8 + 4 + 4 + 8 + 4 + 4 + 12 + 24 + 4
+N_LINKS = 20 + 4 + 20 + 4 + 12 + 24 + 4
 
 
 def reach(n):
@@ -364,7 +380,8 @@
     names = ("x", "tiles", "rows") + MATS
     count = len(names)
     hbm, out_ref, vmem = refs[:count], refs[count], refs[count + 1 : 2 * count + 1]
-    (fine_send, fine_recv, mid_send, mid_recv, line_send, line_recv, mode_send, mode_recv,
+    (pair_send, pair_recv, edge_send, corner_recv, twice_recv, knight_send, knight_recv, g3_all,
+     fine_send, fine_recv, mid_send, mid_recv, line_send, line_recv, mode_send, mode_recv,
      rest3_all, x3_all, rest7_all, load_sem, send_sem, recv_sem, line_ss, line_rs, mode_ss, mode_rs, known) = refs[2 * count + 1 :]
     sx, cx = lax.axis_index("stream"), lax.axis_index("cross")
     tile_ref, row_ref = vmem[1], vmem[2]
@@ -382,13 +399,12 @@
         return row_ref[start : start + size]
 
     bar = pltpu.get_barrier_semaphore()
-    corners = ((1, 1), (1, -1), (-1, 1), (-1, -1))
     faces = FACES
     near_x, hops_x = reach(nx)
     near_y, hops_y = reach(ny)
     near = [(s * d, 0) for d in near_x for s in (1, -1)]
     near += [(0, s * d) for d in near_y for s in (1, -1)]
-    near += corners
+    near += CORNERS + KNIGHTS
     for d in near:
         pl.semaphore_signal(bar, inc=1, device_id=at(*d), device_id_type=MESH_ID)
     loads = {}
@@ -438,8 +454,15 @@
     _, keep_f, gain_f = smoother(ORDER)
     _, keep_m, gain_m = smoother(MID_ORDER)
 
+    def halves(a):
+        top = a.astype(jnp.bfloat16)
+        return top, (a - top.astype(jnp.float32)).astype(jnp.bfloat16)
+
     def dot(a, b):
-        return jnp.dot(a, b, preferred_element_type=jnp.float32, precision=EXACT)
+        (a1, a2), (b1, b2) = halves(a), halves(b)
+        parts = [jnp.dot(x, y, preferred_element_type=jnp.float32)
+                 for x, y in ((a1, b2), (a2, b1), (a1, b1))]
+        return parts[0] + parts[1] + parts[2]
 
     def fine_xy(u):
         kx = tab("kx").reshape(8, 8, 8, LANES)
@@ -457,13 +480,13 @@
         az = dot(u.reshape(128, LANES), mat["az7"][...])
         return az.reshape(2, 8, 8, LANES) * tab("tij")[None]
 
-    def fine_send_faces(n, ax, ay):
-        fine_send[n, 0] = ax[:, 7].reshape(16, LANES)
-        fine_send[n, 1] = ax[:, 0].reshape(16, LANES)
+    def fine_send_faces(ax, ay):
+        fine_send[0] = ax[:, 7].reshape(16, LANES)
+        fine_send[1] = ax[:, 0].reshape(16, LANES)
         flat = ay.reshape(16, 8, LANES)
-        fine_send[n, 2] = flat[:, 7, :]
-        fine_send[n, 3] = flat[:, 0, :]
-        return [start(fine_send.at[n, d], fine_recv.at[n, d], faces[d]) for d in range(4)]
+        fine_send[2] = flat[:, 7, :]
+        fine_send[3] = flat[:, 0, :]
+        return [start(fine_send.at[d], fine_recv.at[d], faces[d]) for d in range(4)]
 
     def add_x(field, low, high):
         return jnp.concatenate(
@@ -476,11 +499,11 @@
         flat = flat + jnp.where(jrow[None] == 7, high[:, None, :], 0.0)
         return flat.reshape(2, 8, 8, LANES)
 
-    def fine_join(n, copies, field):
+    def fine_join(copies, field):
         for copy in copies:
             copy.wait_recv()
-        field = add_x(field, fine_recv[n, 0], fine_recv[n, 1])
-        return add_y(field, fine_recv[n, 2], fine_recv[n, 3])
+        field = add_x(field, fine_recv[0], fine_recv[1])
+        return add_y(field, fine_recv[2], fine_recv[3])
 
     def left(name, v):
         start_row, size = where[name]
@@ -489,61 +512,132 @@
             acc = acc + row_ref[start_row + c] * v[c : c + 1]
         return acc
 
-    def mid_start(n, ax, ay):
-        mid_send[n, 0] = ax
-        mid_send[n, 1] = ay
-        return [start(mid_send.at[n, d // 2], mid_recv.at[n, d], faces[d]) for d in range(4)]
+    def mid_start(ax, ay):
+        mid_send[0] = ax
+        mid_send[1] = ay
+        return [start(mid_send.at[d // 2], mid_recv.at[d], faces[d]) for d in range(4)]
 
     def shifted(v, shift, mask):
         return jnp.where(mask, pltpu.roll(v, shift, 0), 0.0)
 
-    def mid_join(n, copies, field):
+    def mid_join(copies, field):
         for copy in copies:
             copy.wait_recv()
-        field = field + shifted(mid_recv[n, 0], 4, mrow < 4)
-        field = field + shifted(mid_recv[n, 1], 12, mrow >= 12)
-        field = field + shifted(mid_recv[n, 2], 13, brow == 0)
-        return field + shifted(mid_recv[n, 3], 3, brow == 3)
+        field = field + shifted(mid_recv[0], 4, mrow < 4)
+        field = field + shifted(mid_recv[1], 12, mrow >= 12)
+        field = field + shifted(mid_recv[2], 13, brow == 0)
+        return field + shifted(mid_recv[3], 3, brow == 3)
+
+    def masked(dy, table, top, index):
+        low = jnp.where(cx + dy == 0, 0, -1)
+        high = jnp.where(cx + dy == ny - 1, top, -1)
+        return table * jnp.where((index == low) | (index == high), 0.0, 1.0)
+
+    def along_x(u, row):
+        acc = kx[0][row][None] * u[:, 0]
+        for a in range(1, 8):
+            acc = acc + kx[a][row][None] * u[:, a]
+        return acc.reshape(16, LANES)
+
+    def along_y(u, table):
+        weighted = jnp.sum(table[None] * u, axis=2)
+        return (tab("ti")[:, 0][None] * weighted).reshape(16, LANES)
 
     need("x")
     src = vmem[0][...].reshape(16, 8, LANES)
     knode = lax.rem(lane, 8)
     src = (src + jnp.where(knode[None] == 7, pltpu.roll(src, LANES - 1, 2), 0.0)
            + jnp.where(knode[None] == 0, pltpu.roll(src, 1, 2), 0.0))
-    fine_send[0, 2] = src[:, 7, :]
-    fine_send[0, 3] = src[:, 0, :]
+    y7, y0 = src[:, 7, :], src[:, 0, :]
     src = src.reshape(2, 8, 8, LANES)
-    fine_send[0, 0] = src[:, 7].reshape(16, LANES)
-    fine_send[0, 1] = src[:, 0].reshape(16, LANES)
+    x7, x0 = src[:, 7].reshape(16, LANES), src[:, 0].reshape(16, LANES)
+    for n, edge in enumerate((x7, y7, x0, y0, x7)):
+        edge_send[n] = edge
+    for i, row in ((1, 7), (0, 0)):
+        for j, line in ((1, y7), (0, y0)):
+            knight_send[2 * i + j] = line.reshape(2, 8, LANES)[:, row : row + 1]
+    need("tiles")
+    e7 = masked(0, tab("e7"), ORDER, jrow[None])
+    kx = tab("kx").reshape(8, 8, 8, LANES)
+    ky_last, ky_first = tab("kyl"), tab("kyf")
+    scaled = e7[None] * src
+    pairs = ((x0, along_x(scaled, 0)), (x7, along_x(scaled, 7)),
+             (y0, along_y(scaled, ky_first)), (y7, along_y(scaled, ky_last)))
+    for n, (raw, contracted) in enumerate(pairs):
+        pair_send[n, 0] = raw
+        pair_send[n, 1] = contracted
     pl.semaphore_wait(bar, len(near))
     tell(0)
-    copies = [start(fine_send.at[0, 2 if d[1] > 0 else 3], fine_recv.at[5, n], d)
-              for n, d in enumerate(corners)]
-    copies += [start(fine_send.at[0, d], fine_recv.at[0, d], faces[d]) for d in range(4)]
-    need("tiles", "az7")
-    e7 = tab("e7") * keep7[None]
+    copies = [start(knight_send.at[2 * (dx < 0) + (dy < 0)], knight_recv.at[n], (-dx, -dy))
+              for n, (dx, dy) in enumerate(KNIGHTS)]
+    pick_edge = {(1, 1): 2, (1, -1): 1, (-1, 1): 3, (-1, -1): 0}
+    copies += [start(edge_send.at[pick_edge[d] : pick_edge[d] + 2], corner_recv.at[n],
+                     (-d[0], -d[1])) for n, d in enumerate(CORNERS)]
+    copies += [start(edge_send.at[(2, 0, 3, 1)[n]], twice_recv.at[n], (-dx, -dy))
+               for n, (dx, dy) in enumerate(TWICE)]
+    copies += [start(pair_send.at[n], pair_recv.at[n], (-dx, -dy))
+               for n, (dx, dy) in enumerate(FACES)]
+    need("az7")
     for copy in copies:
         copy.wait_recv()
     told(0)
     tell(1)
     irow = jrow[None]
 
-    def end(n, shift, row):
-        line = fine_recv[5, n].reshape(2, 8, LANES)
-        return jnp.where(irow == row, pltpu.roll(line, shift, 1), 0.0).reshape(16, LANES)
-
-    low = fine_recv[0, 2] + end(0, 1, 0) + end(2, 7, 7)
-    high = fine_recv[0, 3] + end(1, 1, 0) + end(3, 7, 7)
-    b7 = add_y(add_x(src, fine_recv[0, 0], fine_recv[0, 1]), low, high)
+    def lines_of(value):
+        return value.reshape(2, 8, LANES)
+
+    def row_of(value, row):
+        return lines_of(value)[:, row : row + 1]
+
+    def with_ends(line, first, last):
+        line = lines_of(line) + jnp.where(irow == 0, first, 0.0) + jnp.where(irow == 7, last, 0.0)
+        return line.reshape(16, LANES)
+
+    knight = {d: knight_recv[n] for n, d in enumerate(KNIGHTS)}
+    twice = {d: twice_recv[n] for n, d in enumerate(TWICE)}
+    raw = {d: pair_recv[n, 0] for n, d in enumerate(FACES)}
+    corner_x = {d: corner_recv[n, 0 if d[0] == d[1] else 1] for n, d in enumerate(CORNERS)}
+    corner_y = {d: corner_recv[n, 1 if d[0] == d[1] else 0] for n, d in enumerate(CORNERS)}
+
+    def joined(center, low_x, high_x, low_y, high_y):
+        return add_y(add_x(center, low_x, high_x), low_y, high_y)
+
+    b7 = joined(
+        src, raw[-1, 0], raw[1, 0],
+        with_ends(raw[0, -1], row_of(corner_y[-1, -1], 7), row_of(corner_y[1, -1], 0)),
+        with_ends(raw[0, 1], row_of(corner_y[-1, 1], 7), row_of(corner_y[1, 1], 0)))
+    zero = jnp.zeros_like(src)
+    extra = {
+        (1, 0): joined(
+            zero, x7, twice[2, 0],
+            with_ends(corner_y[1, -1], row_of(raw[0, -1], 7), knight[2, -1]),
+            with_ends(corner_y[1, 1], row_of(raw[0, 1], 7), knight[2, 1])),
+        (-1, 0): joined(
+            zero, twice[-2, 0], x0,
+            with_ends(corner_y[-1, -1], knight[-2, -1], row_of(raw[0, -1], 0)),
+            with_ends(corner_y[-1, 1], knight[-2, 1], row_of(raw[0, 1], 0))),
+        (0, 1): joined(
+            zero, corner_x[-1, 1], corner_x[1, 1],
+            with_ends(y7, row_of(raw[-1, 0], 7), row_of(raw[1, 0], 7)),
+            with_ends(twice[0, 2], knight[-1, 2], knight[1, 2])),
+        (0, -1): joined(
+            zero, corner_x[-1, -1], corner_x[1, -1],
+            with_ends(twice[0, -2], knight[-1, -2], knight[1, -2]),
+            with_ends(y0, row_of(raw[-1, 0], 0), row_of(raw[1, 0], 0))),
+    }
+    extra = {d: masked(d[1], tab("e7"), ORDER, jrow[None])[None] * v for d, v in extra.items()}
 
     u1 = e7[None] * b7
     ax, ay = fine_xy(u1)
-    copies = fine_send_faces(1, ax, ay)
-    az = fine_z(u1)
-    r1 = b7 - fine_join(1, copies, ax + ay + az)
+    au = add_x(ax + ay + fine_z(u1), pair_recv[1, 1] + along_x(extra[-1, 0], 7),
+               pair_recv[0, 1] + along_x(extra[1, 0], 0))
+    au = add_y(au, pair_recv[3, 1] + along_y(extra[0, -1], ky_last),
+               pair_recv[2, 1] + along_y(extra[0, 1], ky_first))
+    r1 = b7 - au
     x7 = (1.0 + keep_f) * u1 + gain_f * (e7[None] * r1)
     ax, ay = fine_xy(x7)
-    side7 = fine_send_faces(2, ax, ay)
+    side7 = fine_send_faces(ax, ay)
     az = fine_z(x7)
     local7 = ax + ay + az
     ci = tab("ci")[None]
@@ -555,33 +649,29 @@
         g = g + jx[i][None] * rest7[:, i : i + 1]
     g = jnp.concatenate([g[0].reshape(32, LANES), g[1].reshape(32, LANES)], axis=1)
     g3 = left("jy", dot(g, mat["down"][...]))
-    mid_send[3, 0] = g3
-    around = faces + corners
-    copies = [start(mid_send.at[3, 0], mid_recv.at[3 + n // 4, n % 4], d)
-              for n, d in enumerate(around)]
-    rest7_all[0] = (b7 - fine_join(2, side7, local7)).reshape(128, LANES)
+    g3_all[0] = g3
+    copies = [start(g3_all.at[0], g3_all.at[n], (-dx, -dy))
+              for n, (dx, dy) in enumerate(AROUND) if n]
+    rest7_all[0] = (b7 - fine_join(side7, local7)).reshape(128, LANES)
+    need("az3", "b12", "pick", "lown")
+    told(1)
+    ring1, ring2, ring3 = offsets(1), offsets(2), offsets(3)
+    e3 = {dy: masked(dy, rtab("e3")[0], MID_ORDER, brow) for dy in range(-3, 4)}
+    e3_all = jnp.concatenate([e3[dy] for _, dy in ring3], axis=0)
+    tc, tab3 = rtab("tc")[0], rtab("tab")[0]
+    n1, n2, n3 = 16 * len(ring1), 16 * len(ring2), 16 * len(ring3)
+
+    def mid_z(v):
+        return tab3 * dot(v, mat["az3"][...])
+
     for copy in copies:
         copy.wait_recv()
-    shifts = ((4, mrow < 4), (12, mrow >= 12), (13, brow == 0), (3, brow == 3),
-              (1, mrow == 0), (7, mrow == 3), (9, mrow == 12), (15, mrow == 15))
-    b3 = g3
-    for n, (shift, mask) in enumerate(shifts):
-        b3 = b3 + shifted(mid_recv[3 + n // 4, n % 4], shift, mask)
-
-    need("az3", "b12")
-    told(1)
-    e3 = rtab("e3")[0] * keep3
-    tab3 = rtab("tab")[0]
-
-    def mid_z(v):
-        return tab3 * dot(v, mat["az3"][...])
-
-    v1 = e3 * b3
-    ax, ay = left("lx", v1), left("ly", v1)
-    copies = mid_start(0, ax, ay)
-    az = mid_z(v1)
-    r1 = b3 - mid_join(0, copies, ax + ay + az)
-    x3 = (1.0 + keep_m) * v1 + gain_m * (e3 * r1)
+
+    b3 = dot(mat["pick"][...], g3_all[...].reshape(16 * len(AROUND), LANES))
+    v1 = e3_all[:n1] * b3
+    b3, e3 = b3[:16], e3[0]
+    r1 = b3 - tc * dot(mat["lown"][...], v1) - mid_z(v1[:16])
+    x3 = (1.0 + keep_m) * v1[:16] + gain_m * (e3 * r1)
     ax, ay = left("lx", x3), left("ly", x3)
     ca, cb = rtab("ca")[0], rtab("cb")[0]
     part = keep3 * (g3 - cb * ax - ca * ay)
@@ -595,14 +685,18 @@
             line_send.at[0], line_recv.at[slot], line_ss.at[d], line_rs.at[d],
             device_id={"cross": to}, device_id_type=MESH_ID)
 
-    def line_out(d, carry):
+    def far_first(n, size):
+        step = lax.div(n + 1, 2)
+        return size // 2 + step * (1 - 2 * lax.rem(n, 2))
+
+    def line_out(n, carry):
+        d = far_first(n, ny)
         line_copy(d, cx, lax.rem(cx + d, ny)).start()
         return carry
 
-    lax.fori_loop(1, ny, line_out, 0)
+    lax.fori_loop(0, ny - 1, line_out, 0)
     line_recv[cx] = line
-    ring1, ring2, ring3 = offsets(1), offsets(2), offsets(3)
-    side3 = mid_start(1, ax, ay)
+    side3 = mid_start(ax, ay)
     x3_all[0] = x3
     side = [start(x3_all.at[0], x3_all.at[n], (-dx, -dy))
             for n, (dx, dy) in enumerate(ring2) if n]
@@ -610,7 +704,7 @@
              for n, (dx, dy) in enumerate(ring1) if n]
     if ny < 32:
         line_recv[ny:] = jnp.zeros((32 - ny, 1, LANES), jnp.float32)
-    rest3_all[0] = b3 - mid_join(1, side3, ax + ay + mid_z(x3))
+    rest3_all[0] = b3 - mid_join(side3, ax + ay + mid_z(x3))
     side += [start(rest3_all.at[0], rest3_all.at[n], (-dx, -dy))
              for n, (dx, dy) in enumerate(ring3) if n]
     need("sin")
@@ -638,7 +732,8 @@
             mode_send, mode_recv.at[d], mode_ss.at[d], mode_rs.at[d],
             device_id={"stream": to}, device_id_type=MESH_ID)
 
-    def mode_out(d, carry):
+    def mode_out(n, carry):
+        d = far_first(n, nx)
         mode_copy(d, lax.rem(sx + d, nx)).start()
         return carry
 
@@ -646,7 +741,7 @@
         mode_copy(d, sx).wait()
         return carry
 
-    lax.fori_loop(1, nx, mode_out, 0)
+    lax.fori_loop(0, nx - 1, mode_out, 0)
     mode_recv[0] = mode_send[...]
     lax.fori_loop(1, nx, mode_in, 0)
     first = mode_recv[:, 0]
@@ -662,14 +757,6 @@
     window = dot(window, mat["back"][...])
     zval, zstiff = window[:, :LANES], window[:, LANES:]
 
-    def masked(dy, table, top, index):
-        low = jnp.where(cx + dy == 0, 0, -1)
-        high = jnp.where(cx + dy == ny - 1, top, -1)
-        return table * jnp.where((index == low) | (index == high), 0.0, 1.0)
-
-    e3 = {dy: masked(dy, rtab("e3")[0], MID_ORDER, brow) for dy in range(-3, 4)}
-    tc = rtab("tc")[0]
-    n2, n3 = 16 * len(ring2), 16 * len(ring3)
     for copy in side:
         copy.wait_recv()
 
@@ -679,14 +766,12 @@
     from_low = dot(mat["kt"][...], zval)
     r0 = rest3_all[...].reshape(n3, LANES) - per(tc, len(ring3)) * from_low[:n3]
     r0 = r0 - dot(mat["tt"][...], zstiff)
-    e3_all = jnp.concatenate([e3[dy] for _, dy in ring3], axis=0)
     w1 = e3_all * r0
     aw = per(tc, len(ring2)) * dot(mat["lxy"][...], w1)
     aw = aw + per(tab3, len(ring2)) * dot(w1[:n2], mat["az3"][...])
     x3 = x3_all[...].reshape(n2, LANES) + from_low[n3:]
     x3 = x3 + (1.0 + keep_m) * w1[:n2] + gain_m * (e3_all[:n2] * (r0[:n2] - aw))
 
-    n1 = 16 * len(ring1)
     lines = dot(dot(mat["lines"][...], x3), mat["upt"][:, : 2 * LANES])
     mine = dot(x3[:n1], mat["upt"][...])
     px = dot(x3[:16], mat["up"][...])
@@ -700,24 +785,12 @@
             columns.append(jnp.concatenate(
                 [mine[at_n, at_r], lines[at_n, at_r], mine[at_n, also]], axis=0))
     apx = dot(mat["fine"][...], jnp.concatenate(columns, axis=1))
-    kx = tab("kx").reshape(8, 8, 8, LANES)
-    ky_last, ky_first = tab("kyl"), tab("kyf")
     r0, u1 = [], []
     for n, (dx, dy) in enumerate(ring1):
         moved = jnp.stack([apx[:, (2 * n + r) * LANES : (2 * n + r + 1) * LANES] for r in range(2)])
         r0.append(rest7_all[n].reshape(2, 8, 8, LANES) - moved.reshape(2, 8, 8, LANES))
         scale = masked(dy, tab("e7"), ORDER, jrow[None]) if dy else e7
         u1.append(scale[None] * r0[n])
-
-    def along_x(u, row):
-        acc = kx[0][row][None] * u[:, 0]
-        for a in range(1, 8):
-            acc = acc + kx[a][row][None] * u[:, a]
-        return acc.reshape(16, LANES)
-
-    def along_y(u, table):
-        weighted = jnp.sum(table[None] * u, axis=2)
-        return (tab("ti")[:, 0][None] * weighted).reshape(16, LANES)
 
     ax, ay = fine_xy(u1[0])
     au = ax + ay + fine_z(u1[0])
@@ -746,10 +819,18 @@
             out_specs=pl.BlockSpec(memory_space=pltpu.VMEM),
             scratch_shapes=[pltpu.VMEM(o.shape, f32) for o in operands]
             + [
-                pltpu.VMEM((5, 4, 16, LANES), f32),
-                pltpu.VMEM((6, 4, 16, LANES), f32),
                 pltpu.VMEM((4, 2, 16, LANES), f32),
-                pltpu.VMEM((5, 4, 16, LANES), f32),
+                pltpu.VMEM((4, 2, 16, LANES), f32),
+                pltpu.VMEM((5, 16, LANES), f32),
+                pltpu.VMEM((4, 2, 16, LANES), f32),
+                pltpu.VMEM((4, 16, LANES), f32),
+                pltpu.VMEM((4, 2, 1, LANES), f32),
+                pltpu.VMEM((8, 2, 1, LANES), f32),
+                pltpu.VMEM((len(AROUND), 16, LANES), f32),
+                pltpu.VMEM((4, 16, LANES), f32),
+                pltpu.VMEM((4, 16, LANES), f32),
+                pltpu.VMEM((2, 16, LANES), f32),
+                pltpu.VMEM((4, 16, LANES), f32),
                 pltpu.VMEM((1, 1, LANES), f32),
                 pltpu.VMEM((32, 1, LANES), f32),
                 pltpu.VMEM((2, 8, LANES), f32),

time: 67.5 us -> 61.7 us (0.914)
  Pallas kernels: 65.8 us -> 60 us
    pallas_call x1, Pallas kernels: 65.8 us -> 60 us  [body(): pl.pallas_call(functools.partial(kernel, nx, ny, where), out_shape=jax.Sh...]
where the time goes in v4:
time: 61.7 us; the launch traced here: 61.5 us
  Pallas kernels  60 us (97%)
  local copies, waits for them, and re-layouts  1.47 us (2%)
    pallas_call x1, Pallas kernels, body(): pl.pallas_call(functools.partial(kernel, nx, ny, where), out_shape=jax.Sh...  60 us
    unnamed x1, local copies, waits for them, and re-layouts  1.47 us

profile of v4, /device:TPU:1, one launch (start us, length us, event | category | flops | bytes accessed | tf_op | source)
XLA Modules:
  0.0 61.5 jit_solution(14458446717397053269)
XLA Ops:
  0.0 60.0 %vcycle.1 = f32[128,128]{1,0:T(8,128)} custom-call(f32[128,128]{1,0:T(8,128)} %bitcast.5, f32[228,8,128]{2,1,0:T(8,128)} %constant.36.clone.refs_1_, f32[70,16,128]{2,1,0:T(8,128)} %constant.37.clone.refs_2_, f32[128,128]{1,0:T(8,128)} %constant.38.clone.refs_3_, f32[256,128]{1,0:T(8,128)} %constant.39.clone.refs_4_, f32[80,336]{1,0:T(8,128)} %constant.40.clone.refs_5_, ...), custom_call_target="tpu_custom_call" | custom-call | tf_op jit(solution)/shard_map/vcycle/pallas_call | solution.py:815
  60.0 1.5 %copy.22 = f32[2,1,1,8,8,128]{5,4,3,2,1,0:T(8,128)} copy(f32[2,1,1,8,8,128]{5,4,3,2,1,0:T(8,128)} %bitcast.4) | data formatting | bytes 131072

commit v5 on v4

--- a/solution.py
+++ b/solution.py
@@ -3,6 +3,7 @@
 
 import jax
 import jax.numpy as jnp
+import ml_dtypes
 import numpy as np
 from jax import lax
 from jax.experimental import pallas as pl
@@ -289,29 +290,22 @@
     mat["pick"] = pick.reshape(len(ring1) * 16, len(AROUND) * 16)
     mat["lxy"] = cross.reshape(len(ring2) * 16, len(ring3) * 16)
     k7j = k7 @ j73
-    lines = np.zeros((len(ring1), 4, 4, len(ring2), q, q))
-    fine = np.zeros((f, f, 48))
     t7j = t7[:, None] * j73
-    fine[:, :, :16] = (
-        np.einsum("ia,jb->ijab", k7j, t7j) + np.einsum("ia,jb->ijab", t7j, k7j)
-    ).reshape(f, f, 16)
-    fine[:, :, 32:] = np.einsum("ia,jb->ijab", t7j, t7j).reshape(f, f, 16)
-    for face, ((fx, fy), (mine, theirs)) in enumerate(ends.items()):
-        mine, theirs = (f - 1 if mine else 0), (f - 1 if theirs else 0)
-        for n, (dx, dy) in enumerate(ring1):
+    fine = np.zeros((len(ring1), f, f, len(ring2), q, q))
+    own_z = np.zeros((len(ring1), f, f, len(ring1), q, q))
+    for n, (dx, dy) in enumerate(ring1):
+        fine[n, :, :, n] += np.einsum("ia,jb->ijab", k7j, t7j) + np.einsum("ia,jb->ijab", t7j, k7j)
+        own_z[n, :, :, n] = np.einsum("ia,jb->ijab", t7j, t7j)
+        for (fx, fy), (mine, theirs) in ends.items():
+            mine, theirs = (f - 1 if mine else 0), (f - 1 if theirs else 0)
             m = ring2.index((dx + fx, dy + fy))
-            for c in range(q):
-                if fx:
-                    lines[n, face, c, m, :, c] = k7j[theirs]
-                else:
-                    lines[n, face, c, m, c, :] = k7j[theirs]
-        if fx:
-            fine[mine, :, 16 + 4 * face : 20 + 4 * face] = t7j
-        else:
-            fine[:, mine, 16 + 4 * face : 20 + 4 * face] = t7j
+            if fx:
+                fine[n, mine, :, m] += np.einsum("a,jb->jab", k7j[theirs], t7j)
+            else:
+                fine[n, :, mine, m] += np.einsum("ia,b->iab", t7j, k7j[theirs])
+    count = len(ring1) * f * f
+    mat["fine"] = np.concatenate([fine.reshape(count, -1), own_z.reshape(count, -1)], axis=1)
     mat["lown"] = mat["lxy"][:16, : 16 * len(ring1)]
-    mat["lines"] = lines.reshape(len(ring1) * 16, len(ring2) * 16)
-    mat["fine"] = fine.reshape(f * f, 48)
     mat["pfine"] = np.einsum("ia,jb->ijab", j73, j73).reshape(f * f, 16)
     row["tc"] = np.broadcast_to(tc, (1, 16, LANES))
     az7 = (join_z(f) @ np.kron(np.eye(EZ), k7)).T
@@ -345,26 +339,36 @@
     s0 = np.where(here < ny, sine_rows(mode, here, ny), 0.0)
     s1 = np.where(here < ny, sine_rows(mode, here + 1, ny), 0.0)
     mat["sin"] = np.concatenate([s0, s1], axis=0)
-    packed, where = [], {}
-    at = 0
-    for name, value in tile.items():
-        where[name] = (at, value.shape[0])
+    where, tiles = {}, []
+    for names in EARLY, LATE:
+        packed, start = [], 0
+        for name in names:
+            where[name] = (start, tile[name].shape[0])
+            packed.append(tile[name])
+            start += tile[name].shape[0]
+        tiles.append(np.concatenate(packed).astype(np.float32))
+    packed, start = [], 0
+    for name, value in row.items():
+        where[name] = (start, value.shape[0])
         packed.append(value)
-        at += value.shape[0]
-    tiles = np.concatenate(packed).astype(np.float32)
-    packed, at = [], 0
-    for name, value in row.items():
-        where[name] = (at, value.shape[0])
-        packed.append(value)
-        at += value.shape[0]
+        start += value.shape[0]
     row16 = np.concatenate(packed).astype(np.float32)
-    mats = {name: value.astype(np.float32) for name, value in mat.items()}
-    return tiles, row16, mats, where
-
-
-MATS = ("az7", "down", "pick", "lown", "az3", "b12", "sin", "back", "kt", "tt", "lxy", "lines", "up", "upt",
+    mats = []
+    for name in MATS:
+        value = mat[name].astype(np.float32)
+        top = value.astype(ml_dtypes.bfloat16)
+        rest = (value - top.astype(np.float32)).astype(ml_dtypes.bfloat16)
+        parts = [top, top] if name == "pick" else [top, rest, top]
+        mats.append(np.concatenate(parts, axis=0 if name in RIGHT else 1))
+    return (*tiles, row16, *mats), where
+
+
+EARLY = ("e7", "kx", "kyl", "kyf", "ti", "ky", "tij")
+LATE = ("cj", "ci", "jx", "green", "sine")
+RIGHT = ("az7", "down", "az3", "b12", "back", "up", "upt")
+MATS = ("az7", "down", "pick", "lown", "az3", "b12", "sin", "back", "kt", "tt", "lxy", "up", "upt",
         "fine", "pfine")
-N_LINKS = 20 + 4 + 20 + 4 + 12 + 24 + 4
+LINKS = 20 + 4 + 20 + 4 + 12 + 4 + 24
 
 
 def reach(n):
@@ -377,22 +381,22 @@
 
 
 def kernel(nx, ny, where, *refs):
-    names = ("x", "tiles", "rows") + MATS
+    names = ("x", "early", "late", "rows") + MATS
     count = len(names)
     hbm, out_ref, vmem = refs[:count], refs[count], refs[count + 1 : 2 * count + 1]
     (pair_send, pair_recv, edge_send, corner_recv, twice_recv, knight_send, knight_recv, g3_all,
      fine_send, fine_recv, mid_send, mid_recv, line_send, line_recv, mode_send, mode_recv,
-     rest3_all, x3_all, rest7_all, load_sem, send_sem, recv_sem, line_ss, line_rs, mode_ss, mode_rs, known) = refs[2 * count + 1 :]
+     rest3_all, x3_all, rest7_all, load_sem, send_sem, recv_sem, known) = refs[2 * count + 1 :]
     sx, cx = lax.axis_index("stream"), lax.axis_index("cross")
-    tile_ref, row_ref = vmem[1], vmem[2]
-    mat = dict(zip(MATS, vmem[3:]))
+    early_ref, late_ref, row_ref = vmem[1:4]
+    mat = dict(zip(MATS, vmem[4:]))
 
     def at(dx, dy):
         return {"stream": lax.rem(sx + (nx + dx), nx), "cross": lax.rem(cx + (ny + dy), ny)}
 
     def tab(name):
         start, size = where[name]
-        return tile_ref[start : start + size]
+        return (early_ref if name in EARLY else late_ref)[start : start + size]
 
     def rtab(name):
         start, size = where[name]
@@ -408,9 +412,14 @@
     for d in near:
         pl.semaphore_signal(bar, inc=1, device_id=at(*d), device_id_type=MESH_ID)
     loads = {}
-    for n, name in enumerate(names):
-        loads[name] = pltpu.make_async_copy(hbm[n], vmem[n], load_sem.at[n])
-        loads[name].start()
+
+    def load(first, last):
+        for n in range(first, last):
+            copy = pltpu.make_async_copy(hbm[n], vmem[n], load_sem.at[n])
+            copy.start()
+            loads[names[n]] = copy
+
+    load(0, 2)
 
     def need(*wanted):
         for name in wanted:
@@ -430,17 +439,30 @@
             if step < len(hops):
                 pl.semaphore_wait(known.at[step, n], 2)
 
-    links = [0]
-    sent = []
-
-    def start(src, dst, to):
-        n = links[0]
-        links[0] += 1
-        copy = pltpu.make_async_remote_copy(
-            src, dst, send_sem.at[n], recv_sem.at[n], device_id=at(*to), device_id_type=MESH_ID)
-        copy.start()
-        sent.append(copy)
-        return copy
+    used = [0]
+
+    class Group:
+        def __init__(self, size):
+            self.base, self.copies = used[0], []
+            used[0] += size
+
+        def make(self, n, src, dst, device):
+            return pltpu.make_async_remote_copy(
+                src, dst, send_sem.at[self.base + n], recv_sem.at[self.base + n],
+                device_id=device, device_id_type=MESH_ID)
+
+        def start(self, src, dst, to):
+            copy = self.make(len(self.copies), src, dst, at(*to))
+            copy.start()
+            self.copies.append(copy)
+
+        def arrived(self):
+            for copy in self.copies:
+                copy.wait_recv()
+
+        def left(self):
+            for copy in self.copies:
+                copy.wait_send()
 
     jrow = lax.broadcasted_iota(jnp.int32, (8, LANES), 0)
     lane = lax.broadcasted_iota(jnp.int32, (8, LANES), 1)
@@ -458,11 +480,16 @@
         top = a.astype(jnp.bfloat16)
         return top, (a - top.astype(jnp.float32)).astype(jnp.bfloat16)
 
-    def dot(a, b):
-        (a1, a2), (b1, b2) = halves(a), halves(b)
-        parts = [jnp.dot(x, y, preferred_element_type=jnp.float32)
-                 for x, y in ((a1, b2), (a2, b1), (a1, b1))]
-        return parts[0] + parts[1] + parts[2]
+    def rdot(a, name):
+        top, rest = halves(a)
+        return jnp.dot(jnp.concatenate([top, top, rest], axis=1), mat[name][...],
+                       preferred_element_type=jnp.float32)
+
+    def ldot(name, b):
+        top, rest = halves(b)
+        parts = [top, rest] if name == "pick" else [top, top, rest]
+        return jnp.dot(mat[name][...], jnp.concatenate(parts, axis=0),
+                       preferred_element_type=jnp.float32)
 
     def fine_xy(u):
         kx = tab("kx").reshape(8, 8, 8, LANES)
@@ -477,7 +504,7 @@
         return ax, ay.reshape(2, 8, 8, LANES) * tab("ti")[None]
 
     def fine_z(u):
-        az = dot(u.reshape(128, LANES), mat["az7"][...])
+        az = rdot(u.reshape(128, LANES), "az7")
         return az.reshape(2, 8, 8, LANES) * tab("tij")[None]
 
     def fine_send_faces(ax, ay):
@@ -486,7 +513,10 @@
         flat = ay.reshape(16, 8, LANES)
         fine_send[2] = flat[:, 7, :]
         fine_send[3] = flat[:, 0, :]
-        return [start(fine_send.at[d], fine_recv.at[d], faces[d]) for d in range(4)]
+        group = Group(4)
+        for d in range(4):
+            group.start(fine_send.at[d], fine_recv.at[d], faces[d])
+        return group
 
     def add_x(field, low, high):
         return jnp.concatenate(
@@ -499,9 +529,8 @@
         flat = flat + jnp.where(jrow[None] == 7, high[:, None, :], 0.0)
         return flat.reshape(2, 8, 8, LANES)
 
-    def fine_join(copies, field):
-        for copy in copies:
-            copy.wait_recv()
+    def fine_join(group, field):
+        group.arrived()
         field = add_x(field, fine_recv[0], fine_recv[1])
         return add_y(field, fine_recv[2], fine_recv[3])
 
@@ -515,14 +544,16 @@
     def mid_start(ax, ay):
         mid_send[0] = ax
         mid_send[1] = ay
-        return [start(mid_send.at[d // 2], mid_recv.at[d], faces[d]) for d in range(4)]
+        group = Group(4)
+        for d in range(4):
+            group.start(mid_send.at[d // 2], mid_recv.at[d], faces[d])
+        return group
 
     def shifted(v, shift, mask):
         return jnp.where(mask, pltpu.roll(v, shift, 0), 0.0)
 
-    def mid_join(copies, field):
-        for copy in copies:
-            copy.wait_recv()
+    def mid_join(group, field):
+        group.arrived()
         field = field + shifted(mid_recv[0], 4, mrow < 4)
         field = field + shifted(mid_recv[1], 12, mrow >= 12)
         field = field + shifted(mid_recv[2], 13, brow == 0)
@@ -556,7 +587,7 @@
     for i, row in ((1, 7), (0, 0)):
         for j, line in ((1, y7), (0, y0)):
             knight_send[2 * i + j] = line.reshape(2, 8, LANES)[:, row : row + 1]
-    need("tiles")
+    need("early")
     e7 = masked(0, tab("e7"), ORDER, jrow[None])
     kx = tab("kx").reshape(8, 8, 8, LANES)
     ky_last, ky_first = tab("kyl"), tab("kyf")
@@ -568,18 +599,21 @@
         pair_send[n, 1] = contracted
     pl.semaphore_wait(bar, len(near))
     tell(0)
-    copies = [start(knight_send.at[2 * (dx < 0) + (dy < 0)], knight_recv.at[n], (-dx, -dy))
-              for n, (dx, dy) in enumerate(KNIGHTS)]
+    first = [Group(size) for size in (8, 4, 4, 4)]
+    for n, (dx, dy) in enumerate(KNIGHTS):
+        first[0].start(knight_send.at[2 * (dx < 0) + (dy < 0)], knight_recv.at[n], (-dx, -dy))
     pick_edge = {(1, 1): 2, (1, -1): 1, (-1, 1): 3, (-1, -1): 0}
-    copies += [start(edge_send.at[pick_edge[d] : pick_edge[d] + 2], corner_recv.at[n],
-                     (-d[0], -d[1])) for n, d in enumerate(CORNERS)]
-    copies += [start(edge_send.at[(2, 0, 3, 1)[n]], twice_recv.at[n], (-dx, -dy))
-               for n, (dx, dy) in enumerate(TWICE)]
-    copies += [start(pair_send.at[n], pair_recv.at[n], (-dx, -dy))
-               for n, (dx, dy) in enumerate(FACES)]
+    for n, d in enumerate(CORNERS):
+        first[1].start(edge_send.at[pick_edge[d] : pick_edge[d] + 2], corner_recv.at[n],
+                       (-d[0], -d[1]))
+    for n, (dx, dy) in enumerate(TWICE):
+        first[2].start(edge_send.at[(2, 0, 3, 1)[n]], twice_recv.at[n], (-dx, -dy))
+    for n, (dx, dy) in enumerate(FACES):
+        first[3].start(pair_send.at[n], pair_recv.at[n], (-dx, -dy))
+    load(2, count)
     need("az7")
-    for copy in copies:
-        copy.wait_recv()
+    for group in first:
+        group.arrived()
     told(0)
     tell(1)
     irow = jrow[None]
@@ -640,18 +674,20 @@
     side7 = fine_send_faces(ax, ay)
     az = fine_z(x7)
     local7 = ax + ay + az
+    need("late", "rows", "down")
     ci = tab("ci")[None]
     rest7 = (src - tab("cj")[None] * (ax + ci * az) - ci * ay) * keep7[None, None]
-    need("rows", "down")
     jx = tab("jx").reshape(8, 4, 8, LANES)
     g = jx[0][None] * rest7[:, 0:1]
     for i in range(1, 8):
         g = g + jx[i][None] * rest7[:, i : i + 1]
     g = jnp.concatenate([g[0].reshape(32, LANES), g[1].reshape(32, LANES)], axis=1)
-    g3 = left("jy", dot(g, mat["down"][...]))
+    g3 = left("jy", rdot(g, "down"))
     g3_all[0] = g3
-    copies = [start(g3_all.at[0], g3_all.at[n], (-dx, -dy))
-              for n, (dx, dy) in enumerate(AROUND) if n]
+    wide = Group(len(AROUND) - 1)
+    for n, (dx, dy) in enumerate(AROUND):
+        if n:
+            wide.start(g3_all.at[0], g3_all.at[n], (-dx, -dy))
     rest7_all[0] = (b7 - fine_join(side7, local7)).reshape(128, LANES)
     need("az3", "b12", "pick", "lown")
     told(1)
@@ -662,28 +698,27 @@
     n1, n2, n3 = 16 * len(ring1), 16 * len(ring2), 16 * len(ring3)
 
     def mid_z(v):
-        return tab3 * dot(v, mat["az3"][...])
-
-    for copy in copies:
-        copy.wait_recv()
-
-    b3 = dot(mat["pick"][...], g3_all[...].reshape(16 * len(AROUND), LANES))
+        return tab3 * rdot(v, "az3")
+
+    wide.arrived()
+
+    b3 = ldot("pick", g3_all[...].reshape(16 * len(AROUND), LANES))
     v1 = e3_all[:n1] * b3
     b3, e3 = b3[:16], e3[0]
-    r1 = b3 - tc * dot(mat["lown"][...], v1) - mid_z(v1[:16])
+    r1 = b3 - tc * ldot("lown", v1) - mid_z(v1[:16])
     x3 = (1.0 + keep_m) * v1[:16] + gain_m * (e3 * r1)
     ax, ay = left("lx", x3), left("ly", x3)
     ca, cb = rtab("ca")[0], rtab("cb")[0]
     part = keep3 * (g3 - cb * ax - ca * ay)
     other = keep3 * (ca * cb * tab3) * x3
-    line = dot(jnp.concatenate([part, -other], axis=1), mat["b12"][...])
+    line = rdot(jnp.concatenate([part, -other], axis=1), "b12")
     line = jnp.sum(rtab("jj")[0] * line, axis=0, keepdims=True)
     line_send[0] = line
 
+    lines = Group(ny)
+
     def line_copy(d, slot, to):
-        return pltpu.make_async_remote_copy(
-            line_send.at[0], line_recv.at[slot], line_ss.at[d], line_rs.at[d],
-            device_id={"cross": to}, device_id_type=MESH_ID)
+        return lines.make(d, line_send.at[0], line_recv.at[slot], {"cross": to})
 
     def far_first(n, size):
         step = lax.div(n + 1, 2)
@@ -694,27 +729,38 @@
         line_copy(d, cx, lax.rem(cx + d, ny)).start()
         return carry
 
+    def line_left(d, carry):
+        line_copy(d, cx, cx).wait_send()
+        return carry
+
+    def line_arrived(n, carry):
+        d = far_first(ny - 2 - n, ny)
+        line_copy(d, lax.rem(cx + ny - d, ny), cx).wait_recv()
+        return carry
+
     lax.fori_loop(0, ny - 1, line_out, 0)
     line_recv[cx] = line
     side3 = mid_start(ax, ay)
     x3_all[0] = x3
-    side = [start(x3_all.at[0], x3_all.at[n], (-dx, -dy))
-            for n, (dx, dy) in enumerate(ring2) if n]
-    side += [start(rest7_all.at[0], rest7_all.at[n], (-dx, -dy))
-             for n, (dx, dy) in enumerate(ring1) if n]
+    side = [Group(len(ring) - 1) for ring in (ring2, ring1, ring3)]
+    for n, (dx, dy) in enumerate(ring2):
+        if n:
+            side[0].start(x3_all.at[0], x3_all.at[n], (-dx, -dy))
+    for n, (dx, dy) in enumerate(ring1):
+        if n:
+            side[1].start(rest7_all.at[0], rest7_all.at[n], (-dx, -dy))
     if ny < 32:
         line_recv[ny:] = jnp.zeros((32 - ny, 1, LANES), jnp.float32)
     rest3_all[0] = b3 - mid_join(side3, ax + ay + mid_z(x3))
-    side += [start(rest3_all.at[0], rest3_all.at[n], (-dx, -dy))
-             for n, (dx, dy) in enumerate(ring3) if n]
+    for n, (dx, dy) in enumerate(ring3):
+        if n:
+            side[2].start(rest3_all.at[0], rest3_all.at[n], (-dx, -dy))
     need("sin")
-
-    def line_in(d, carry):
-        line_copy(d, lax.rem(cx + ny - d, ny), cx).wait()
-        return carry
-
-    lax.fori_loop(1, ny, line_in, 0)
-    spectrum = dot(mat["sin"][...], line_recv[:, 0, :])
+    for group in first + [wide, side7]:
+        group.left()
+    lax.fori_loop(1, ny, line_left, 0)
+    lax.fori_loop(0, ny - 1, line_arrived, 0)
+    spectrum = ldot("sin", line_recv[:, 0, :])
     group = lax.div(lane, 32)
     for alpha in range(2):
         total = jnp.zeros((8, LANES), jnp.float32)
@@ -727,67 +773,67 @@
                 total = total + jnp.where(group == hi, piece, 0.0)
         mode_send[alpha] = total
 
+    modes = Group(nx)
+
     def mode_copy(d, to):
-        return pltpu.make_async_remote_copy(
-            mode_send, mode_recv.at[d], mode_ss.at[d], mode_rs.at[d],
-            device_id={"stream": to}, device_id_type=MESH_ID)
+        return modes.make(d, mode_send, mode_recv.at[d], {"stream": to})
 
     def mode_out(n, carry):
         d = far_first(n, nx)
         mode_copy(d, lax.rem(sx + d, nx)).start()
         return carry
 
-    def mode_in(d, carry):
-        mode_copy(d, sx).wait()
+    def mode_left(d, carry):
+        mode_copy(d, sx).wait_send()
+        return carry
+
+    def mode_arrived(n, carry):
+        mode_copy(far_first(nx - 2 - n, nx), sx).wait_recv()
         return carry
 
     lax.fori_loop(0, nx - 1, mode_out, 0)
     mode_recv[0] = mode_send[...]
-    lax.fori_loop(1, nx, mode_in, 0)
+    need(*MATS)
+    for group in side:
+        group.arrived()
+    for group in [side3] + side:
+        group.left()
+    lax.fori_loop(1, nx, mode_left, 0)
+    lax.fori_loop(0, nx - 1, mode_arrived, 0)
     first = mode_recv[:, 0]
     second = mode_recv[:, 1]
     nodes = first + jnp.concatenate([second[1:], second[:1]], axis=0)
     start_g = where["green"][0]
-    solved = [jnp.sum(tile_ref[start_g + n : start_g + n + nx] * nodes, axis=0)
+    solved = [jnp.sum(late_ref[start_g + n : start_g + n + nx] * nodes, axis=0)
               for n in range(SPAN)]
-    sine = tile_ref[pl.ds(where["sine"][0] + cx, PAD)]
+    sine = late_ref[pl.ds(where["sine"][0] + cx, PAD)]
     window = [jnp.sum(sine * s[None], axis=1) for s in solved]
     window = jnp.concatenate(window, axis=0)
-    need(*MATS)
-    window = dot(window, mat["back"][...])
+    window = rdot(window, "back")
     zval, zstiff = window[:, :LANES], window[:, LANES:]
-
-    for copy in side:
-        copy.wait_recv()
 
     def per(table, count):
         return jnp.concatenate([table] * count, axis=0)
 
-    from_low = dot(mat["kt"][...], zval)
+    from_low = ldot("kt", zval)
     r0 = rest3_all[...].reshape(n3, LANES) - per(tc, len(ring3)) * from_low[:n3]
-    r0 = r0 - dot(mat["tt"][...], zstiff)
+    r0 = r0 - ldot("tt", zstiff)
     w1 = e3_all * r0
-    aw = per(tc, len(ring2)) * dot(mat["lxy"][...], w1)
-    aw = aw + per(tab3, len(ring2)) * dot(w1[:n2], mat["az3"][...])
+    aw = per(tc, len(ring2)) * ldot("lxy", w1)
+    aw = aw + per(tab3, len(ring2)) * rdot(w1[:n2], "az3")
     x3 = x3_all[...].reshape(n2, LANES) + from_low[n3:]
     x3 = x3 + (1.0 + keep_m) * w1[:n2] + gain_m * (e3_all[:n2] * (r0[:n2] - aw))
 
-    lines = dot(dot(mat["lines"][...], x3), mat["upt"][:, : 2 * LANES])
-    mine = dot(x3[:n1], mat["upt"][...])
-    px = dot(x3[:16], mat["up"][...])
-    px = jnp.stack([dot(mat["pfine"][...], px[:, r * LANES : (r + 1) * LANES]) for r in range(2)])
+    raised = rdot(x3, "upt")
+    apx = ldot("fine", jnp.concatenate(
+        [raised[:, : 2 * LANES], raised[:n1, 2 * LANES :]], axis=0))
+    px = rdot(x3[:16], "up")
+    px = jnp.stack([ldot("pfine", px[:, r * LANES : (r + 1) * LANES]) for r in range(2)])
     px = px.reshape(2, 8, 8, LANES)
-    columns = []
-    for n in range(len(ring1)):
-        for r in range(2):
-            at_n, at_r = slice(16 * n, 16 * n + 16), slice(r * LANES, (r + 1) * LANES)
-            also = slice((2 + r) * LANES, (3 + r) * LANES)
-            columns.append(jnp.concatenate(
-                [mine[at_n, at_r], lines[at_n, at_r], mine[at_n, also]], axis=0))
-    apx = dot(mat["fine"][...], jnp.concatenate(columns, axis=1))
     r0, u1 = [], []
     for n, (dx, dy) in enumerate(ring1):
-        moved = jnp.stack([apx[:, (2 * n + r) * LANES : (2 * n + r + 1) * LANES] for r in range(2)])
+        mine = apx[64 * n : 64 * n + 64]
+        moved = jnp.stack([mine[:, r * LANES : (r + 1) * LANES] for r in range(2)])
         r0.append(rest7_all[n].reshape(2, 8, 8, LANES) - moved.reshape(2, 8, 8, LANES))
         scale = masked(dy, tab("e7"), ORDER, jrow[None]) if dy else e7
         u1.append(scale[None] * r0[n])
@@ -799,25 +845,22 @@
     x7 = x7 + px
     out = x7 + (1.0 + keep_f) * u1[0] + gain_f * (e7[None] * (r0[0] - au))
     out_ref[...] = out.reshape(128, LANES)
-    for copy in sent:
-        copy.wait_send()
 
 
 def solution(mesh):
     nx, ny = mesh.shape["stream"], mesh.shape["cross"]
-    tiles, row16, mats, where = build_tables(nx, ny)
+    tables, where = build_tables(nx, ny)
 
     def body(sources):
         flat = sources.reshape(128, LANES)
-        operands = [flat, jnp.asarray(tiles), jnp.asarray(row16)]
-        operands += [jnp.asarray(mats[name]) for name in MATS]
+        operands = [flat] + [jnp.asarray(table) for table in tables]
         links, f32 = pltpu.SemaphoreType.DMA, jnp.float32
         out = pl.pallas_call(
             functools.partial(kernel, nx, ny, where),
             out_shape=jax.ShapeDtypeStruct((128, LANES), jnp.float32),
             in_specs=[pl.BlockSpec(memory_space=pl.ANY)] * len(operands),
             out_specs=pl.BlockSpec(memory_space=pltpu.VMEM),
-            scratch_shapes=[pltpu.VMEM(o.shape, f32) for o in operands]
+            scratch_shapes=[pltpu.VMEM(o.shape, o.dtype) for o in operands]
             + [
                 pltpu.VMEM((4, 2, 16, LANES), f32),
                 pltpu.VMEM((4, 2, 16, LANES), f32),
@@ -839,12 +882,8 @@
                 pltpu.VMEM((len(offsets(2)), 16, LANES), f32),
                 pltpu.VMEM((len(offsets(1)), 128, LANES), f32),
                 links((len(operands),)),
-                links((N_LINKS,)),
-                links((N_LINKS,)),
-                links((ny,)),
-                links((ny,)),
-                links((nx,)),
-                links((nx,)),
+                links((LINKS + nx + ny,)),
+                links((LINKS + nx + ny,)),
                 pltpu.SemaphoreType.REGULAR((2, 2)),
             ],
             compiler_params=pltpu.CompilerParams(collective_id=0, has_side_effects=True),

time: 61.7 us -> 61 us (0.989)
  Pallas kernels: 60 us -> 59.3 us
    pallas_call x1, Pallas kernels: 60 us -> 59.3 us  [body(): pl.pallas_call(functools.partial(kernel, nx, ny, where), out_shape=jax.Sh...]
where the time goes in v5:
time: 61 us; the launch traced here: 60.8 us
  Pallas kernels  59.3 us (97%)
  local copies, waits for them, and re-layouts  1.47 us (2%)
    pallas_call x1, Pallas kernels, body(): pl.pallas_call(functools.partial(kernel, nx, ny, where), out_shape=jax.Sh...  59.3 us
    unnamed x1, local copies, waits for them, and re-layouts  1.47 us

profile of v5, /device:TPU:1, one launch (start us, length us, event | category | flops | bytes accessed | tf_op | source)
XLA Modules:
  0.0 60.8 jit_solution(1630111310165223168)
XLA Ops:
  0.0 59.3 %vcycle.1 = f32[128,128]{1,0:T(8,128)} custom-call(f32[128,128]{1,0:T(8,128)} %bitcast.5, f32[98,8,128]{2,1,0:T(8,128)} %constant.36.clone.refs_1_, f32[130,8,128]{2,1,0:T(8,128)} %constant.37.clone.refs_2_, f32[70,16,128]{2,1,0:T(8,128)} %constant.38.clone.refs_3_, bf16[384,128]{1,0:T(8,128)(2,1)} %constant.39.clone.refs_4_, ...), custom_call_target="tpu_custom_call" | custom-call | tf_op jit(solution)/shard_map/vcycle/pallas_call | solution.py:858
  59.3 1.5 %copy.22 = f32[2,1,1,8,8,128]{5,4,3,2,1,0:T(8,128)} copy(f32[2,1,1,8,8,128]{5,4,3,2,1,0:T(8,128)} %bitcast.4) | data formatting | bytes 131072

commit v6 on v5

--- a/solution.py
+++ b/solution.py
@@ -21,6 +21,7 @@
 TWICE = ((2, 0), (-2, 0), (0, 2), (0, -2))
 KNIGHTS = tuple((s * a, t * b) for a, b in ((2, 1), (1, 2)) for s in (1, -1) for t in (1, -1))
 AROUND = ((0, 0),) + FACES + CORNERS + TWICE + KNIGHTS
+VMEM_LIMIT = 55168 * 1024
 WIDE, SPAN, PAD = 4, 10, 16
 
 
@@ -339,28 +340,26 @@
     s0 = np.where(here < ny, sine_rows(mode, here, ny), 0.0)
     s1 = np.where(here < ny, sine_rows(mode, here + 1, ny), 0.0)
     mat["sin"] = np.concatenate([s0, s1], axis=0)
-    where, tiles = {}, []
-    for names in EARLY, LATE:
-        packed, start = [], 0
-        for name in names:
-            where[name] = (start, tile[name].shape[0])
-            packed.append(tile[name])
-            start += tile[name].shape[0]
-        tiles.append(np.concatenate(packed).astype(np.float32))
-    packed, start = [], 0
-    for name, value in row.items():
-        where[name] = (start, value.shape[0])
-        packed.append(value)
-        start += value.shape[0]
-    row16 = np.concatenate(packed).astype(np.float32)
-    mats = []
+    where, tiles, at = {}, [], 0
+    for name in EARLY + LATE + tuple(row):
+        value = tile[name] if name in tile else row[name].reshape(-1, 8, LANES)
+        where[name] = (at, value.shape[0])
+        tiles.append(value.astype(np.float32))
+        at += value.shape[0]
+    blocks, at = [], 0
     for name in MATS:
         value = mat[name].astype(np.float32)
         top = value.astype(ml_dtypes.bfloat16)
         rest = (value - top.astype(np.float32)).astype(ml_dtypes.bfloat16)
         parts = [top, top] if name == "pick" else [top, rest, top]
-        mats.append(np.concatenate(parts, axis=0 if name in RIGHT else 1))
-    return (*tiles, row16, *mats), where
+        value = np.concatenate(parts, axis=0 if name in RIGHT else 1)
+        height, width = value.shape
+        count = -(-width // LANES)
+        value = np.pad(value, ((0, 0), (0, count * LANES - width)))
+        where[name] = (at, height, width)
+        blocks += [value[:, LANES * n : LANES * n + LANES] for n in range(count)]
+        at += height * count
+    return np.concatenate(tiles), np.concatenate(blocks), where
 
 
 EARLY = ("e7", "kx", "kyl", "kyf", "ti", "ky", "tij")
@@ -381,45 +380,52 @@
 
 
 def kernel(nx, ny, where, *refs):
-    names = ("x", "early", "late", "rows") + MATS
-    count = len(names)
-    hbm, out_ref, vmem = refs[:count], refs[count], refs[count + 1 : 2 * count + 1]
+    hbm, out_ref, vmem = refs[:3], refs[3], refs[4:7]
     (pair_send, pair_recv, edge_send, corner_recv, twice_recv, knight_send, knight_recv, g3_all,
      fine_send, fine_recv, mid_send, mid_recv, line_send, line_recv, mode_send, mode_recv,
-     rest3_all, x3_all, rest7_all, load_sem, send_sem, recv_sem, known) = refs[2 * count + 1 :]
+     rest3_all, x3_all, rest7_all, load_sem, send_sem, recv_sem, known) = refs[7:]
     sx, cx = lax.axis_index("stream"), lax.axis_index("cross")
-    early_ref, late_ref, row_ref = vmem[1:4]
-    mat = dict(zip(MATS, vmem[4:]))
+    tile_ref, block_ref = vmem[1:]
 
     def at(dx, dy):
         return {"stream": lax.rem(sx + (nx + dx), nx), "cross": lax.rem(cx + (ny + dy), ny)}
 
     def tab(name):
         start, size = where[name]
-        return (early_ref if name in EARLY else late_ref)[start : start + size]
+        return tile_ref[start : start + size]
 
     def rtab(name):
-        start, size = where[name]
-        return row_ref[start : start + size]
+        return tab(name).reshape(-1, 16, LANES)
+
+    def mat(name):
+        start, height, width = where[name]
+        parts = [block_ref[start + n * height : start + (n + 1) * height]
+                 for n in range(-(-width // LANES))]
+        return (parts[0] if len(parts) == 1 else jnp.concatenate(parts, axis=1))[:, :width]
 
     bar = pltpu.get_barrier_semaphore()
     faces = FACES
     near_x, hops_x = reach(nx)
     near_y, hops_y = reach(ny)
-    near = [(s * d, 0) for d in near_x for s in (1, -1)]
-    near += [(0, s * d) for d in near_y for s in (1, -1)]
-    near += CORNERS + KNIGHTS
+    near = list(KNIGHTS + CORNERS)
+    near += [(s * d, 0) for d in reversed(near_x) for s in (1, -1)]
+    near += [(0, s * d) for d in reversed(near_y) for s in (1, -1)]
     for d in near:
         pl.semaphore_signal(bar, inc=1, device_id=at(*d), device_id_type=MESH_ID)
+    late, last = where[LATE[0]][0], where["sin"][0]
+    spans = {"x": (0, 0, 128), "early": (1, 0, late), "late": (1, late, hbm[1].shape[0]),
+             "first": (2, 0, last), "last": (2, last, hbm[2].shape[0])}
     loads = {}
 
-    def load(first, last):
-        for n in range(first, last):
-            copy = pltpu.make_async_copy(hbm[n], vmem[n], load_sem.at[n])
-            copy.start()
-            loads[names[n]] = copy
-
-    load(0, 2)
+    def load(*wanted):
+        for name in wanted:
+            operand, start, end = spans[name]
+            part = pl.ds(start, end - start)
+            loads[name] = pltpu.make_async_copy(
+                hbm[operand].at[part], vmem[operand].at[part], load_sem.at[list(spans).index(name)])
+            loads[name].start()
+
+    load("x", "early")
 
     def need(*wanted):
         for name in wanted:
@@ -482,13 +488,13 @@
 
     def rdot(a, name):
         top, rest = halves(a)
-        return jnp.dot(jnp.concatenate([top, top, rest], axis=1), mat[name][...],
+        return jnp.dot(jnp.concatenate([top, top, rest], axis=1), mat(name),
                        preferred_element_type=jnp.float32)
 
     def ldot(name, b):
         top, rest = halves(b)
         parts = [top, rest] if name == "pick" else [top, top, rest]
-        return jnp.dot(mat[name][...], jnp.concatenate(parts, axis=0),
+        return jnp.dot(mat(name), jnp.concatenate(parts, axis=0),
                        preferred_element_type=jnp.float32)
 
     def fine_xy(u):
@@ -536,9 +542,10 @@
 
     def left(name, v):
         start_row, size = where[name]
-        acc = row_ref[start_row] * v[0:1]
-        for c in range(1, size):
-            acc = acc + row_ref[start_row + c] * v[c : c + 1]
+        acc = 0.0
+        for c in range(size // 2):
+            both = tile_ref[start_row + 2 * c : start_row + 2 * c + 2].reshape(16, LANES)
+            acc = acc + both * v[c : c + 1]
         return acc
 
     def mid_start(ax, ay):
@@ -610,8 +617,8 @@
         first[2].start(edge_send.at[(2, 0, 3, 1)[n]], twice_recv.at[n], (-dx, -dy))
     for n, (dx, dy) in enumerate(FACES):
         first[3].start(pair_send.at[n], pair_recv.at[n], (-dx, -dy))
-    load(2, count)
-    need("az7")
+    load("first", "late", "last")
+    need("first")
     for group in first:
         group.arrived()
     told(0)
@@ -674,7 +681,7 @@
     side7 = fine_send_faces(ax, ay)
     az = fine_z(x7)
     local7 = ax + ay + az
-    need("late", "rows", "down")
+    need("late")
     ci = tab("ci")[None]
     rest7 = (src - tab("cj")[None] * (ax + ci * az) - ci * ay) * keep7[None, None]
     jx = tab("jx").reshape(8, 4, 8, LANES)
@@ -689,7 +696,6 @@
         if n:
             wide.start(g3_all.at[0], g3_all.at[n], (-dx, -dy))
     rest7_all[0] = (b7 - fine_join(side7, local7)).reshape(128, LANES)
-    need("az3", "b12", "pick", "lown")
     told(1)
     ring1, ring2, ring3 = offsets(1), offsets(2), offsets(3)
     e3 = {dy: masked(dy, rtab("e3")[0], MID_ORDER, brow) for dy in range(-3, 4)}
@@ -755,7 +761,7 @@
     for n, (dx, dy) in enumerate(ring3):
         if n:
             side[2].start(rest3_all.at[0], rest3_all.at[n], (-dx, -dy))
-    need("sin")
+    need("last")
     for group in first + [wide, side7]:
         group.left()
     lax.fori_loop(1, ny, line_left, 0)
@@ -793,7 +799,6 @@
 
     lax.fori_loop(0, nx - 1, mode_out, 0)
     mode_recv[0] = mode_send[...]
-    need(*MATS)
     for group in side:
         group.arrived()
     for group in [side3] + side:
@@ -804,9 +809,9 @@
     second = mode_recv[:, 1]
     nodes = first + jnp.concatenate([second[1:], second[:1]], axis=0)
     start_g = where["green"][0]
-    solved = [jnp.sum(late_ref[start_g + n : start_g + n + nx] * nodes, axis=0)
+    solved = [jnp.sum(tile_ref[start_g + n : start_g + n + nx] * nodes, axis=0)
               for n in range(SPAN)]
-    sine = late_ref[pl.ds(where["sine"][0] + cx, PAD)]
+    sine = tile_ref[pl.ds(where["sine"][0] + cx, PAD)]
     window = [jnp.sum(sine * s[None], axis=1) for s in solved]
     window = jnp.concatenate(window, axis=0)
     window = rdot(window, "back")
@@ -849,11 +854,11 @@
 
 def solution(mesh):
     nx, ny = mesh.shape["stream"], mesh.shape["cross"]
-    tables, where = build_tables(nx, ny)
+    tiles, blocks, where = build_tables(nx, ny)
 
     def body(sources):
         flat = sources.reshape(128, LANES)
-        operands = [flat] + [jnp.asarray(table) for table in tables]
+        operands = [flat, jnp.asarray(tiles), jnp.asarray(blocks)]
         links, f32 = pltpu.SemaphoreType.DMA, jnp.float32
         out = pl.pallas_call(
             functools.partial(kernel, nx, ny, where),
@@ -881,12 +886,13 @@
                 pltpu.VMEM((len(offsets(3)), 16, LANES), f32),
                 pltpu.VMEM((len(offsets(2)), 16, LANES), f32),
                 pltpu.VMEM((len(offsets(1)), 128, LANES), f32),
-                links((len(operands),)),
+                links((5,)),
                 links((LINKS + nx + ny,)),
                 links((LINKS + nx + ny,)),
                 pltpu.SemaphoreType.REGULAR((2, 2)),
             ],
-            compiler_params=pltpu.CompilerParams(collective_id=0, has_side_effects=True),
+            compiler_params=pltpu.CompilerParams(
+                collective_id=0, has_side_effects=True, vmem_limit_bytes=VMEM_LIMIT),
             name="vcycle",
         )(*operands)
         return out.reshape(sources.shape)

time: 61 us -> 59.3 us (0.972)
  local copies, waits for them, and re-layouts: 1.47 us -> 0.63 us
  Pallas kernels: 59.3 us -> 58.6 us
    unnamed x1, local copies, waits for them, and re-layouts: 1.47 us -> 0.63 us
    pallas_call x1, Pallas kernels: 59.3 us -> 58.6 us  [body(): pl.pallas_call(functools.partial(kernel, nx, ny, where), out_shape=jax.Sh...]
where the time goes in v6:
time: 59.3 us; the launch traced here: 59.2 us
  Pallas kernels  58.6 us (99%)
  local copies, waits for them, and re-layouts  0.63 us (1%)
    pallas_call x1, Pallas kernels, body(): pl.pallas_call(functools.partial(kernel, nx, ny, where), out_shape=jax.Sh...  58.6 us

profile of v6, /device:TPU:1, one launch (start us, length us, event | category | flops | bytes accessed | tf_op | source)
XLA Modules:
  0.0 59.2 jit_solution(12087296049715717697)
XLA Ops:
  0.0 58.6 %vcycle.1 = f32[128,128]{1,0:T(8,128)S(1)} custom-call(f32[128,128]{1,0:T(8,128)} %bitcast.5, f32[368,8,128]{2,1,0:T(8,128)} %constant.4.clone.refs_1_, bf16[14368,128]{1,0:T(8,128)(2,1)} %constant.5.clone.refs_2_), custom_call_target="tpu_custom_call" | custom-call | tf_op jit(solution)/shard_map/vcycle/pallas_call | solution.py:863
  58.6 0.6 %copy.6 = f32[2,1,1,8,8,128]{5,4,3,2,1,0:T(8,128)} copy(f32[2,1,1,8,8,128]{5,4,3,2,1,0:T(8,128)S(1)} %bitcast.4) | data formatting | bytes 131072

commit v7 on v6

--- a/solution.py
+++ b/solution.py
@@ -277,9 +277,9 @@
                 cross[n, :, :, m] += np.einsum("ac,bd->abcd", line, diag3)
             else:
                 cross[n, :, :, m] += np.einsum("ac,bd->abcd", diag3, line)
-    pick = np.zeros((len(ring1), q, q, len(AROUND), q, q))
+    pick = np.zeros((len(ring1), q, q, 144))
     for n, (dx, dy) in enumerate(ring1):
-        for m, (gx, gy) in enumerate(AROUND):
+        for gx, gy in AROUND:
             sx, sy = gx - dx, gy - dy
             if max(abs(sx), abs(sy)) > 1:
                 continue
@@ -287,8 +287,18 @@
             span_y = [(b, b) for b in range(q)] if sy == 0 else [(q - 1, 0) if sy > 0 else (0, q - 1)]
             for a, a2 in span_x:
                 for b, b2 in span_y:
-                    pick[n, a, b, m, a2, b2] = 1.0
-    mat["pick"] = pick.reshape(len(ring1) * 16, len(AROUND) * 16)
+                    d = (gx, gy)
+                    if d in ring1:
+                        column = 16 * ring1.index(d) + 4 * a2 + b2
+                    elif d in CORNERS:
+                        part = (d[0] != d[1]) if sx else (d[0] == d[1])
+                        column = 80 + 8 * CORNERS.index(d) + 4 * part + (b2 if sx else a2)
+                    elif d in TWICE:
+                        column = 112 + 4 * TWICE.index(d) + (b2 if sx else a2)
+                    else:
+                        column = 128 + KNIGHTS.index(d)
+                    pick[n, a, b, column] = 1.0
+    mat["pick"] = pick.reshape(len(ring1) * 16, 144)
     mat["lxy"] = cross.reshape(len(ring2) * 16, len(ring3) * 16)
     k7j = k7 @ j73
     t7j = t7[:, None] * j73
@@ -379,11 +389,23 @@
     return range(1, base + 1), hops
 
 
+def mean_hops(d, size):
+    def ring(a, b):
+        return min((a - b) % 4, (b - a) % 4)
+
+    total = 0
+    for p in range(size):
+        t = (p + d) % size
+        total += ring(p // 8, t // 8) + ring(p // 2 % 4, t // 2 % 4) + 0.5 * (p % 2 != t % 2)
+    return total
+
+
 def kernel(nx, ny, where, *refs):
     hbm, out_ref, vmem = refs[:3], refs[3], refs[4:7]
     (pair_send, pair_recv, edge_send, corner_recv, twice_recv, knight_send, knight_recv, g3_all,
+     edge3_send, corner3_recv, twice3_recv, knight3_send, knight3_recv, line7_send, line7_recv,
      fine_send, fine_recv, mid_send, mid_recv, line_send, line_recv, mode_send, mode_recv,
-     rest3_all, x3_all, rest7_all, load_sem, send_sem, recv_sem, known) = refs[7:]
+     rest3_all, x3_all, load_sem, send_sem, recv_sem, known) = refs[7:]
     sx, cx = lax.axis_index("stream"), lax.axis_index("cross")
     tile_ref, block_ref = vmem[1:]
 
@@ -667,7 +689,10 @@
             with_ends(twice[0, -2], knight[-1, -2], knight[1, -2]),
             with_ends(y0, row_of(raw[-1, 0], 0), row_of(raw[1, 0], 0))),
     }
-    extra = {d: masked(d[1], tab("e7"), ORDER, jrow[None])[None] * v for d, v in extra.items()}
+    e7_of = {0: e7}
+    for dy in (1, -1):
+        e7_of[dy] = masked(dy, tab("e7"), ORDER, jrow[None])
+    extra = {d: e7_of[d[1]][None] * v for d, v in extra.items()}
 
     u1 = e7[None] * b7
     ax, ay = fine_xy(u1)
@@ -691,11 +716,28 @@
     g = jnp.concatenate([g[0].reshape(32, LANES), g[1].reshape(32, LANES)], axis=1)
     g3 = left("jy", rdot(g, "down"))
     g3_all[0] = g3
+    by_a = g3.reshape(4, 4, LANES)
+    for n, edge in enumerate((by_a[3], by_a[:, 3], by_a[0], by_a[:, 0], by_a[3])):
+        edge3_send[n] = edge
+    for i, row in ((1, 12), (0, 0)):
+        for j in (0, 1):
+            knight3_send[2 * i + j] = g3[row + 3 * j : row + 3 * j + 1]
     wide = Group(len(AROUND) - 1)
-    for n, (dx, dy) in enumerate(AROUND):
-        if n:
-            wide.start(g3_all.at[0], g3_all.at[n], (-dx, -dy))
-    rest7_all[0] = (b7 - fine_join(side7, local7)).reshape(128, LANES)
+    for n, (dx, dy) in enumerate(KNIGHTS):
+        wide.start(knight3_send.at[2 * (dx < 0) + (dy < 0)], knight3_recv.at[n], (-dx, -dy))
+    for n, d in enumerate(CORNERS):
+        wide.start(edge3_send.at[pick_edge[d] : pick_edge[d] + 2], corner3_recv.at[n],
+                   (-d[0], -d[1]))
+    for n, (dx, dy) in enumerate(TWICE):
+        wide.start(edge3_send.at[(2, 0, 3, 1)[n]], twice3_recv.at[n], (-dx, -dy))
+    for n, (dx, dy) in enumerate(FACES):
+        wide.start(g3_all.at[0], g3_all.at[n + 1], (-dx, -dy))
+    rest7 = b7 - fine_join(side7, local7)
+    scaled = e7[None] * rest7
+    line7_send[0] = along_x(scaled, 0)
+    line7_send[1] = along_x(scaled, 7)
+    line7_send[2] = along_y(scaled, ky_first)
+    line7_send[3] = along_y(scaled, ky_last)
     told(1)
     ring1, ring2, ring3 = offsets(1), offsets(2), offsets(3)
     e3 = {dy: masked(dy, rtab("e3")[0], MID_ORDER, brow) for dy in range(-3, 4)}
@@ -708,7 +750,10 @@
 
     wide.arrived()
 
-    b3 = ldot("pick", g3_all[...].reshape(16 * len(AROUND), LANES))
+    b3 = ldot("pick", jnp.concatenate(
+        [g3_all[...].reshape(80, LANES), corner3_recv[...].reshape(32, LANES),
+         twice3_recv[...].reshape(16, LANES), knight3_recv[:, 0, :],
+         jnp.zeros((8, LANES), jnp.float32)], axis=0))
     v1 = e3_all[:n1] * b3
     b3, e3 = b3[:16], e3[0]
     r1 = b3 - tc * ldot("lown", v1) - mid_z(v1[:16])
@@ -730,11 +775,6 @@
         step = lax.div(n + 1, 2)
         return size // 2 + step * (1 - 2 * lax.rem(n, 2))
 
-    def line_out(n, carry):
-        d = far_first(n, ny)
-        line_copy(d, cx, lax.rem(cx + d, ny)).start()
-        return carry
-
     def line_left(d, carry):
         line_copy(d, cx, cx).wait_send()
         return carry
@@ -744,7 +784,9 @@
         line_copy(d, lax.rem(cx + ny - d, ny), cx).wait_recv()
         return carry
 
-    lax.fori_loop(0, ny - 1, line_out, 0)
+    for n in range(ny - 1):
+        d = ny // 2 + (n + 1) // 2 * (1 - 2 * (n % 2))
+        line_copy(d, cx, lax.rem(cx + d, ny)).start()
     line_recv[cx] = line
     side3 = mid_start(ax, ay)
     x3_all[0] = x3
@@ -752,9 +794,8 @@
     for n, (dx, dy) in enumerate(ring2):
         if n:
             side[0].start(x3_all.at[0], x3_all.at[n], (-dx, -dy))
-    for n, (dx, dy) in enumerate(ring1):
-        if n:
-            side[1].start(rest7_all.at[0], rest7_all.at[n], (-dx, -dy))
+    for n, (dx, dy) in enumerate(FACES):
+        side[1].start(line7_send.at[n], line7_recv.at[n], (-dx, -dy))
     if ny < 32:
         line_recv[ny:] = jnp.zeros((32 - ny, 1, LANES), jnp.float32)
     rest3_all[0] = b3 - mid_join(side3, ax + ay + mid_z(x3))
@@ -784,35 +825,32 @@
     def mode_copy(d, to):
         return modes.make(d, mode_send, mode_recv.at[d], {"stream": to})
 
-    def mode_out(n, carry):
-        d = far_first(n, nx)
-        mode_copy(d, lax.rem(sx + d, nx)).start()
-        return carry
-
     def mode_left(d, carry):
         mode_copy(d, sx).wait_send()
         return carry
 
-    def mode_arrived(n, carry):
-        mode_copy(far_first(nx - 2 - n, nx), sx).wait_recv()
-        return carry
-
-    lax.fori_loop(0, nx - 1, mode_out, 0)
+    by_hops = sorted(range(1, nx), key=lambda d: mean_hops(d, nx))
+    for d in reversed(by_hops):
+        mode_copy(d, lax.rem(sx + d, nx)).start()
     mode_recv[0] = mode_send[...]
     for group in side:
         group.arrived()
     for group in [side3] + side:
         group.left()
     lax.fori_loop(1, nx, mode_left, 0)
-    lax.fori_loop(0, nx - 1, mode_arrived, 0)
+    for d in by_hops:
+        mode_copy(d, sx).wait_recv()
     first = mode_recv[:, 0]
     second = mode_recv[:, 1]
     nodes = first + jnp.concatenate([second[1:], second[:1]], axis=0)
     start_g = where["green"][0]
     solved = [jnp.sum(tile_ref[start_g + n : start_g + n + nx] * nodes, axis=0)
               for n in range(SPAN)]
-    sine = tile_ref[pl.ds(where["sine"][0] + cx, PAD)]
-    window = [jnp.sum(sine * s[None], axis=1) for s in solved]
+    sine = tile_ref[pl.ds(where["sine"][0] + cx, SPAN)]
+    blank = jnp.zeros((PAD - SPAN, LANES), jnp.float32)
+    window = []
+    for s in solved:
+        window += [jnp.sum(sine * s[None], axis=1), blank]
     window = jnp.concatenate(window, axis=0)
     window = rdot(window, "back")
     zval, zstiff = window[:, :LANES], window[:, LANES:]
@@ -835,20 +873,21 @@
     px = rdot(x3[:16], "up")
     px = jnp.stack([ldot("pfine", px[:, r * LANES : (r + 1) * LANES]) for r in range(2)])
     px = px.reshape(2, 8, 8, LANES)
-    r0, u1 = [], []
-    for n, (dx, dy) in enumerate(ring1):
+    moved = []
+    for n in range(len(ring1)):
         mine = apx[64 * n : 64 * n + 64]
-        moved = jnp.stack([mine[:, r * LANES : (r + 1) * LANES] for r in range(2)])
-        r0.append(rest7_all[n].reshape(2, 8, 8, LANES) - moved.reshape(2, 8, 8, LANES))
-        scale = masked(dy, tab("e7"), ORDER, jrow[None]) if dy else e7
-        u1.append(scale[None] * r0[n])
-
-    ax, ay = fine_xy(u1[0])
-    au = ax + ay + fine_z(u1[0])
-    au = add_x(au, along_x(u1[2], 7), along_x(u1[1], 0))
-    au = add_y(au, along_y(u1[4], ky_last), along_y(u1[3], ky_first))
+        mine = jnp.stack([mine[:, r * LANES : (r + 1) * LANES] for r in range(2)])
+        moved.append(mine.reshape(2, 8, 8, LANES))
+    r0 = rest7 - moved[0]
+    u1 = e7[None] * r0
+    right, left_, above, below = [e7_of[dy][None] * moved[n + 1] for n, (_, dy) in enumerate(FACES)]
+    ax, ay = fine_xy(u1)
+    au = ax + ay + fine_z(u1)
+    au = add_x(au, line7_recv[1] - along_x(left_, 7), line7_recv[0] - along_x(right, 0))
+    au = add_y(au, line7_recv[3] - along_y(below, ky_last),
+               line7_recv[2] - along_y(above, ky_first))
     x7 = x7 + px
-    out = x7 + (1.0 + keep_f) * u1[0] + gain_f * (e7[None] * (r0[0] - au))
+    out = x7 + (1.0 + keep_f) * u1 + gain_f * (e7[None] * (r0 - au))
     out_ref[...] = out.reshape(128, LANES)
 
 
@@ -874,7 +913,14 @@
                 pltpu.VMEM((4, 16, LANES), f32),
                 pltpu.VMEM((4, 2, 1, LANES), f32),
                 pltpu.VMEM((8, 2, 1, LANES), f32),
-                pltpu.VMEM((len(AROUND), 16, LANES), f32),
+                pltpu.VMEM((5, 16, LANES), f32),
+                pltpu.VMEM((5, 4, LANES), f32),
+                pltpu.VMEM((4, 2, 4, LANES), f32),
+                pltpu.VMEM((4, 4, LANES), f32),
+                pltpu.VMEM((4, 1, LANES), f32),
+                pltpu.VMEM((8, 1, LANES), f32),
+                pltpu.VMEM((4, 16, LANES), f32),
+                pltpu.VMEM((4, 16, LANES), f32),
                 pltpu.VMEM((4, 16, LANES), f32),
                 pltpu.VMEM((4, 16, LANES), f32),
                 pltpu.VMEM((2, 16, LANES), f32),
@@ -885,7 +931,6 @@
                 pltpu.VMEM((nx, 2, 8, LANES), f32),
                 pltpu.VMEM((len(offsets(3)), 16, LANES), f32),
                 pltpu.VMEM((len(offsets(2)), 16, LANES), f32),
-                pltpu.VMEM((len(offsets(1)), 128, LANES), f32),
                 links((5,)),
                 links((LINKS + nx + ny,)),
                 links((LINKS + nx + ny,)),

time: 59.3 us -> 57.7 us (0.973)
  Pallas kernels: 58.6 us -> 56.9 us
    pallas_call x1, Pallas kernels: 58.6 us -> 56.9 us  [body(): pl.pallas_call(functools.partial(kernel, nx, ny, where), out_shape=jax.Sh...]
where the time goes in v7:
time: 57.7 us; the launch traced here: 57.5 us
  Pallas kernels  56.9 us (99%)
  local copies, waits for them, and re-layouts  0.63 us (1%)
    pallas_call x1, Pallas kernels, body(): pl.pallas_call(functools.partial(kernel, nx, ny, where), out_shape=jax.Sh...  56.9 us

profile of v7, /device:TPU:1, one launch (start us, length us, event | category | flops | bytes accessed | tf_op | source)
XLA Modules:
  0.0 57.5 jit_solution(1697080914760995660)
XLA Ops:
  0.0 56.9 %vcycle.1 = f32[128,128]{1,0:T(8,128)S(1)} custom-call(f32[128,128]{1,0:T(8,128)} %bitcast.5, f32[368,8,128]{2,1,0:T(8,128)} %constant.4.clone.refs_1_, bf16[14128,128]{1,0:T(8,128)(2,1)} %constant.5.clone.refs_2_), custom_call_target="tpu_custom_call" | custom-call | tf_op jit(solution)/shard_map/vcycle/pallas_call | solution.py:902
  56.9 0.6 %copy.6 = f32[2,1,1,8,8,128]{5,4,3,2,1,0:T(8,128)} copy(f32[2,1,1,8,8,128]{5,4,3,2,1,0:T(8,128)S(1)} %bitcast.4) | data formatting | bytes 131072

commit v8 on v7

--- a/solution.py
+++ b/solution.py
@@ -19,7 +19,7 @@
 FACES = ((1, 0), (-1, 0), (0, 1), (0, -1))
 CORNERS = ((1, 1), (1, -1), (-1, 1), (-1, -1))
 TWICE = ((2, 0), (-2, 0), (0, 2), (0, -2))
-KNIGHTS = tuple((s * a, t * b) for a, b in ((2, 1), (1, 2)) for s in (1, -1) for t in (1, -1))
+KNIGHTS = tuple((s * a, t * b) for a, b in ((1, 2), (2, 1)) for s in (1, -1) for t in (1, -1))
 AROUND = ((0, 0),) + FACES + CORNERS + TWICE + KNIGHTS
 VMEM_LIMIT = 55168 * 1024
 WIDE, SPAN, PAD = 4, 10, 16
@@ -639,7 +639,7 @@
         first[2].start(edge_send.at[(2, 0, 3, 1)[n]], twice_recv.at[n], (-dx, -dy))
     for n, (dx, dy) in enumerate(FACES):
         first[3].start(pair_send.at[n], pair_recv.at[n], (-dx, -dy))
-    load("first", "late", "last")
+    load("first", "late")
     need("first")
     for group in first:
         group.arrived()
@@ -732,6 +732,7 @@
         wide.start(edge3_send.at[(2, 0, 3, 1)[n]], twice3_recv.at[n], (-dx, -dy))
     for n, (dx, dy) in enumerate(FACES):
         wide.start(g3_all.at[0], g3_all.at[n + 1], (-dx, -dy))
+    load("last")
     rest7 = b7 - fine_join(side7, local7)
     scaled = e7[None] * rest7
     line7_send[0] = along_x(scaled, 0)

time: 57.7 us -> 57.7 us (level)
  no operation moved by 1% of the time
where the time goes in v8:
time: 57.7 us; the launch traced here: 57.5 us
  Pallas kernels  56.9 us (99%)
  local copies, waits for them, and re-layouts  0.63 us (1%)
    pallas_call x1, Pallas kernels, body(): pl.pallas_call(functools.partial(kernel, nx, ny, where), out_shape=jax.Sh...  56.9 us

profile of v8, /device:TPU:1, one launch (start us, length us, event | category | flops | bytes accessed | tf_op | source)
XLA Modules:
  0.0 57.5 jit_solution(9333679159474316261)
XLA Ops:
  0.0 56.9 %vcycle.1 = f32[128,128]{1,0:T(8,128)S(1)} custom-call(f32[128,128]{1,0:T(8,128)} %bitcast.5, f32[368,8,128]{2,1,0:T(8,128)} %constant.4.clone.refs_1_, bf16[14128,128]{1,0:T(8,128)(2,1)} %constant.5.clone.refs_2_), custom_call_target="tpu_custom_call" | custom-call | tf_op jit(solution)/shard_map/vcycle/pallas_call | solution.py:903
  56.9 0.6 %copy.6 = f32[2,1,1,8,8,128]{5,4,3,2,1,0:T(8,128)} copy(f32[2,1,1,8,8,128]{5,4,3,2,1,0:T(8,128)S(1)} %bitcast.4) | data formatting | bytes 131072
